TPU v7x, 128 devices: a whole 4x4x4 slice. The times are simulated.
128 devices in a mesh: dp: 32 (over y, z, core), fsdp: 4 (over x).
Axes of the slice: x: 4, y: 4, z: 4, core: 2. Of those that a mesh axis runs over, the one named last changes fastest.
Arguments:
- stash: bfloat16 [32, 4, 32, 32, 1024], P('dp', 'fsdp'), may hold values from -6 to 6
- stash_place: int32 [32, 32], replicated, may hold values from 0 to 1023, as said below
- pack_start: int32 [131072], P(('dp', 'fsdp')), may hold values from 0 to 1023, as said below
- d_out: bfloat16 [131072, 1536], P(('dp', 'fsdp')), may hold values from -6 to 6
- out_weight: bfloat16 [768, 1536], P('fsdp'), may hold values from -0.21875 to 0.21875
Outputs:
- grad_query: bfloat16 [131072, 768], P(('dp', 'fsdp'))
- grad_keyval: bfloat16 [131072, 256], P(('dp', 'fsdp'))
- grad_weight: float32 [768, 1536], P('fsdp')
Inputs may be any that keep to these rules, and one draw needn't show every extreme that they name: `pack_start`: each value is the index, among its device's 1024 rows, of the first row of the row's pack: packs are runs of consecutive rows of one device, never crossing devices, of at most 1024 rows, and some pack has exactly 1024 rows. `stash_place`: A permutation of 0 to 1023; one placement serves all 4 fsdp shards of a group alike. Exactly 16 blocks of every group are held by other groups, each by a different group; a group holds exactly 1 block of each other group that it holds any of, and blocks of exactly 16 other groups.
All inputs are finite; a program needn't handle non-finite values.
Results may differ from a plain program's by a relative error of at most 0.012.
The roundings to bfloat16 on the way count: a program that leaves them out, or rounds other values in their place, can miss the bound.
Values may be sent and summed in bfloat16 or wider, within the bound.
No kernel may reach another device: no remote copies, remote signals or barrier semaphores. Data moves between devices by JAX's collectives and lax.ppermute only.
A program may use at most 128 MiB of HBM per device.

v0:
```python
import functools

import jax
import jax.numpy as jnp
from jax import lax
from jax.experimental import pallas as pl
from jax.experimental.pallas import tpu as pltpu
from jax.sharding import PartitionSpec as P

HQ = 6
HD = 128
TILE = 256
TOK = 1024
TILES = TOK // TILE
D = 1536
HALF = D // 2
NB = 32
BLK = 32
WIDTH = 1024
N_FSDP = 4
SHARD = HQ * HD // N_FSDP
SCALE = HD ** (-0.5)
EXP2_SCALE = SCALE * 1.4426950408889634
KEY = slice(HQ * HD, (HQ + 1) * HD)
VALUE = slice((HQ + 1) * HD, (HQ + 2) * HD)
NT = (((1,), (1,)), ((), ()))
NN = (((1,), (0,)), ((), ()))
ANY = pl.BlockSpec(memory_space=pl.ANY)
SMEM = pl.BlockSpec(memory_space=pltpu.SMEM)
VMEM = pl.BlockSpec(memory_space=pltpu.VMEM)
HBM = pl.BlockSpec(memory_space=pltpu.HBM)


def params(mib):
    return pltpu.CompilerParams(vmem_limit_bytes=mib * 2**20)


BF16 = jnp.bfloat16
LARGE = 56
F32 = jnp.float32


def dot(a, b, dims):
    return lax.dot_general(a, b, dims, preferred_element_type=F32)


def shape(dims, dtype=BF16):
    return jax.ShapeDtypeStruct(dims, dtype)


def cost(flops, size, exps=0):
    return pl.CostEstimate(flops=int(flops), bytes_accessed=int(size), transcendentals=int(exps))


def d_attn_kernel(x_ref, w0, w1, w2, w3, dout_ref, out_ref, weight, sems):
    @pl.when(pl.program_id(0) == 0)
    def _():
        copies = []
        for k, w in enumerate((w0, w1, w2, w3)):
            at = pl.multiple_of(lax.rem(x_ref[0] - k + N_FSDP, N_FSDP) * SHARD, SHARD)
            copies.append(pltpu.make_async_copy(w, weight.at[pl.ds(at, SHARD), :], sems.at[k]))
        for copy in copies:
            copy.start()
        for copy in copies:
            copy.wait()

    out_ref[...] = dot(weight[...], dout_ref[...], NT).astype(BF16)


def d_attn_transposed(x, weights, dout):
    return pl.pallas_call(
        d_attn_kernel,
        grid=(TILES,),
        out_shape=shape((HQ * HD, TOK)),
        in_specs=[SMEM] + [ANY] * 4 + [pl.BlockSpec((TILE, D), lambda i: (i, 0))],
        out_specs=pl.BlockSpec((HQ * HD, TILE), lambda i: (0, i)),
        scratch_shapes=[pltpu.VMEM((HQ * HD, D), BF16), pltpu.SemaphoreType.DMA((N_FSDP,))],
        compiler_params=params(LARGE),
        name="d_attn",
        cost_estimate=cost(2 * TOK * D * HQ * HD, 8 * 2**20),
    )(x, *weights, dout)


def keep_mask(tile, start):
    width = (tile + 1) * TILE
    key = lax.broadcasted_iota(jnp.int32, (width, TILE), 0)
    query = tile * TILE + lax.broadcasted_iota(jnp.int32, (width, TILE), 1)
    return (key >= start[:, tile * TILE : width]) & (key <= query)


def transposed(x):
    return x.astype(F32).T.astype(BF16)


def forward_tile(rows, value_t, mask, head, tile):
    width = (tile + 1) * TILE
    query = rows[tile * TILE : width, head * HD : (head + 1) * HD]
    scores = jnp.where(mask, dot(rows[:width, KEY], query, NT), -jnp.inf)
    top = jnp.max(scores, axis=0, keepdims=True)
    expo = jnp.exp2((scores - top) * EXP2_SCALE)
    total = jnp.sum(expo, axis=0, keepdims=True)
    weights = (expo * (1.0 / total)).astype(BF16)
    attn = dot(value_t[:, :width], weights, NN).astype(BF16)
    return attn, top * EXP2_SCALE + jnp.log2(total)


def gather_rows(src_ref, held_ref, inc_ref, rows, sems):
    def copy(ref, b, source):
        return pltpu.make_async_copy(ref.at[source], rows.at[pl.ds(b * BLK, BLK), :], sems.at[b])

    for b in range(NB):
        source = src_ref[b]

        @pl.when(source < NB)
        def _(b=b, source=source):
            copy(held_ref, b, source).start()

        @pl.when(source >= NB)
        def _(b=b, source=source):
            copy(inc_ref, b, source - NB).start()

    def wait_rows(tile):
        per_tile = TILE // BLK
        for b in range(tile * per_tile, (tile + 1) * per_tile):
            copy(held_ref, b, 0).wait()

    return wait_rows


def forward_kernel(
    core_ref, src_ref, held_ref, inc_ref, pack_ref, dout_hbm, _w1, _w2, _w3,
    rows_out, attn_out, stat_ref, keep_out, send_out,
    rows, attn_ref, keep_ref, send_ref, dout, value_t, sems, side_sems,
):
    wait_rows = gather_rows(src_ref, held_ref, inc_ref, rows, sems)
    dout_copy = pltpu.make_async_copy(dout_hbm, dout, side_sems.at[0])
    dout_copy.start()
    start = pack_ref[...]
    for tile in range(TILES):
        span = slice(tile * TILE, (tile + 1) * TILE)
        wait_rows(tile)
        value_t[:, span] = transposed(rows[span, VALUE])
        mask = keep_mask(tile, start)
        for head in range(HQ):
            attn, stat = forward_tile(rows, value_t, mask, head, tile)
            attn_ref[head * HD : (head + 1) * HD, span] = attn
            stat_ref[head : head + 1, span] = stat
    rows_copy = pltpu.make_async_copy(rows, rows_out, side_sems.at[1])
    rows_copy.start()
    attn_copy = pltpu.make_async_copy(attn_ref, attn_out, side_sems.at[2])
    attn_copy.start()
    dout_copy.wait()
    core = core_ref[0]
    mine = pl.multiple_of(core * HALF, HALF)
    other = pl.multiple_of((1 - core) * HALF, HALF)
    send_ref[...] = dot(attn_ref[...], dout[:, pl.ds(other, HALF)], NN).astype(BF16)
    send_copy = pltpu.make_async_copy(send_ref, send_out, side_sems.at[3])
    send_copy.start()
    keep_ref[...] = dot(attn_ref[...], dout[:, pl.ds(mine, HALF)], NN).astype(BF16)
    keep_copy = pltpu.make_async_copy(keep_ref, keep_out, side_sems.at[4])
    keep_copy.start()
    for copy in (rows_copy, attn_copy, send_copy, keep_copy):
        copy.wait()


def forward(core, src, held, inc, pack, dout, after):
    n = HQ * HD
    return pl.pallas_call(
        forward_kernel,
        out_shape=[
            shape((TOK, WIDTH)), shape((n, TOK)), shape((8, TOK), F32), shape((n, HALF)), shape((n, HALF))
        ],
        in_specs=[SMEM, SMEM, ANY, ANY, VMEM, ANY] + [ANY] * 3,
        out_specs=[ANY, ANY, VMEM, ANY, ANY],
        scratch_shapes=[
            pltpu.VMEM((TOK, WIDTH), BF16),
            pltpu.VMEM((n, TOK), BF16),
            pltpu.VMEM((n, HALF), BF16),
            pltpu.VMEM((n, HALF), BF16),
            pltpu.VMEM((TOK, D), BF16),
            pltpu.VMEM((HD, TOK), BF16),
            pltpu.SemaphoreType.DMA((NB,)),
            pltpu.SemaphoreType.DMA((5,)),
        ],
        compiler_params=params(LARGE),
        name="forward",
        cost_estimate=cost(12 * 10**9, 8 * 2**20, HQ * 655360),
    )(core, src, held, inc, pack, dout, *after)


PAIR = 2


def backward_kernel(
    rows_hbm, pack_ref, dt_hbm, attn_hbm, stat_ref, _, dq_out, kv_ref,
    rows, dt, attn_ref, key_t, weight_t, score_t, acc, dq, dq_sems, load_sems,
):
    loads = [
        pltpu.make_async_copy(source, target, load_sems.at[i])
        for i, (source, target) in enumerate(((rows_hbm, rows), (dt_hbm, dt), (attn_hbm, attn_ref)))
    ]
    for load in loads:
        load.start()
    for load in loads:
        load.wait()
    key_t[...] = transposed(rows[:, KEY])
    start = pack_ref[...]
    stores = []
    for first in range(0, HQ, PAIR):
        for head in range(first, first + PAIR):
            here = slice(head * HD, (head + 1) * HD)
            up = dt[here, :]
            delta = jnp.sum(up.astype(F32) * attn_ref[here, :].astype(F32), axis=0, keepdims=True)
            stat = stat_ref[head : head + 1, :]
            for tile in range(TILES):
                width = (tile + 1) * TILE
                span = slice(tile * TILE, width)
                at = (head - first) * TOK
                spot = slice(at + tile * TILE, at + width)
                scores = dot(rows[:width, KEY], rows[span, here], NT)
                mask = keep_mask(tile, start)
                prob = jnp.exp2(jnp.where(mask, scores * EXP2_SCALE - stat[:, span], -jnp.inf))
                weight_t[:width, spot] = prob.astype(BF16)
                dprob = dot(rows[:width, VALUE], up[:, span], NN)
                dscore = (prob * (dprob - delta[:, span])).astype(BF16)
                score_t[:width, spot] = dscore
                dq_t = dot(key_t[:, :width], dscore, NN) * SCALE
                dq[head, span, :] = dq_t.T.astype(BF16)
            store = pltpu.make_async_copy(dq.at[head], dq_out.at[:, pl.ds(head * HD, HD)], dq_sems.at[head])
            store.start()
            stores.append(store)
        for tile in range(TILES):
            span = slice(tile * TILE, (tile + 1) * TILE)
            dk = jnp.zeros((TILE, HD), F32) if first == 0 else acc[span, :HD]
            dv = jnp.zeros((TILE, HD), F32) if first == 0 else acc[span, HD:]
            for head in range(first, first + PAIR):
                here = slice(head * HD, (head + 1) * HD)
                at = (head - first) * TOK
                spot = slice(at + tile * TILE, at + TOK)
                dk = dk + dot(score_t[span, spot], rows[tile * TILE :, here], NN)
                dv = dv + dot(weight_t[span, spot], dt[here, tile * TILE :], NT)
            if first + PAIR == HQ:
                kv_ref[span, :HD] = (dk * SCALE).astype(BF16)
                kv_ref[span, HD:] = dv.astype(BF16)
            else:
                acc[span, :HD] = dk
                acc[span, HD:] = dv
    for store in stores:
        store.wait()


def backward(rows, pack, d_attn_t, attn_t, stats, after):
    return pl.pallas_call(
        backward_kernel,
        out_shape=[shape((TOK, HQ * HD)), shape((TOK, 2 * HD))],
        in_specs=[ANY, VMEM, ANY, ANY, VMEM, ANY],
        out_specs=[ANY, VMEM],
        scratch_shapes=[
            pltpu.VMEM((TOK, WIDTH), BF16),
            pltpu.VMEM((HQ * HD, TOK), BF16),
            pltpu.VMEM((HQ * HD, TOK), BF16),
            pltpu.VMEM((HD, TOK), BF16),
            pltpu.VMEM((TOK, PAIR * TOK), BF16),
            pltpu.VMEM((TOK, PAIR * TOK), BF16),
            pltpu.VMEM((TOK, 2 * HD), F32),
            pltpu.VMEM((HQ, TOK, HD), BF16),
            pltpu.SemaphoreType.DMA((HQ,)),
            pltpu.SemaphoreType.DMA((3,)),
        ],
        compiler_params=params(LARGE),
        name="backward",
        cost_estimate=cost(30 * 10**9, 8 * 2**20, HQ * 655360),
    )(rows, pack, d_attn_t, attn_t, stats, after)


def add_pair_kernel(x_ref, keep_ref, got_ref, *outs):
    x = x_ref[0]
    for k, out in enumerate(outs):
        shard = lax.rem(x + k, N_FSDP)
        out[...] = (keep_ref[shard].astype(F32) + got_ref[shard].astype(F32)).astype(out.dtype)


def add_pair(x, keep, got):
    rows = keep.shape[0] // N_FSDP
    dims = (rows, HALF)
    return pl.pallas_call(
        add_pair_kernel,
        out_shape=[shape(dims, F32)] + [shape(dims)] * 3,
        in_specs=[SMEM, VMEM, VMEM],
        out_specs=[VMEM] * 4,
        compiler_params=params(4),
        name="add_pair",
        cost_estimate=cost(4 * rows * HALF, 10 * rows * HALF * 2),
    )(x, keep.reshape(N_FSDP, *dims), got.reshape(N_FSDP, *dims))


def sum4(parts):
    total = parts[0].astype(F32)
    for part in parts[1:]:
        total = total + part.astype(F32)
    return total


def split_z_kernel(z_ref, _, *refs):
    parts, outs, total = refs[:4], refs[4:8], refs[8]
    total[...] = sum4([r[...] for r in parts])
    size = SHARD // 4
    z = z_ref[0]
    for k, out in enumerate(outs):
        at = pl.multiple_of(lax.rem(z + k, 4) * size, size)
        out[...] = total[pl.ds(at, size), :].astype(out.dtype)


def split_z(z, after, parts):
    dims = (SHARD // 4, HALF)
    return pl.pallas_call(
        split_z_kernel,
        out_shape=[shape(dims, F32)] + [shape(dims)] * 3,
        in_specs=[SMEM, ANY] + [VMEM] * 4,
        out_specs=[VMEM] * 4,
        scratch_shapes=[pltpu.VMEM((SHARD, HALF), F32)],
        compiler_params=params(4),
        name="split_z",
        cost_estimate=cost(4 * SHARD * HALF, 10 * SHARD * HALF),
    )(z, after, *parts)


def sum4_kernel(factor, *refs):
    refs[4][...] = (sum4([r[...] for r in refs[:4]]) * factor).astype(BF16)


def sum_four(parts, factor=1.0):
    return pl.pallas_call(
        functools.partial(sum4_kernel, factor),
        out_shape=shape(parts[0].shape),
        in_specs=[VMEM] * 4,
        out_specs=VMEM,
        compiler_params=params(8),
        name="sum_four",
        cost_estimate=cost(4 * parts[0].size, 10 * parts[0].size),
    )(*parts)


def lay_out_kernel(pos_ref, *refs):
    own, got, out = refs[:4], refs[4:8], refs[8]
    z, core = pos_ref[0], pos_ref[1]
    size = SHARD // 4
    for parts, side in ((own, core), (got, 1 - core)):
        columns = pl.ds(pl.multiple_of(side * HALF, HALF), HALF)
        for k, ref in enumerate(parts):
            at = pl.multiple_of(lax.rem(z - k + 4, 4) * size, size)
            out[pl.ds(at, size), columns] = ref[...].astype(F32)


def lay_out(pos, own, got):
    return pl.pallas_call(
        lay_out_kernel,
        out_shape=shape((SHARD, D), F32),
        in_specs=[SMEM] + [VMEM] * 8,
        out_specs=VMEM,
        compiler_params=params(8),
        name="lay_out",
        cost_estimate=cost(SHARD * D, 8 * SHARD * D),
    )(pos, *own, *got)


def dp_shift(dy, dz, dc):
    pairs = []
    for i in range(32):
        y, z, c = i // 8, (i // 2) % 4, i % 2
        pairs.append((i, ((y + dy) % 4) * 8 + ((z + dz) % 4) * 2 + (c + dc) % 2))
    return pairs


def x_shift(k):
    return [(i, (i + k) % N_FSDP) for i in range(N_FSDP)]


def per_device(stash, stash_place, pack_start, d_out, out_weight):
    group = lax.axis_index("dp")
    x = lax.axis_index("fsdp")
    core = lax.rem(group, 2)
    z = lax.rem(group // 2, 4)
    held = stash.reshape(NB, BLK, WIDTH)
    peers = jnp.arange(NB, dtype=jnp.int32)
    holder = stash_place // NB
    slot = stash_place % NB
    chosen = jnp.sum(jnp.where((holder == group) & (peers[:, None] != group), slot, 0), axis=1)
    mine = lax.dynamic_index_in_dim(stash_place, group, 0, keepdims=False)
    source = jnp.where(mine // NB == group, mine % NB, NB + mine // NB)
    x1, z1, core1 = x.reshape(1), z.reshape(1), core.reshape(1)

    incoming = lax.all_to_all(held[chosen], "dp", split_axis=0, concat_axis=0, tiled=True)
    weights = [out_weight] + [lax.ppermute(out_weight, "fsdp", x_shift(k)) for k in (1, 2, 3)]

    pack = pack_start.reshape(1, TOK)
    swap = dp_shift(0, 0, 1)
    rows, attn_t, stats, keep, send = forward(core1, source, held, incoming, pack, d_out, weights[1:])
    d_attn_t = d_attn_transposed(x1, weights, d_out)
    parts = add_pair(x1, keep, lax.ppermute(send, "dp", swap))
    by_x = [parts[0]] + [lax.ppermute(parts[k], "fsdp", x_shift(k)) for k in (1, 2, 3)]
    grad_query, grad_keyval = backward(rows, pack, d_attn_t, attn_t, stats, parts[0])
    by_z = split_z(z1, grad_keyval, by_x)
    by_z = [by_z[0]] + [lax.ppermute(by_z[k], "dp", dp_shift(0, k, 0)) for k in (1, 2, 3)]
    z_sum = sum_four(by_z)
    by_y = [z_sum] + [lax.ppermute(z_sum, "dp", dp_shift(k, 0, 0)) for k in (1, 2, 3)]
    factor = (TOK * lax.axis_size("dp") * lax.axis_size("fsdp")) ** (-0.5)
    total = sum_four(by_y, factor)
    own = [total] + [lax.ppermute(total, "dp", dp_shift(0, k, 0)) for k in (1, 2, 3)]
    got = [lax.ppermute(part, "dp", swap) for part in own]
    grad_weight = lay_out(jnp.stack([z, core]), own, got)
    return (grad_query, grad_keyval, grad_weight)


def solution(mesh):
    in_specs = (
        P("dp", "fsdp", None, None, None),
        P(),
        P(("dp", "fsdp")),
        P(("dp", "fsdp"), None),
        P("fsdp", None),
    )
    out_specs = (P(("dp", "fsdp"), None), P(("dp", "fsdp"), None), P("fsdp", None))
    return jax.shard_map(
        per_device, mesh=mesh, in_specs=in_specs, out_specs=out_specs, check_vma=False
    )
```

profile of v0, /device:TPU:1, one launch (start us, length us, event | category | flops | bytes accessed | tf_op | source)
XLA Modules:
  0.0 128.7 jit_solution(14265054225689198865)
XLA Ops:
  1.6 3.6 %gather_fusion = bf16[32,32,1024]{2,1,0:T(8,128)(2,1)} fusion(bf16[32,32,1024]{2,1,0:T(8,128)(2,1)} %bitcast.26, s32[1024]{0:T(1024)S(1)} %pad_clamp_fusion), kind=kCustom, calls=%fused_computation | custom fusion | bytes 4194432 | tf_op jit(solution)/shard_map/gather | solution.py:393
  5.2 9.7 %all-to-all-start = ((bf16[32,32,1024]{2,1,0:T(8,128)(2,1)}), bf16[32,32,1024]{2,1,0:T(8,128)(2,1)S(1)}, u32[]{:S(2)}, u32[]{:S(2)}) async-start(bf16[32,32,1024]{2,1,0:T(8,128)(2,1)} %gather_fusion), calls=%async_computation | async-start | bytes 4194304 | tf_op jit(solution)/shard_map/all_to_all | solution.py:393
  14.9 1.3 collective-permute-start
  16.2 2.5 %collective-permute-start.1 = (bf16[192,1536]{1,0:T(8,128)(2,1)S(1)}, bf16[192,1536]{1,0:T(8,128)(2,1)}, u32[]{:S(2)}, u32[]{:S(2)}) collective-permute-start(bf16[192,1536]{1,0:T(8,128)(2,1)S(1)} %copy-done.5), channel_id=1, source_target_pairs={{0,2},{1,3},{2,0},{3,1},{4,6},{5,7},{6,4},{7,5},{8,10},{9,11},{10,... | collective-permute-start | bytes 1769480 | tf_op jit(solution)/shard_map/ppermute | solution.py:394
  21.0 9.9 %collective-permute-done._w1.w1 = bf16[192,1536]{1,0:T(8,128)(2,1)S(1)} collective-permute-done((bf16[192,1536]{1,0:T(8,128)(2,1)S(1)}, bf16[192,1536]{1,0:T(8,128)(2,1)S(1)}, u32[]{:S(2)}, u32[]{:S(2)}) %collective-permute-start) | collective-permute-done | bytes 589856 | tf_op jit(solution)/shard_map/ppermute | solution.py:394
  30.9 13.7 %collective-permute-done.1._w2.w2 = bf16[192,1536]{1,0:T(8,128)(2,1)} collective-permute-done((bf16[192,1536]{1,0:T(8,128)(2,1)S(1)}, bf16[192,1536]{1,0:T(8,128)(2,1)}, u32[]{:S(2)}, u32[]{:S(2)}) %collective-permute-start.1) | collective-permute-done | bytes 589856 | tf_op jit(solution)/shard_map/ppermute | solution.py:394
  44.7 1.3 copy-done.4
  46.0 20.5 %forward.1 = (bf16[1024,1024]{1,0:T(8,128)(2,1)}, bf16[768,1024]{1,0:T(8,128)(2,1)}, f32[8,1024]{1,0:T(8,128)}, bf16[768,768]{1,0:T(8,128)(2,1)}, bf16[768,768]{1,0:T(8,128)(2,1)}) custom-call(s32[1]{0:T(128)} %bitcast.core_ref, s32[32]{0:T(128)} %compare_select_fusion.1.src_ref, bf16[32,32,1024]{2,1,0:T(8,128)(2,1)} %bitcast.27, ...), custom_call_target="tpu_custom_call" | custom-call | flops 12000000000 | bytes 8388608 | tf_op jit(solution)/shard_map/forward/pallas_call | solution.py:168
  67.6 7.5 %d_attn.1.dt_hbm = bf16[768,1024]{1,0:T(8,128)(2,1)} custom-call(s32[1]{0:T(128)} %bitcast.6.x_ref, bf16[192,1536]{1,0:T(8,128)(2,1)} %w0.1, bf16[192,1536]{1,0:T(8,128)(2,1)} %copy-done.6, bf16[192,1536]{1,0:T(8,128)(2,1)} %collective-permute-done.1._w2.w2, bf16[192,1536]{1,0:T(8,128)(2,1)} %collective-permute-done.2._w3.w3, bf16[1024,1536]{1,0:T(8,128)(2,1)} %dout_ref.1), custom_call_target="tpu_custom_call" | custom-call | flops 2415919104 | bytes 8388608 | tf_op jit(solution)/shard_map/d_attn/pallas_call | solution.py:71
  77.3 2.1 %collective-permute-start.5 = (bf16[192,768]{1,0:T(8,128)(2,1)S(1)}, bf16[192,768]{1,0:T(8,128)(2,1)S(1)}, u32[]{:S(2)}, u32[]{:S(2)}) collective-permute-start(bf16[192,768]{1,0:T(8,128)(2,1)S(1)} %get-tuple-element.27), channel_id=1, source_target_pairs={{0,2},{1,3},{2,0},{3,1},{4,6},{5,7},{6,4},{7,5},{8,10},{9,11},{10,... | collective-permute-start | bytes 884744 | tf_op jit(solution)/shard_map/ppermute | solution.py:401
  79.4 1.3 collective-permute-start.6
  80.7 17.0 %backward.1 = (bf16[1024,768]{1,0:T(8,128)(2,1)}, bf16[1024,256]{1,0:T(8,128)(2,1)}) custom-call(bf16[1024,1024]{1,0:T(8,128)(2,1)} %get-tuple-element.18.rows_hbm, s32[1,1024]{1,0:T(1,128)} %bitcast.29, bf16[768,1024]{1,0:T(8,128)(2,1)} %d_attn.1.dt_hbm, bf16[768,1024]{1,0:T(8,128)(2,1)} %get-tuple-element.19.attn_hbm, ...), custom_call_target="tpu_custom_call" | custom-call | flops 30000001024 | bytes 8388608 | tf_op jit(solution)/shard_map/backward/pallas_call | solution.py:253
  98.9 1.7 %collective-permute-start.7 = (bf16[48,768]{1,0:T(8,128)(2,1)S(1)}, bf16[48,768]{1,0:T(8,128)(2,1)S(1)}, u32[]{:S(2)}, u32[]{:S(2)}) collective-permute-start(bf16[48,768]{1,0:T(8,128)(2,1)S(1)} %get-tuple-element.30), channel_id=1, source_target_pairs={{0,8},{4,12},{8,16},{12,20},{16,24},{20,28},{24,0},{28,4},{32,40},... | collective-permute-start | bytes 221192 | tf_op jit(solution)/shard_map/ppermute | solution.py:404
  100.6 2.4 %collective-permute-start.8 = (bf16[48,768]{1,0:T(8,128)(2,1)S(1)}, bf16[48,768]{1,0:T(8,128)(2,1)S(1)}, u32[]{:S(2)}, u32[]{:S(2)}) collective-permute-start(bf16[48,768]{1,0:T(8,128)(2,1)S(1)} %get-tuple-element.31), channel_id=1, source_target_pairs={{0,16},{4,20},{8,24},{12,28},{16,0},{20,4},{24,8},{28,12},{32,48},... | collective-permute-start | bytes 221192 | tf_op jit(solution)/shard_map/ppermute | solution.py:404
  104.2 1.5 %collective-permute-done.8.refs_2_ = bf16[48,768]{1,0:T(8,128)(2,1)S(1)} collective-permute-done((bf16[48,768]{1,0:T(8,128)(2,1)S(1)}, bf16[48,768]{1,0:T(8,128)(2,1)S(1)}, u32[]{:S(2)}, u32[]{:S(2)}) %collective-permute-start.8) | collective-permute-done | bytes 73760 | tf_op jit(solution)/shard_map/ppermute | solution.py:404
  107.0 1.5 %collective-permute-start.10 = (bf16[48,768]{1,0:T(8,128)(2,1)S(1)}, bf16[48,768]{1,0:T(8,128)(2,1)S(1)}, u32[]{:S(2)}, u32[]{:S(2)}) collective-permute-start(bf16[48,768]{1,0:T(8,128)(2,1)S(1)} %sum_four.2.refs_0_), channel_id=1, source_target_pairs={{0,32},{4,36},{8,40},{12,44},{16,48},{20,52},{24,56},{28,60},{32,6... | collective-permute-start | bytes 221192 | tf_op jit(solution)/shard_map/ppermute | solution.py:406
  108.5 2.4 %collective-permute-start.11 = (bf16[48,768]{1,0:T(8,128)(2,1)S(1)}, bf16[48,768]{1,0:T(8,128)(2,1)S(1)}, u32[]{:S(2)}, u32[]{:S(2)}) collective-permute-start(bf16[48,768]{1,0:T(8,128)(2,1)S(1)} %sum_four.2.refs_0_), channel_id=1, source_target_pairs={{0,64},{4,68},{8,72},{12,76},{16,80},{20,84},{24,88},{28,92},{32,9... | collective-permute-start | bytes 221192 | tf_op jit(solution)/shard_map/ppermute | solution.py:406
  112.1 1.4 %collective-permute-done.11.refs_2_ = bf16[48,768]{1,0:T(8,128)(2,1)S(1)} collective-permute-done((bf16[48,768]{1,0:T(8,128)(2,1)S(1)}, bf16[48,768]{1,0:T(8,128)(2,1)S(1)}, u32[]{:S(2)}, u32[]{:S(2)}) %collective-permute-start.11) | collective-permute-done | bytes 73760 | tf_op jit(solution)/shard_map/ppermute | solution.py:406
  114.6 3.3 %collective-permute-start.14 = (bf16[48,768]{1,0:T(8,128)(2,1)S(1)}, bf16[48,768]{1,0:T(8,128)(2,1)S(1)}, u32[]{:S(2)}, u32[]{:S(2)}) collective-permute-start(bf16[48,768]{1,0:T(8,128)(2,1)S(1)} %sum_four.3.refs_0_), channel_id=1, source_target_pairs={{0,16},{4,20},{8,24},{12,28},{16,0},{20,4},{24,8},{28,12},{32,48},... | collective-permute-start | bytes 221192 | tf_op jit(solution)/shard_map/ppermute | solution.py:409
  118.0 4.0 %collective-permute-start.16 = (bf16[48,768]{1,0:T(8,128)(2,1)S(1)}, bf16[48,768]{1,0:T(8,128)(2,1)S(1)}, u32[]{:S(2)}, u32[]{:S(2)}) collective-permute-start(bf16[48,768]{1,0:T(8,128)(2,1)S(1)} %sum_four.3.refs_0_), channel_id=1, source_target_pairs={{0,4},{4,0},{8,12},{12,8},{16,20},{20,16},{24,28},{28,24},{32,36},... | collective-permute-start | bytes 221192 | tf_op jit(solution)/shard_map/ppermute | solution.py:410
  122.0 1.3 collective-permute-start.17
  123.2 1.7 %collective-permute-start.18 = (bf16[48,768]{1,0:T(8,128)(2,1)S(1)}, bf16[48,768]{1,0:T(8,128)(2,1)S(1)}, u32[]{:S(2)}, u32[]{:S(2)}) collective-permute-start(bf16[48,768]{1,0:T(8,128)(2,1)S(1)} %collective-permute-done.14.refs_2_), channel_id=1, source_target_pairs={{0,4},{4,0},{8,12},{12,8},{16,20},{20,16},{24,28},{28,24},{32,36},... | collective-permute-start | bytes 221192 | tf_op jit(solution)/shard_map/ppermute | solution.py:410
  124.9 1.2 collective-permute-start.19
  127.0 1.6 %lay_out.1 = f32[192,1536]{1,0:T(8,128)} custom-call(s32[2]{0:T(128)S(1)} %pad_add_fusion.pos_ref, bf16[48,768]{1,0:T(8,128)(2,1)S(1)} %sum_four.3.refs_0_, bf16[48,768]{1,0:T(8,128)(2,1)S(1)} %collective-permute-done.13.refs_1_, bf16[48,768]{1,0:T(8,128)(2,1)S(1)} %collective-permute-done.14.refs_2_, bf16[48,768]{1,0:T(8,128)(2,1)S(1)} %collective-permute-done.15.refs_3_, ...), custom_call_target="tpu_custom_call" | custom-call | flops 294912 | bytes 2359296 | tf_op jit(solution)/shard_map/lay_out/pallas_call | solution.py:356
  (47 shorter events, 13.5 us)
Async XLA Ops:
  5.2 9.7 %copy-start.5 = (bf16[192,1536]{1,0:T(8,128)(2,1)S(1)}, bf16[192,1536]{1,0:T(8,128)(2,1)}, u32[]{:S(2)}) copy-start(bf16[192,1536]{1,0:T(8,128)(2,1)} %w0.1) | copy-start | bytes 1769476
  5.2 39.5 %all-to-all-start = ((bf16[32,32,1024]{2,1,0:T(8,128)(2,1)}), bf16[32,32,1024]{2,1,0:T(8,128)(2,1)S(1)}, u32[]{:S(2)}, u32[]{:S(2)}) async-start(bf16[32,32,1024]{2,1,0:T(8,128)(2,1)} %gather_fusion), calls=%async_computation | async-start | bytes 4194304 | tf_op jit(solution)/shard_map/all_to_all | solution.py:393
  14.9 16.0 %collective-permute-start = (bf16[192,1536]{1,0:T(8,128)(2,1)S(1)}, bf16[192,1536]{1,0:T(8,128)(2,1)S(1)}, u32[]{:S(2)}, u32[]{:S(2)}) collective-permute-start(bf16[192,1536]{1,0:T(8,128)(2,1)S(1)} %copy-done.5), channel_id=1, source_target_pairs={{0,1},{1,2},{2,3},{3,0},{4,5},{5,6},{6,7},{7,4},{8,9},{9,10},{10,1... | collective-permute-start | bytes 1769480 | tf_op jit(solution)/shard_map/ppermute | solution.py:394
  16.2 28.4 %collective-permute-start.1 = (bf16[192,1536]{1,0:T(8,128)(2,1)S(1)}, bf16[192,1536]{1,0:T(8,128)(2,1)}, u32[]{:S(2)}, u32[]{:S(2)}) collective-permute-start(bf16[192,1536]{1,0:T(8,128)(2,1)S(1)} %copy-done.5), channel_id=1, source_target_pairs={{0,2},{1,3},{2,0},{3,1},{4,6},{5,7},{6,4},{7,5},{8,10},{9,11},{10,... | collective-permute-start | bytes 1769480 | tf_op jit(solution)/shard_map/ppermute | solution.py:394
  18.7 26.0 %collective-permute-start.2 = (bf16[192,1536]{1,0:T(8,128)(2,1)S(1)}, bf16[192,1536]{1,0:T(8,128)(2,1)}, u32[]{:S(2)}, u32[]{:S(2)}) collective-permute-start(bf16[192,1536]{1,0:T(8,128)(2,1)S(1)} %copy-done.5), channel_id=1, source_target_pairs={{0,3},{1,0},{2,1},{3,2},{4,7},{5,4},{6,5},{7,6},{8,11},{9,8},{10,9... | collective-permute-start | bytes 1769480 | tf_op jit(solution)/shard_map/ppermute | solution.py:394
  30.9 13.7 %copy-start.6 = (bf16[192,1536]{1,0:T(8,128)(2,1)}, bf16[192,1536]{1,0:T(8,128)(2,1)S(1)}, u32[]{:S(2)}) copy-start(bf16[192,1536]{1,0:T(8,128)(2,1)S(1)} %collective-permute-done._w1.w1) | copy-start | bytes 1769476
  66.5 8.6 %collective-permute-start.3 = (bf16[768,768]{1,0:T(8,128)(2,1)}, bf16[768,768]{1,0:T(8,128)(2,1)S(1)}, u32[]{:S(2)}, u32[]{:S(2)}) collective-permute-start(bf16[768,768]{1,0:T(8,128)(2,1)} %get-tuple-element.22), channel_id=1, source_target_pairs={{0,4},{4,0},{8,12},{12,8},{16,20},{20,16},{24,28},{28,24},{32,36},... | collective-permute-start | bytes 3538952 | tf_op jit(solution)/shard_map/ppermute | solution.py:400
  76.2 21.4 %collective-permute-start.4 = (bf16[192,768]{1,0:T(8,128)(2,1)S(1)}, bf16[192,768]{1,0:T(8,128)(2,1)S(1)}, u32[]{:S(2)}, u32[]{:S(2)}) collective-permute-start(bf16[192,768]{1,0:T(8,128)(2,1)S(1)} %get-tuple-element.26), channel_id=1, source_target_pairs={{0,1},{1,2},{2,3},{3,0},{4,5},{5,6},{6,7},{7,4},{8,9},{9,10},{10,1... | collective-permute-start | bytes 884744 | tf_op jit(solution)/shard_map/ppermute | solution.py:401
  77.3 20.4 %collective-permute-start.5 = (bf16[192,768]{1,0:T(8,128)(2,1)S(1)}, bf16[192,768]{1,0:T(8,128)(2,1)S(1)}, u32[]{:S(2)}, u32[]{:S(2)}) collective-permute-start(bf16[192,768]{1,0:T(8,128)(2,1)S(1)} %get-tuple-element.27), channel_id=1, source_target_pairs={{0,2},{1,3},{2,0},{3,1},{4,6},{5,7},{6,4},{7,5},{8,10},{9,11},{10,... | collective-permute-start | bytes 884744 | tf_op jit(solution)/shard_map/ppermute | solution.py:401
  79.4 18.3 %collective-permute-start.6 = (bf16[192,768]{1,0:T(8,128)(2,1)S(1)}, bf16[192,768]{1,0:T(8,128)(2,1)S(1)}, u32[]{:S(2)}, u32[]{:S(2)}) collective-permute-start(bf16[192,768]{1,0:T(8,128)(2,1)S(1)} %get-tuple-element.28), channel_id=1, source_target_pairs={{0,3},{1,0},{2,1},{3,2},{4,7},{5,4},{6,5},{7,6},{8,11},{9,8},{10,9... | collective-permute-start | bytes 884744 | tf_op jit(solution)/shard_map/ppermute | solution.py:401
  80.6 17.0 %copy-start.2 = (f32[192,768]{1,0:T(8,128)S(1)}, f32[192,768]{1,0:T(8,128)}, u32[]{:S(2)}) copy-start(f32[192,768]{1,0:T(8,128)} %copy-done.1) | copy-start | bytes 1769476
  98.9 5.3 %collective-permute-start.7 = (bf16[48,768]{1,0:T(8,128)(2,1)S(1)}, bf16[48,768]{1,0:T(8,128)(2,1)S(1)}, u32[]{:S(2)}, u32[]{:S(2)}) collective-permute-start(bf16[48,768]{1,0:T(8,128)(2,1)S(1)} %get-tuple-element.30), channel_id=1, source_target_pairs={{0,8},{4,12},{8,16},{12,20},{16,24},{20,28},{24,0},{28,4},{32,40},... | collective-permute-start | bytes 221192 | tf_op jit(solution)/shard_map/ppermute | solution.py:404
  100.6 5.1 %collective-permute-start.8 = (bf16[48,768]{1,0:T(8,128)(2,1)S(1)}, bf16[48,768]{1,0:T(8,128)(2,1)S(1)}, u32[]{:S(2)}, u32[]{:S(2)}) collective-permute-start(bf16[48,768]{1,0:T(8,128)(2,1)S(1)} %get-tuple-element.31), channel_id=1, source_target_pairs={{0,16},{4,20},{8,24},{12,28},{16,0},{20,4},{24,8},{28,12},{32,48},... | collective-permute-start | bytes 221192 | tf_op jit(solution)/shard_map/ppermute | solution.py:404
  103.0 3.9 %collective-permute-start.9 = (bf16[48,768]{1,0:T(8,128)(2,1)S(1)}, bf16[48,768]{1,0:T(8,128)(2,1)S(1)}, u32[]{:S(2)}, u32[]{:S(2)}) collective-permute-start(bf16[48,768]{1,0:T(8,128)(2,1)S(1)} %get-tuple-element.32), channel_id=1, source_target_pairs={{0,24},{4,28},{8,0},{12,4},{16,8},{20,12},{24,16},{28,20},{32,56},... | collective-permute-start | bytes 221192 | tf_op jit(solution)/shard_map/ppermute | solution.py:404
  107.0 5.1 %collective-permute-start.10 = (bf16[48,768]{1,0:T(8,128)(2,1)S(1)}, bf16[48,768]{1,0:T(8,128)(2,1)S(1)}, u32[]{:S(2)}, u32[]{:S(2)}) collective-permute-start(bf16[48,768]{1,0:T(8,128)(2,1)S(1)} %sum_four.2.refs_0_), channel_id=1, source_target_pairs={{0,32},{4,36},{8,40},{12,44},{16,48},{20,52},{24,56},{28,60},{32,6... | collective-permute-start | bytes 221192 | tf_op jit(solution)/shard_map/ppermute | solution.py:406
  108.5 5.0 %collective-permute-start.11 = (bf16[48,768]{1,0:T(8,128)(2,1)S(1)}, bf16[48,768]{1,0:T(8,128)(2,1)S(1)}, u32[]{:S(2)}, u32[]{:S(2)}) collective-permute-start(bf16[48,768]{1,0:T(8,128)(2,1)S(1)} %sum_four.2.refs_0_), channel_id=1, source_target_pairs={{0,64},{4,68},{8,72},{12,76},{16,80},{20,84},{24,88},{28,92},{32,9... | collective-permute-start | bytes 221192 | tf_op jit(solution)/shard_map/ppermute | solution.py:406
  110.9 3.6 %collective-permute-start.12 = (bf16[48,768]{1,0:T(8,128)(2,1)S(1)}, bf16[48,768]{1,0:T(8,128)(2,1)S(1)}, u32[]{:S(2)}, u32[]{:S(2)}) collective-permute-start(bf16[48,768]{1,0:T(8,128)(2,1)S(1)} %sum_four.2.refs_0_), channel_id=1, source_target_pairs={{0,96},{4,100},{8,104},{12,108},{16,112},{20,116},{24,120},{28,124... | collective-permute-start | bytes 221192 | tf_op jit(solution)/shard_map/ppermute | solution.py:406
  114.6 7.4 %collective-permute-start.13 = (bf16[48,768]{1,0:T(8,128)(2,1)S(1)}, bf16[48,768]{1,0:T(8,128)(2,1)S(1)}, u32[]{:S(2)}, u32[]{:S(2)}) collective-permute-start(bf16[48,768]{1,0:T(8,128)(2,1)S(1)} %sum_four.3.refs_0_), channel_id=1, source_target_pairs={{0,8},{4,12},{8,16},{12,20},{16,24},{20,28},{24,0},{28,4},{32,40},... | collective-permute-start | bytes 221192 | tf_op jit(solution)/shard_map/ppermute | solution.py:409
  114.6 8.6 %collective-permute-start.14 = (bf16[48,768]{1,0:T(8,128)(2,1)S(1)}, bf16[48,768]{1,0:T(8,128)(2,1)S(1)}, u32[]{:S(2)}, u32[]{:S(2)}) collective-permute-start(bf16[48,768]{1,0:T(8,128)(2,1)S(1)} %sum_four.3.refs_0_), channel_id=1, source_target_pairs={{0,16},{4,20},{8,24},{12,28},{16,0},{20,4},{24,8},{28,12},{32,48},... | collective-permute-start | bytes 221192 | tf_op jit(solution)/shard_map/ppermute | solution.py:409
  118.0 6.9 %collective-permute-start.15 = (bf16[48,768]{1,0:T(8,128)(2,1)S(1)}, bf16[48,768]{1,0:T(8,128)(2,1)S(1)}, u32[]{:S(2)}, u32[]{:S(2)}) collective-permute-start(bf16[48,768]{1,0:T(8,128)(2,1)S(1)} %sum_four.3.refs_0_), channel_id=1, source_target_pairs={{0,24},{4,28},{8,0},{12,4},{16,8},{20,12},{24,16},{28,20},{32,56},... | collective-permute-start | bytes 221192 | tf_op jit(solution)/shard_map/ppermute | solution.py:409
  118.0 8.2 %collective-permute-start.16 = (bf16[48,768]{1,0:T(8,128)(2,1)S(1)}, bf16[48,768]{1,0:T(8,128)(2,1)S(1)}, u32[]{:S(2)}, u32[]{:S(2)}) collective-permute-start(bf16[48,768]{1,0:T(8,128)(2,1)S(1)} %sum_four.3.refs_0_), channel_id=1, source_target_pairs={{0,4},{4,0},{8,12},{12,8},{16,20},{20,16},{24,28},{28,24},{32,36},... | collective-permute-start | bytes 221192 | tf_op jit(solution)/shard_map/ppermute | solution.py:410
  122.0 4.2 %collective-permute-start.17 = (bf16[48,768]{1,0:T(8,128)(2,1)S(1)}, bf16[48,768]{1,0:T(8,128)(2,1)S(1)}, u32[]{:S(2)}, u32[]{:S(2)}) collective-permute-start(bf16[48,768]{1,0:T(8,128)(2,1)S(1)} %collective-permute-done.13.refs_1_), channel_id=1, source_target_pairs={{0,4},{4,0},{8,12},{12,8},{16,20},{20,16},{24,28},{28,24},{32,36},... | collective-permute-start | bytes 221192 | tf_op jit(solution)/shard_map/ppermute | solution.py:410
  123.2 3.0 %collective-permute-start.18 = (bf16[48,768]{1,0:T(8,128)(2,1)S(1)}, bf16[48,768]{1,0:T(8,128)(2,1)S(1)}, u32[]{:S(2)}, u32[]{:S(2)}) collective-permute-start(bf16[48,768]{1,0:T(8,128)(2,1)S(1)} %collective-permute-done.14.refs_2_), channel_id=1, source_target_pairs={{0,4},{4,0},{8,12},{12,8},{16,20},{20,16},{24,28},{28,24},{32,36},... | collective-permute-start | bytes 221192 | tf_op jit(solution)/shard_map/ppermute | solution.py:410
  124.9 2.1 %collective-permute-start.19 = (bf16[48,768]{1,0:T(8,128)(2,1)S(1)}, bf16[48,768]{1,0:T(8,128)(2,1)S(1)}, u32[]{:S(2)}, u32[]{:S(2)}) collective-permute-start(bf16[48,768]{1,0:T(8,128)(2,1)S(1)} %collective-permute-done.15.refs_3_), channel_id=1, source_target_pairs={{0,4},{4,0},{8,12},{12,8},{16,20},{20,16},{24,28},{28,24},{32,36},... | collective-permute-start | bytes 221192 | tf_op jit(solution)/shard_map/ppermute | solution.py:410
  (4 other events, 10.7 us)
where the time goes:
time: 129 us
  Pallas kernels  47.2 us (37%)
  starting transfers between devices  42.1 us (33%)
  waiting for transfers between devices  29.6 us (23%)
  local copies, waits for them, and re-layouts  6.77 us (5%)
  other arithmetic  2.21 us (2%)
    ppermute x3, waiting for transfers between devices, per_device(): lax.ppermute(out_weight, 'fsdp', x_shift(k))  23.6 us
    pallas_call x1, Pallas kernels, forward(): pl.pallas_call(forward_kernel, out_shape=[shape((TOK, WIDTH)), shape((n,...  20.5 us
    pallas_call x1, Pallas kernels, backward(): pl.pallas_call(backward_kernel, out_shape=[shape((TOK, HQ * HD)), shape((...  17 us
    all_to_all x1, starting transfers between devices, per_device(): lax.all_to_all(held[chosen], 'dp', split_axis=0, concat_axis=0, tiled=True)  9.73 us
    ppermute x4, starting transfers between devices, per_device(): got = [lax.ppermute(part, 'dp', swap) for part in own]  8.15 us
    pallas_call x1, Pallas kernels, d_attn_transposed(): pl.pallas_call(d_attn_kernel, grid=(TILES,), out_shape=shape((HQ * HD, TO...  7.49 us
    ppermute x3, starting transfers between devices, per_device(): lax.ppermute(by_z[k], 'dp', dp_shift(0, k, 0))  5.29 us
    ppermute x3, starting transfers between devices, per_device(): lax.ppermute(z_sum, 'dp', dp_shift(k, 0, 0))  5.05 us
  transfers between devices with their start and end apart: 21, of which 7 were waited for; matrix products, arithmetic and copies ran while one was open for 1% of the time, Pallas kernels for 19%

commit v1 on v0

v1 whole, which is shorter than its diff:
```python
import functools

import jax
import jax.numpy as jnp
from jax import lax
from jax.experimental import pallas as pl
from jax.experimental.pallas import tpu as pltpu
from jax.sharding import PartitionSpec as P

HQ = 6
HD = 128
TILE = 256
TOK = 1024
TILES = TOK // TILE
D = 1536
HALF = D // 2
NB = 32
BLK = 32
WIDTH = 1024
N_FSDP = 4
SHARD = HQ * HD // N_FSDP
SCALE = HD ** (-0.5)
EXP2_SCALE = SCALE * 1.4426950408889634
KEY = slice(HQ * HD, (HQ + 1) * HD)
VALUE = slice((HQ + 1) * HD, (HQ + 2) * HD)
NT = (((1,), (1,)), ((), ()))
NN = (((1,), (0,)), ((), ()))
ANY = pl.BlockSpec(memory_space=pl.ANY)
SMEM = pl.BlockSpec(memory_space=pltpu.SMEM)
VMEM = pl.BlockSpec(memory_space=pltpu.VMEM)
HBM = pl.BlockSpec(memory_space=pltpu.HBM)


def params(mib):
    return pltpu.CompilerParams(vmem_limit_bytes=mib * 2**20)


BF16 = jnp.bfloat16
LARGE = 56
F32 = jnp.float32


def dot(a, b, dims):
    return lax.dot_general(a, b, dims, preferred_element_type=F32)


def shape(dims, dtype=BF16):
    return jax.ShapeDtypeStruct(dims, dtype)


TOKEN = shape((8, 128), F32)


def cost(flops, size, exps=0):
    return pl.CostEstimate(flops=int(flops), bytes_accessed=int(size), transcendentals=int(exps))


def d_attn_kernel(pos_ref, *refs):
    own, mine, others, dout_hbm, out_ref, weight, dout, sems, dout_sem = (
        refs[0], refs[1:4], refs[4:7], *refs[7:]
    )
    x, core = pos_ref[0], pos_ref[1]

    def shard_rows(k):
        return pl.ds(pl.multiple_of(lax.rem(x - k + N_FSDP, N_FSDP) * SHARD, SHARD), SHARD)

    loads = [pltpu.make_async_copy(own, weight.at[shard_rows(0), :], sems.at[0])]
    for k in range(1, N_FSDP):
        for i, (part, side) in enumerate(((mine[k - 1], core), (others[k - 1], 1 - core))):
            columns = pl.ds(pl.multiple_of(side * HALF, HALF), HALF)
            loads.append(pltpu.make_async_copy(part, weight.at[shard_rows(k), columns], sems.at[2 * k - 1 + i]))
    block = pltpu.make_async_copy(dout_hbm, dout, dout_sem)
    for load in loads + [block]:
        load.start()
    for load in loads:
        load.wait()
    block.wait()
    out_ref[...] = dot(weight[...], dout[...], NT).astype(BF16)


def d_attn_transposed(pos, own, mine, others, dout):
    return pl.pallas_call(
        d_attn_kernel,
        out_shape=shape((HQ * HD, TOK)),
        in_specs=[SMEM] + [ANY] * 8,
        out_specs=VMEM,
        scratch_shapes=[
            pltpu.VMEM((HQ * HD, D), BF16),
            pltpu.VMEM((TOK, D), BF16),
            pltpu.SemaphoreType.DMA((7,)),
            pltpu.SemaphoreType.DMA,
        ],
        compiler_params=params(LARGE),
        name="d_attn",
        cost_estimate=cost(2 * TOK * D * HQ * HD, 8 * 2**20),
    )(pos, own, *mine, *others, dout)


def keep_mask(tile, start):
    width = (tile + 1) * TILE
    key = lax.broadcasted_iota(jnp.int32, (width, TILE), 0)
    query = tile * TILE + lax.broadcasted_iota(jnp.int32, (width, TILE), 1)
    return (key >= start[:, tile * TILE : width]) & (key <= query)


def transposed(x):
    return x.astype(F32).T.astype(BF16)


def gather_rows(src_ref, held_ref, inc_ref, rows, sems):
    def copy(ref, b, source):
        return pltpu.make_async_copy(ref.at[source], rows.at[pl.ds(b * BLK, BLK), :], sems.at[b])

    for b in range(NB):
        source = src_ref[b]

        @pl.when(source < NB)
        def _(b=b, source=source):
            copy(held_ref, b, source).start()

        @pl.when(source >= NB)
        def _(b=b, source=source):
            copy(inc_ref, b, source - NB).start()

    def wait_rows(tile):
        per_tile = TILE // BLK
        for b in range(tile * per_tile, (tile + 1) * per_tile):
            copy(held_ref, b, 0).wait()

    return wait_rows


def forward_kernel(
    core_ref, src_ref, held_ref, inc_ref, pack_ref, dout_hbm, _,
    rows_out, attn_out, stat_ref, send_out,
    rows, attn_ref, send_ref, dout, value_t, sems, side_sems, attn_sems,
):
    wait_rows = gather_rows(src_ref, held_ref, inc_ref, rows, sems)
    other = pl.ds(pl.multiple_of((1 - core_ref[0]) * HALF, HALF), HALF)
    dout_copy = pltpu.make_async_copy(dout_hbm.at[:, other], dout, side_sems.at[0])
    dout_copy.start()
    rows_copy = pltpu.make_async_copy(rows, rows_out, side_sems.at[1])
    send_copy = pltpu.make_async_copy(send_ref, send_out, side_sems.at[2])
    attn_copies = [
        pltpu.make_async_copy(
            attn_ref.at[pl.ds(h * HD, HD), :], attn_out.at[pl.ds(h * HD, HD), :], attn_sems.at[h]
        )
        for h in range(HQ)
    ]
    start = pack_ref[...]
    for tile in range(TILES):
        width = (tile + 1) * TILE
        span = slice(tile * TILE, width)
        wait_rows(tile)
        if tile == TILES - 1:
            rows_copy.start()
        value_t[:, span] = transposed(rows[span, VALUE])
        mask = keep_mask(tile, start)

        def raw_scores(head, width=width, span=span):
            return dot(rows[:width, KEY], rows[span, head * HD : (head + 1) * HD], NT)

        ahead = raw_scores(0)
        for head in range(HQ):
            here = slice(head * HD, (head + 1) * HD)
            scores = ahead
            if head + 1 < HQ:
                ahead = raw_scores(head + 1)
            scores = jnp.where(mask, scores, -jnp.inf)
            top = jnp.max(scores, axis=0, keepdims=True)
            expo = jnp.exp2((scores - top) * EXP2_SCALE)
            total = jnp.sum(expo, axis=0, keepdims=True)
            weights = (expo * (1.0 / total)).astype(BF16)
            attn_ref[here, span] = dot(value_t[:, :width], weights, NN).astype(BF16)
            stat_ref[head : head + 1, span] = top * EXP2_SCALE + jnp.log2(total)
    for copy in attn_copies:
        copy.start()
    dout_copy.wait()
    send_ref[...] = dot(attn_ref[...], dout[...], NN).astype(BF16)
    send_copy.start()
    for copy in (rows_copy, *attn_copies, send_copy):
        copy.wait()


def forward(core, src, held, inc, pack, dout, after):
    n = HQ * HD
    return pl.pallas_call(
        forward_kernel,
        out_shape=[
            shape((TOK, WIDTH)), shape((n, TOK)), shape((8, TOK), F32), shape((n, HALF))
        ],
        in_specs=[SMEM, SMEM, ANY, ANY, VMEM, ANY, ANY],
        out_specs=[ANY, ANY, VMEM, ANY],
        scratch_shapes=[
            pltpu.VMEM((TOK, WIDTH), BF16),
            pltpu.VMEM((n, TOK), BF16),
            pltpu.VMEM((n, HALF), BF16),
            pltpu.VMEM((TOK, HALF), BF16),
            pltpu.VMEM((HD, TOK), BF16),
            pltpu.SemaphoreType.DMA((NB,)),
            pltpu.SemaphoreType.DMA((3,)),
            pltpu.SemaphoreType.DMA((HQ,)),
        ],
        compiler_params=params(LARGE),
        name="forward",
        cost_estimate=cost(12 * 10**9, 8 * 2**20, HQ * 655360),
    )(core, src, held, inc, pack, dout, after)


def keep_kernel(core_ref, attn_ref, dout_hbm, keep_ref, dout, sem):
    mine = pl.ds(pl.multiple_of(core_ref[0] * HALF, HALF), HALF)
    load = pltpu.make_async_copy(dout_hbm.at[:, mine], dout, sem)
    load.start()
    load.wait()
    keep_ref[...] = dot(attn_ref[...], dout[...], NN).astype(BF16)


def keep_half(core, attn_t, dout):
    return pl.pallas_call(
        keep_kernel,
        out_shape=shape((HQ * HD, HALF)),
        in_specs=[SMEM, VMEM, ANY],
        out_specs=VMEM,
        scratch_shapes=[pltpu.VMEM((TOK, HALF), BF16), pltpu.SemaphoreType.DMA],
        compiler_params=params(12),
        name="keep_half",
        cost_estimate=cost(2 * TOK * HALF * HQ * HD, 8 * 2**20),
    )(core, attn_t, dout)


PAIR = 2


def backward_kernel(
    rows_hbm, pack_ref, dt_hbm, attn_hbm, stat_ref, _, dq_out, kv_ref, token,
    rows, dt, attn_ref, key_t, weight_t, score_t, acc, dq, dq_sems, load_sems,
):
    token[...] = jnp.zeros(token.shape, F32)
    rows_load = pltpu.make_async_copy(rows_hbm, rows, load_sems.at[0])
    rows_load.start()
    head_loads = []
    for h in range(HQ):
        here = pl.ds(h * HD, HD)
        head_loads.append(
            [
                pltpu.make_async_copy(dt_hbm.at[here, :], dt.at[here, :], load_sems.at[2 * h + 1]),
                pltpu.make_async_copy(attn_hbm.at[here, :], attn_ref.at[here, :], load_sems.at[2 * h + 2]),
            ]
        )
        for load in head_loads[h]:
            load.start()
    start = pack_ref[...]
    rows_load.wait()
    key_t[...] = transposed(rows[:, KEY])
    stores = []
    for first in range(0, HQ, PAIR):
        heads = range(first, first + PAIR)
        for head in heads:
            for load in head_loads[head]:
                load.wait()
        steps = [(head, tile) for head in heads for tile in range(TILES)]

        def products(step):
            head, tile = step
            width = (tile + 1) * TILE
            span = slice(tile * TILE, width)
            here = slice(head * HD, (head + 1) * HD)
            return dot(rows[:width, KEY], rows[span, here], NT), dot(rows[:width, VALUE], dt[here, span], NN)

        ahead = products(steps[0])
        for n, (head, tile) in enumerate(steps):
            scores, dprob = ahead
            if n + 1 < len(steps):
                ahead = products(steps[n + 1])
            here = slice(head * HD, (head + 1) * HD)
            width = (tile + 1) * TILE
            span = slice(tile * TILE, width)
            at = (head - first) * TOK
            spot = slice(at + tile * TILE, at + width)
            delta = jnp.sum(
                dt[here, span].astype(F32) * attn_ref[here, span].astype(F32), axis=0, keepdims=True
            )
            mask = keep_mask(tile, start)
            prob = jnp.exp2(jnp.where(mask, scores * EXP2_SCALE - stat_ref[head : head + 1, span], -jnp.inf))
            weight_t[:width, spot] = prob.astype(BF16)
            dscore = (prob * (dprob - delta)).astype(BF16)
            score_t[:width, spot] = dscore
            dq_t = dot(key_t[:, :width], dscore, NN) * SCALE
            dq[head, span, :] = dq_t.T.astype(BF16)
            if tile == TILES - 1:
                store = pltpu.make_async_copy(dq.at[head], dq_out.at[:, pl.ds(head * HD, HD)], dq_sems.at[head])
                store.start()
                stores.append(store)
        for tile in range(TILES):
            span = slice(tile * TILE, (tile + 1) * TILE)
            dk = jnp.zeros((TILE, HD), F32) if first == 0 else acc[span, :HD]
            dv = jnp.zeros((TILE, HD), F32) if first == 0 else acc[span, HD:]
            for head in range(first, first + PAIR):
                here = slice(head * HD, (head + 1) * HD)
                at = (head - first) * TOK
                spot = slice(at + tile * TILE, at + TOK)
                dk = dk + dot(score_t[span, spot], rows[tile * TILE :, here], NN)
                dv = dv + dot(weight_t[span, spot], dt[here, tile * TILE :], NT)
            if first + PAIR == HQ:
                kv_ref[span, :HD] = (dk * SCALE).astype(BF16)
                kv_ref[span, HD:] = dv.astype(BF16)
            else:
                acc[span, :HD] = dk
                acc[span, HD:] = dv
    for store in stores:
        store.wait()


def backward(rows, pack, d_attn_t, attn_t, stats, after):
    return pl.pallas_call(
        backward_kernel,
        out_shape=[shape((TOK, HQ * HD)), shape((TOK, 2 * HD)), TOKEN],
        in_specs=[ANY, VMEM, ANY, ANY, VMEM, ANY],
        out_specs=[ANY, VMEM, VMEM],
        scratch_shapes=[
            pltpu.VMEM((TOK, WIDTH), BF16),
            pltpu.VMEM((HQ * HD, TOK), BF16),
            pltpu.VMEM((HQ * HD, TOK), BF16),
            pltpu.VMEM((HD, TOK), BF16),
            pltpu.VMEM((TOK, PAIR * TOK), BF16),
            pltpu.VMEM((TOK, PAIR * TOK), BF16),
            pltpu.VMEM((TOK, 2 * HD), F32),
            pltpu.VMEM((HQ, TOK, HD), BF16),
            pltpu.SemaphoreType.DMA((HQ,)),
            pltpu.SemaphoreType.DMA((2 * HQ + 1,)),
        ],
        compiler_params=params(LARGE),
        name="backward",
        cost_estimate=cost(30 * 10**9, 8 * 2**20, HQ * 655360),
    )(rows, pack, d_attn_t, attn_t, stats, after)


def add_pair_kernel(x_ref, keep_ref, got_ref, *outs):
    *outs, token = outs
    token[...] = jnp.zeros(token.shape, F32)
    x = x_ref[0]
    for k, out in enumerate(outs):
        shard = lax.rem(x + k, N_FSDP)
        out[...] = (keep_ref[shard].astype(F32) + got_ref[shard].astype(F32)).astype(out.dtype)


def add_pair(x, keep, got):
    rows = keep.shape[0] // N_FSDP
    dims = (rows, HALF)
    return pl.pallas_call(
        add_pair_kernel,
        out_shape=[shape(dims, F32)] + [shape(dims)] * 3 + [TOKEN],
        in_specs=[SMEM, VMEM, VMEM],
        out_specs=[VMEM] * 5,
        compiler_params=params(4),
        name="add_pair",
        cost_estimate=cost(4 * rows * HALF, 10 * rows * HALF * 2),
    )(x, keep.reshape(N_FSDP, *dims), got.reshape(N_FSDP, *dims))


def sum4(parts):
    total = parts[0].astype(F32)
    for part in parts[1:]:
        total = total + part.astype(F32)
    return total


def split_z_kernel(z_ref, _, *refs):
    parts, outs, total = refs[:4], refs[4:8], refs[8]
    total[...] = sum4([r[...] for r in parts])
    size = SHARD // 4
    z = z_ref[0]
    for k, out in enumerate(outs):
        at = pl.multiple_of(lax.rem(z + k, 4) * size, size)
        out[...] = total[pl.ds(at, size), :].astype(out.dtype)


def split_z(z, after, parts):
    dims = (SHARD // 4, HALF)
    return pl.pallas_call(
        split_z_kernel,
        out_shape=[shape(dims, F32)] + [shape(dims)] * 3,
        in_specs=[SMEM, ANY] + [VMEM] * 4,
        out_specs=[VMEM] * 4,
        scratch_shapes=[pltpu.VMEM((SHARD, HALF), F32)],
        compiler_params=params(4),
        name="split_z",
        cost_estimate=cost(4 * SHARD * HALF, 10 * SHARD * HALF),
    )(z, after, *parts)


def sum4_kernel(factor, *refs):
    refs[4][...] = (sum4([r[...] for r in refs[:4]]) * factor).astype(BF16)


def sum_four(parts, factor=1.0):
    return pl.pallas_call(
        functools.partial(sum4_kernel, factor),
        out_shape=shape(parts[0].shape),
        in_specs=[VMEM] * 4,
        out_specs=VMEM,
        compiler_params=params(8),
        name="sum_four",
        cost_estimate=cost(4 * parts[0].size, 10 * parts[0].size),
    )(*parts)


def join_z_kernel(z_ref, *refs):
    parts, out = refs[:4], refs[4]
    size = SHARD // 4
    for k, ref in enumerate(parts):
        at = pl.multiple_of(lax.rem(z_ref[0] - k + 4, 4) * size, size)
        out[pl.ds(at, size), :] = ref[...]


def join_z(z, parts):
    return pl.pallas_call(
        join_z_kernel,
        out_shape=shape((SHARD, HALF)),
        in_specs=[SMEM] + [VMEM] * 4,
        out_specs=VMEM,
        compiler_params=params(4),
        name="join_z",
        cost_estimate=cost(0, 4 * SHARD * HALF),
    )(z, *parts)


def lay_out_kernel(core_ref, own, got, out):
    for part, side in ((own, core_ref[0]), (got, 1 - core_ref[0])):
        columns = pl.ds(pl.multiple_of(side * HALF, HALF), HALF)
        out[:, columns] = part[...].astype(F32)


def lay_out(core, own, got):
    return pl.pallas_call(
        lay_out_kernel,
        out_shape=shape((SHARD, D), F32),
        in_specs=[SMEM, VMEM, VMEM],
        out_specs=VMEM,
        compiler_params=params(4),
        name="lay_out",
        cost_estimate=cost(SHARD * D, 6 * SHARD * D),
    )(core, own, got)


def dp_shift(dy, dz, dc):
    pairs = []
    for i in range(32):
        y, z, c = i // 8, (i // 2) % 4, i % 2
        pairs.append((i, ((y + dy) % 4) * 8 + ((z + dz) % 4) * 2 + (c + dc) % 2))
    return pairs


def x_shift(k):
    return [(i, (i + k) % N_FSDP) for i in range(N_FSDP)]


def per_device(stash, stash_place, pack_start, d_out, out_weight):
    group = lax.axis_index("dp")
    x = lax.axis_index("fsdp")
    core = lax.rem(group, 2)
    z = lax.rem(group // 2, 4)
    held = stash.reshape(NB, BLK, WIDTH)
    peers = jnp.arange(NB, dtype=jnp.int32)
    holder = stash_place // NB
    slot = stash_place % NB
    chosen = jnp.sum(jnp.where((holder == group) & (peers[:, None] != group), slot, 0), axis=1)
    mine = lax.dynamic_index_in_dim(stash_place, group, 0, keepdims=False)
    source = jnp.where(mine // NB == group, mine % NB, NB + mine // NB)
    x1, z1, core1 = x.reshape(1), z.reshape(1), core.reshape(1)

    incoming = lax.all_to_all(held[chosen], "dp", split_axis=0, concat_axis=0, tiled=True)
    swap = dp_shift(0, 0, 1)
    half = lax.dynamic_slice_in_dim(out_weight, core * HALF, HALF, 1)
    weight_mine = [lax.ppermute(half, "fsdp", x_shift(k)) for k in (1, 2, 3)]
    weight_other = [lax.ppermute(part, "dp", swap) for part in weight_mine]
    d_attn_t = d_attn_transposed(jnp.stack([x, core]), out_weight, weight_mine, weight_other, d_out)

    pack = pack_start.reshape(1, TOK)
    rows, attn_t, stats, send = forward(core1, source, held, incoming, pack, d_out, d_attn_t)
    keep = keep_half(core1, attn_t, d_out)
    *parts, x_token = add_pair(x1, keep, lax.ppermute(send, "dp", swap))
    by_x = [parts[0]] + [lax.ppermute(parts[k], "fsdp", x_shift(k)) for k in (1, 2, 3)]
    grad_query, grad_keyval, token = backward(rows, pack, d_attn_t, attn_t, stats, x_token)
    by_z = split_z(z1, token, by_x)
    by_z = [by_z[0]] + [lax.ppermute(by_z[k], "dp", dp_shift(0, k, 0)) for k in (1, 2, 3)]
    z_sum = sum_four(by_z)
    by_y = [z_sum] + [lax.ppermute(z_sum, "dp", dp_shift(k, 0, 0)) for k in (1, 2, 3)]
    factor = (TOK * lax.axis_size("dp") * lax.axis_size("fsdp")) ** (-0.5)
    total = sum_four(by_y, factor)
    own = join_z(z1, [total] + [lax.ppermute(total, "dp", dp_shift(0, k, 0)) for k in (1, 2, 3)])
    grad_weight = lay_out(core1, own, lax.ppermute(own, "dp", swap))
    return (grad_query, grad_keyval, grad_weight)


def solution(mesh):
    in_specs = (
        P("dp", "fsdp", None, None, None),
        P(),
        P(("dp", "fsdp")),
        P(("dp", "fsdp"), None),
        P("fsdp", None),
    )
    out_specs = (P(("dp", "fsdp"), None), P(("dp", "fsdp"), None), P("fsdp", None))
    return jax.shard_map(
        per_device, mesh=mesh, in_specs=in_specs, out_specs=out_specs, check_vma=False
    )
```

time: 129 us -> 115 us (0.89)
  starting transfers between devices: 42.1 us -> 35 us
  Pallas kernels: 47.2 us -> 40.3 us
  waiting for transfers between devices: 29.6 us -> 27.3 us
  local copies, waits for them, and re-layouts: 6.77 us -> 8.32 us
    ppermute x8, waiting for transfers between devices: 24.4 us -> 15.7 us  [the longest x3 14.3 us: per_device(): weight_mine = [lax.ppermute(half, 'fsdp', x_shift(k)) for k in (1, 2, 3)]]
    pallas_call x1, Pallas kernels: 20.5 us -> 14.3 us  [forward(): pl.pallas_call(forward_kernel, out_shape=[shape((TOK, WIDTH)), shape((n,...]
    ppermute x3, waiting for transfers between devices: 0.01 us -> 4.54 us  [per_device(): lax.ppermute(total, 'dp', dp_shift(0, k, 0))]
    ppermute x8, starting transfers between devices: 14.2 us -> 10.5 us  [the longest x1 4.84 us: per_device(): grad_weight = lay_out(core1, own, lax.ppermute(own, 'dp', swap))]
    pallas_call x1, Pallas kernels: 17 us -> 14.5 us  [backward(): pl.pallas_call(backward_kernel, out_shape=[shape((TOK, HQ * HD)), shape((...]
    ppermute x3, waiting for transfers between devices: 2.47 us -> 4.38 us  [per_device(): lax.ppermute(z_sum, 'dp', dp_shift(k, 0, 0))]
    ppermute x3, starting transfers between devices: 5.29 us -> 3.5 us  [per_device(): lax.ppermute(by_z[k], 'dp', dp_shift(0, k, 0))]
    unnamed x14 -> x20, local copies, waits for them, and re-layouts: 3.15 us -> 4.67 us
  transfers between devices with their start and end apart: 21 -> 21, of which waited for: 7 -> 12; matrix products, arithmetic and copies ran while one was open for 1% -> 2% of each run, Pallas kernels for 19% -> 20%
where the time goes in v1:
time: 115 us
  Pallas kernels  40.3 us (35%)
  starting transfers between devices  35 us (30%)
  waiting for transfers between devices  27.3 us (24%)
  local copies, waits for them, and re-layouts  8.32 us (7%)
  other arithmetic  2.79 us (2%)
    pallas_call x1, Pallas kernels, backward(): pl.pallas_call(backward_kernel, out_shape=[shape((TOK, HQ * HD)), shape((...  14.5 us
    ppermute x3, waiting for transfers between devices, per_device(): weight_mine = [lax.ppermute(half, 'fsdp', x_shift(k)) for k in (1, 2, 3)]  14.3 us
    pallas_call x1, Pallas kernels, forward(): pl.pallas_call(forward_kernel, out_shape=[shape((TOK, WIDTH)), shape((n,...  14.3 us
    all_to_all x1, starting transfers between devices, per_device(): lax.all_to_all(held[chosen], 'dp', split_axis=0, concat_axis=0, tiled=True)  9.73 us
    pallas_call x1, Pallas kernels, d_attn_transposed(): pl.pallas_call(d_attn_kernel, out_shape=shape((HQ * HD, TOK)), in_specs=[...  7.07 us
    ppermute x1, starting transfers between devices, per_device(): grad_weight = lay_out(core1, own, lax.ppermute(own, 'dp', swap))  4.84 us
    unnamed x20, local copies, waits for them, and re-layouts  4.67 us
    ppermute x3, waiting for transfers between devices, per_device(): lax.ppermute(total, 'dp', dp_shift(0, k, 0))  4.54 us
  transfers between devices with their start and end apart: 21, of which 12 were waited for; matrix products, arithmetic and copies ran while one was open for 2% of the time, Pallas kernels for 20%

profile of v1, /device:TPU:1, one launch (start us, length us, event | category | flops | bytes accessed | tf_op | source)
XLA Modules:
  0.0 114.6 jit_solution(1959485175711406305)
XLA Ops:
  1.6 3.6 %gather_fusion = bf16[32,32,1024]{2,1,0:T(8,128)(2,1)} fusion(bf16[32,32,1024]{2,1,0:T(8,128)(2,1)} %bitcast.25, s32[1024]{0:T(1024)S(1)} %pad_clamp_fusion), kind=kCustom, calls=%fused_computation | custom fusion | bytes 4194432 | tf_op jit(solution)/shard_map/gather | solution.py:472
  5.2 9.7 %all-to-all-start = ((bf16[32,32,1024]{2,1,0:T(8,128)(2,1)}), bf16[32,32,1024]{2,1,0:T(8,128)(2,1)S(1)}, u32[]{:S(2)}, u32[]{:S(2)}) async-start(bf16[32,32,1024]{2,1,0:T(8,128)(2,1)} %gather_fusion), calls=%async_computation | async-start | bytes 4194304 | tf_op jit(solution)/shard_map/all_to_all | solution.py:472
  15.0 2.5 %collective-permute-start.2 = (bf16[192,768]{1,0:T(8,128)(2,1)S(1)}, bf16[192,768]{1,0:T(8,128)(2,1)S(1)}, u32[]{:S(2)}, u32[]{:S(2)}) collective-permute-start(bf16[192,768]{1,0:T(8,128)(2,1)S(1)} %constant_dynamic-slice_fusion), channel_id=1, source_target_pairs={{0,3},{1,0},{2,1},{3,2},{4,7},{5,4},{6,5},{7,6},{8,11},{9,8},{10,9... | collective-permute-start | bytes 884744 | tf_op jit(solution)/shard_map/ppermute | solution.py:475
  18.7 11.2 %collective-permute-done.2.refs_3_ = bf16[192,768]{1,0:T(8,128)(2,1)S(1)} collective-permute-done((bf16[192,768]{1,0:T(8,128)(2,1)S(1)}, bf16[192,768]{1,0:T(8,128)(2,1)S(1)}, u32[]{:S(2)}, u32[]{:S(2)}) %collective-permute-start.2) | collective-permute-done | bytes 294944 | tf_op jit(solution)/shard_map/ppermute | solution.py:475
  29.9 1.2 %collective-permute-start.5 = (bf16[192,768]{1,0:T(8,128)(2,1)S(1)}, bf16[192,768]{1,0:T(8,128)(2,1)S(1)}, u32[]{:S(2)}, u32[]{:S(2)}) collective-permute-start(bf16[192,768]{1,0:T(8,128)(2,1)S(1)} %collective-permute-done.2.refs_3_), channel_id=1, source_target_pairs={{0,4},{4,0},{8,12},{12,8},{16,20},{20,16},{24,28},{28,24},{32,36},... | collective-permute-start | bytes 884744 | tf_op jit(solution)/shard_map/ppermute | solution.py:476
  31.2 3.1 %collective-permute-done.refs_1_ = bf16[192,768]{1,0:T(8,128)(2,1)S(1)} collective-permute-done((bf16[192,768]{1,0:T(8,128)(2,1)S(1)}, bf16[192,768]{1,0:T(8,128)(2,1)S(1)}, u32[]{:S(2)}, u32[]{:S(2)}) %collective-permute-start) | collective-permute-done | bytes 294944 | tf_op jit(solution)/shard_map/ppermute | solution.py:475
  34.8 1.3 %compare_select_fusion.1.src_ref = s32[32]{0:T(128)} fusion(s32[32,32]{1,0:T(8,128)} %param.6, s32[]{:T(128)S(6)} %select_n.52, s32[]{:T(128)S(6)} %axis_index.23), kind=kLoop, calls=%fused_computation.14 | loop fusion | flops 704 | bytes 264 | tf_op jit(solution)/shard_map/jit(_where)/select_n | solution.py:469
  37.4 7.1 %d_attn.1._.dt_hbm = bf16[768,1024]{1,0:T(8,128)(2,1)} custom-call(s32[2]{0:T(128)} %pad_add_fusion.pos_ref, bf16[192,1536]{1,0:T(8,128)(2,1)} %refs_0_.1, bf16[192,768]{1,0:T(8,128)(2,1)} %copy-done.8, bf16[192,768]{1,0:T(8,128)(2,1)} %copy-done.7, bf16[192,768]{1,0:T(8,128)(2,1)} %copy-done.6, bf16[192,768]{1,0:T(8,128)(2,1)} %collective-permute-done.3.refs_4_, ...), custom_call_target="tpu_custom_call" | custom-call | flops 2415919104 | bytes 8388608 | tf_op jit(solution)/shard_map/d_attn/pallas_call | solution.py:82
  44.5 1.3 %copy-done.4 = bf16[32,32,1024]{2,1,0:T(8,128)(2,1)} copy-done((bf16[32,32,1024]{2,1,0:T(8,128)(2,1)}, bf16[32,32,1024]{2,1,0:T(8,128)(2,1)S(1)}, u32[]{:S(2)}) %copy-start.4) | copy-done | bytes 2097176
  45.8 14.3 %forward.1 = (bf16[1024,1024]{1,0:T(8,128)(2,1)}, bf16[768,1024]{1,0:T(8,128)(2,1)}, f32[8,1024]{1,0:T(8,128)}, bf16[768,768]{1,0:T(8,128)(2,1)}) custom-call(s32[1]{0:T(128)} %bitcast.core_ref, s32[32]{0:T(128)} %compare_select_fusion.1.src_ref, bf16[32,32,1024]{2,1,0:T(8,128)(2,1)} %bitcast.26, bf16[32,32,1024]{2,1,0:T(8,128)(2,1)} %copy-done.4, ...), custom_call_target="tpu_custom_call" | custom-call | flops 12000000000 | bytes 8388608 | tf_op jit(solution)/shard_map/forward/pallas_call | solution.py:187
  60.2 1.4 %copy-done.1 = bf16[768,1024]{1,0:T(8,128)(2,1)S(1)} copy-done((bf16[768,1024]{1,0:T(8,128)(2,1)S(1)}, bf16[768,1024]{1,0:T(8,128)(2,1)}, u32[]{:S(2)}) %copy-start.1) | copy-done | bytes 1572888
  61.7 1.5 %keep_half.1 = bf16[768,768]{1,0:T(8,128)(2,1)S(1)} custom-call(s32[1]{0:T(128)} %bitcast.core_ref, bf16[768,1024]{1,0:T(8,128)(2,1)S(1)} %copy-done.1, bf16[1024,1536]{1,0:T(8,128)(2,1)S(1)} %copy-done), custom_call_target="tpu_custom_call" | custom-call | flops 1207959552 | bytes 8388608 | tf_op jit(solution)/shard_map/keep_half/pallas_call | solution.py:219
  63.4 1.5 %add_pair.1 = (f32[192,768]{1,0:T(8,128)S(1)}, bf16[192,768]{1,0:T(8,128)(2,1)S(1)}, bf16[192,768]{1,0:T(8,128)(2,1)S(1)}, bf16[192,768]{1,0:T(8,128)(2,1)S(1)}, f32[8,128]{1,0:T(8,128)S(1)}) custom-call(s32[1]{0:T(128)} %bitcast.6.x_ref, bf16[4,192,768]{2,1,0:T(8,128)(2,1)S(1)} %bitcast.24, bf16[4,192,768]{2,1,0:T(8,128)(2,1)} %bitcast.8.got_ref), custom_call_target="tpu_custom_call" | custom-call | flops 589824 | bytes 2949120 | tf_op jit(solution)/shard_map/add_pair/pallas_call | solution.py:350
  66.1 2.4 %collective-permute-start.8 = (bf16[192,768]{1,0:T(8,128)(2,1)S(1)}, bf16[192,768]{1,0:T(8,128)(2,1)S(1)}, u32[]{:S(2)}, u32[]{:S(2)}) collective-permute-start(bf16[192,768]{1,0:T(8,128)(2,1)S(1)} %get-tuple-element.29), channel_id=1, source_target_pairs={{0,2},{1,3},{2,0},{3,1},{4,6},{5,7},{6,4},{7,5},{8,10},{9,11},{10,... | collective-permute-start | bytes 884744 | tf_op jit(solution)/shard_map/ppermute | solution.py:483
  69.7 14.5 %backward.1 = (bf16[1024,768]{1,0:T(8,128)(2,1)}, bf16[1024,256]{1,0:T(8,128)(2,1)}, f32[8,128]{1,0:T(8,128)}) custom-call(bf16[1024,1024]{1,0:T(8,128)(2,1)} %get-tuple-element.19.rows_hbm, s32[1,1024]{1,0:T(1,128)} %bitcast.28, bf16[768,1024]{1,0:T(8,128)(2,1)} %d_attn.1._.dt_hbm, bf16[768,1024]{1,0:T(8,128)(2,1)} %get-tuple-element.20.attn_ref.attn_hbm, ...), custom_call_target="tpu_custom_call" | custom-call | flops 30000001024 | bytes 8388608 | tf_op jit(solution)/shard_map/backward/pallas_call | solution.py:315
  85.2 2.2 %collective-permute-start.11 = (bf16[48,768]{1,0:T(8,128)(2,1)S(1)}, bf16[48,768]{1,0:T(8,128)(2,1)S(1)}, u32[]{:S(2)}, u32[]{:S(2)}) collective-permute-start(bf16[48,768]{1,0:T(8,128)(2,1)S(1)} %get-tuple-element.33), channel_id=1, source_target_pairs={{0,16},{4,20},{8,24},{12,28},{16,0},{20,4},{24,8},{28,12},{32,48},... | collective-permute-start | bytes 221192 | tf_op jit(solution)/shard_map/ppermute | solution.py:486
  88.7 1.8 %collective-permute-done.10.refs_1_ = bf16[48,768]{1,0:T(8,128)(2,1)S(1)} collective-permute-done((bf16[48,768]{1,0:T(8,128)(2,1)S(1)}, bf16[48,768]{1,0:T(8,128)(2,1)S(1)}, u32[]{:S(2)}, u32[]{:S(2)}) %collective-permute-start.10) | collective-permute-done | bytes 73760 | tf_op jit(solution)/shard_map/ppermute | solution.py:486
  91.3 2.9 %collective-permute-start.15 = (bf16[48,768]{1,0:T(8,128)(2,1)S(1)}, bf16[48,768]{1,0:T(8,128)(2,1)S(1)}, u32[]{:S(2)}, u32[]{:S(2)}) collective-permute-start(bf16[48,768]{1,0:T(8,128)(2,1)S(1)} %sum_four.2.refs_0_), channel_id=1, source_target_pairs={{0,96},{4,100},{8,104},{12,108},{16,112},{20,116},{24,120},{28,124... | collective-permute-start | bytes 221192 | tf_op jit(solution)/shard_map/ppermute | solution.py:488
  95.7 3.4 %collective-permute-done.14.refs_2_ = bf16[48,768]{1,0:T(8,128)(2,1)S(1)} collective-permute-done((bf16[48,768]{1,0:T(8,128)(2,1)S(1)}, bf16[48,768]{1,0:T(8,128)(2,1)S(1)}, u32[]{:S(2)}, u32[]{:S(2)}) %collective-permute-start.14) | collective-permute-done | bytes 73760 | tf_op jit(solution)/shard_map/ppermute | solution.py:488
  99.8 2.4 %collective-permute-start.18 = (bf16[48,768]{1,0:T(8,128)(2,1)S(1)}, bf16[48,768]{1,0:T(8,128)(2,1)S(1)}, u32[]{:S(2)}, u32[]{:S(2)}) collective-permute-start(bf16[48,768]{1,0:T(8,128)(2,1)S(1)} %sum_four.3.refs_0_), channel_id=1, source_target_pairs={{0,24},{4,28},{8,0},{12,4},{16,8},{20,12},{24,16},{28,20},{32,56},... | collective-permute-start | bytes 221192 | tf_op jit(solution)/shard_map/ppermute | solution.py:491
  102.9 1.4 %collective-permute-done.18.refs_3_ = bf16[48,768]{1,0:T(8,128)(2,1)S(1)} collective-permute-done((bf16[48,768]{1,0:T(8,128)(2,1)S(1)}, bf16[48,768]{1,0:T(8,128)(2,1)S(1)}, u32[]{:S(2)}, u32[]{:S(2)}) %collective-permute-start.18) | collective-permute-done | bytes 73760 | tf_op jit(solution)/shard_map/ppermute | solution.py:491
  104.3 2.7 %collective-permute-done.17.refs_2_ = bf16[48,768]{1,0:T(8,128)(2,1)S(1)} collective-permute-done((bf16[48,768]{1,0:T(8,128)(2,1)S(1)}, bf16[48,768]{1,0:T(8,128)(2,1)S(1)}, u32[]{:S(2)}, u32[]{:S(2)}) %collective-permute-start.17) | collective-permute-done | bytes 73760 | tf_op jit(solution)/shard_map/ppermute | solution.py:491
  107.4 4.8 %collective-permute-start.19 = (bf16[192,768]{1,0:T(8,128)(2,1)S(1)}, bf16[192,768]{1,0:T(8,128)(2,1)S(1)}, u32[]{:S(2)}, u32[]{:S(2)}) collective-permute-start(bf16[192,768]{1,0:T(8,128)(2,1)S(1)} %join_z.1.own), channel_id=1, source_target_pairs={{0,4},{4,0},{8,12},{12,8},{16,20},{20,16},{24,28},{28,24},{32,36},... | collective-permute-start | bytes 884744 | tf_op jit(solution)/shard_map/ppermute | solution.py:492
  112.3 1.2 %collective-permute-done.19.got = bf16[192,768]{1,0:T(8,128)(2,1)S(1)} collective-permute-done((bf16[192,768]{1,0:T(8,128)(2,1)S(1)}, bf16[192,768]{1,0:T(8,128)(2,1)S(1)}, u32[]{:S(2)}, u32[]{:S(2)}) %collective-permute-start.19) | collective-permute-done | bytes 294944 | tf_op jit(solution)/shard_map/ppermute | solution.py:492
  (56 shorter events, 14.0 us)
Async XLA Ops:
  5.2 9.8 %copy-start.5 = (bf16[192,1536]{1,0:T(8,128)(2,1)S(1)}, bf16[192,1536]{1,0:T(8,128)(2,1)}, u32[]{:S(2)}) copy-start(bf16[192,1536]{1,0:T(8,128)(2,1)} %refs_0_.1) | copy-start | bytes 1769476
  5.2 39.3 %all-to-all-start = ((bf16[32,32,1024]{2,1,0:T(8,128)(2,1)}), bf16[32,32,1024]{2,1,0:T(8,128)(2,1)S(1)}, u32[]{:S(2)}, u32[]{:S(2)}) async-start(bf16[32,32,1024]{2,1,0:T(8,128)(2,1)} %gather_fusion), calls=%async_computation | async-start | bytes 4194304 | tf_op jit(solution)/shard_map/all_to_all | solution.py:472
  15.0 14.9 %collective-permute-start.2 = (bf16[192,768]{1,0:T(8,128)(2,1)S(1)}, bf16[192,768]{1,0:T(8,128)(2,1)S(1)}, u32[]{:S(2)}, u32[]{:S(2)}) collective-permute-start(bf16[192,768]{1,0:T(8,128)(2,1)S(1)} %constant_dynamic-slice_fusion), channel_id=1, source_target_pairs={{0,3},{1,0},{2,1},{3,2},{4,7},{5,4},{6,5},{7,6},{8,11},{9,8},{10,9... | collective-permute-start | bytes 884744 | tf_op jit(solution)/shard_map/ppermute | solution.py:475
  17.5 13.6 %collective-permute-start.1 = (bf16[192,768]{1,0:T(8,128)(2,1)S(1)}, bf16[192,768]{1,0:T(8,128)(2,1)S(1)}, u32[]{:S(2)}, u32[]{:S(2)}) collective-permute-start(bf16[192,768]{1,0:T(8,128)(2,1)S(1)} %constant_dynamic-slice_fusion), channel_id=1, source_target_pairs={{0,2},{1,3},{2,0},{3,1},{4,6},{5,7},{6,4},{7,5},{8,10},{9,11},{10,... | collective-permute-start | bytes 884744 | tf_op jit(solution)/shard_map/ppermute | solution.py:475
  18.1 16.2 %collective-permute-start = (bf16[192,768]{1,0:T(8,128)(2,1)S(1)}, bf16[192,768]{1,0:T(8,128)(2,1)S(1)}, u32[]{:S(2)}, u32[]{:S(2)}) collective-permute-start(bf16[192,768]{1,0:T(8,128)(2,1)S(1)} %constant_dynamic-slice_fusion), channel_id=1, source_target_pairs={{0,1},{1,2},{2,3},{3,0},{4,5},{5,6},{6,7},{7,4},{8,9},{9,10},{10,1... | collective-permute-start | bytes 884744 | tf_op jit(solution)/shard_map/ppermute | solution.py:475
  29.9 6.8 %copy-start.6 = (bf16[192,768]{1,0:T(8,128)(2,1)}, bf16[192,768]{1,0:T(8,128)(2,1)S(1)}, u32[]{:S(2)}) copy-start(bf16[192,768]{1,0:T(8,128)(2,1)S(1)} %collective-permute-done.2.refs_3_) | copy-start | bytes 884740
  29.9 6.8 %collective-permute-start.5 = (bf16[192,768]{1,0:T(8,128)(2,1)S(1)}, bf16[192,768]{1,0:T(8,128)(2,1)S(1)}, u32[]{:S(2)}, u32[]{:S(2)}) collective-permute-start(bf16[192,768]{1,0:T(8,128)(2,1)S(1)} %collective-permute-done.2.refs_3_), channel_id=1, source_target_pairs={{0,4},{4,0},{8,12},{12,8},{16,20},{20,16},{24,28},{28,24},{32,36},... | collective-permute-start | bytes 884744 | tf_op jit(solution)/shard_map/ppermute | solution.py:476
  31.1 5.5 %collective-permute-start.4 = (bf16[192,768]{1,0:T(8,128)(2,1)S(1)}, bf16[192,768]{1,0:T(8,128)(2,1)}, u32[]{:S(2)}, u32[]{:S(2)}) collective-permute-start(bf16[192,768]{1,0:T(8,128)(2,1)S(1)} %collective-permute-done.1.refs_2_), channel_id=1, source_target_pairs={{0,4},{4,0},{8,12},{12,8},{16,20},{20,16},{24,28},{28,24},{32,36},... | collective-permute-start | bytes 884744 | tf_op jit(solution)/shard_map/ppermute | solution.py:476
  34.3 2.4 %collective-permute-start.3 = (bf16[192,768]{1,0:T(8,128)(2,1)S(1)}, bf16[192,768]{1,0:T(8,128)(2,1)}, u32[]{:S(2)}, u32[]{:S(2)}) collective-permute-start(bf16[192,768]{1,0:T(8,128)(2,1)S(1)} %collective-permute-done.refs_1_), channel_id=1, source_target_pairs={{0,4},{4,0},{8,12},{12,8},{16,20},{20,16},{24,28},{28,24},{32,36},... | collective-permute-start | bytes 884744 | tf_op jit(solution)/shard_map/ppermute | solution.py:476
  45.8 14.5 %copy-start = (bf16[1024,1536]{1,0:T(8,128)(2,1)S(1)}, bf16[1024,1536]{1,0:T(8,128)(2,1)}, u32[]{:S(2)}) copy-start(bf16[1024,1536]{1,0:T(8,128)(2,1)} %dout_hbm.3) | copy-start | bytes 9437188
  60.1 3.3 %collective-permute-start.6 = (bf16[768,768]{1,0:T(8,128)(2,1)}, bf16[768,768]{1,0:T(8,128)(2,1)}, u32[]{:S(2)}, u32[]{:S(2)}) collective-permute-start(bf16[768,768]{1,0:T(8,128)(2,1)} %get-tuple-element.22), channel_id=1, source_target_pairs={{0,4},{4,0},{8,12},{12,8},{16,20},{20,16},{24,28},{28,24},{32,36},... | collective-permute-start | bytes 3538952 | tf_op jit(solution)/shard_map/ppermute | solution.py:482
  65.5 18.7 %collective-permute-start.7 = (bf16[192,768]{1,0:T(8,128)(2,1)S(1)}, bf16[192,768]{1,0:T(8,128)(2,1)S(1)}, u32[]{:S(2)}, u32[]{:S(2)}) collective-permute-start(bf16[192,768]{1,0:T(8,128)(2,1)S(1)} %get-tuple-element.28), channel_id=1, source_target_pairs={{0,1},{1,2},{2,3},{3,0},{4,5},{5,6},{6,7},{7,4},{8,9},{9,10},{10,1... | collective-permute-start | bytes 884744 | tf_op jit(solution)/shard_map/ppermute | solution.py:483
  66.1 18.2 %collective-permute-start.8 = (bf16[192,768]{1,0:T(8,128)(2,1)S(1)}, bf16[192,768]{1,0:T(8,128)(2,1)S(1)}, u32[]{:S(2)}, u32[]{:S(2)}) collective-permute-start(bf16[192,768]{1,0:T(8,128)(2,1)S(1)} %get-tuple-element.29), channel_id=1, source_target_pairs={{0,2},{1,3},{2,0},{3,1},{4,6},{5,7},{6,4},{7,5},{8,10},{9,11},{10,... | collective-permute-start | bytes 884744 | tf_op jit(solution)/shard_map/ppermute | solution.py:483
  68.5 15.7 %collective-permute-start.9 = (bf16[192,768]{1,0:T(8,128)(2,1)S(1)}, bf16[192,768]{1,0:T(8,128)(2,1)S(1)}, u32[]{:S(2)}, u32[]{:S(2)}) collective-permute-start(bf16[192,768]{1,0:T(8,128)(2,1)S(1)} %get-tuple-element.30), channel_id=1, source_target_pairs={{0,3},{1,0},{2,1},{3,2},{4,7},{5,4},{6,5},{7,6},{8,11},{9,8},{10,9... | collective-permute-start | bytes 884744 | tf_op jit(solution)/shard_map/ppermute | solution.py:483
  85.2 5.3 %collective-permute-start.10 = (bf16[48,768]{1,0:T(8,128)(2,1)S(1)}, bf16[48,768]{1,0:T(8,128)(2,1)S(1)}, u32[]{:S(2)}, u32[]{:S(2)}) collective-permute-start(bf16[48,768]{1,0:T(8,128)(2,1)S(1)} %get-tuple-element.32), channel_id=1, source_target_pairs={{0,8},{4,12},{8,16},{12,20},{16,24},{20,28},{24,0},{28,4},{32,40},... | collective-permute-start | bytes 221192 | tf_op jit(solution)/shard_map/ppermute | solution.py:486
  85.2 5.2 %collective-permute-start.11 = (bf16[48,768]{1,0:T(8,128)(2,1)S(1)}, bf16[48,768]{1,0:T(8,128)(2,1)S(1)}, u32[]{:S(2)}, u32[]{:S(2)}) collective-permute-start(bf16[48,768]{1,0:T(8,128)(2,1)S(1)} %get-tuple-element.33), channel_id=1, source_target_pairs={{0,16},{4,20},{8,24},{12,28},{16,0},{20,4},{24,8},{28,12},{32,48},... | collective-permute-start | bytes 221192 | tf_op jit(solution)/shard_map/ppermute | solution.py:486
  87.5 3.8 %collective-permute-start.12 = (bf16[48,768]{1,0:T(8,128)(2,1)S(1)}, bf16[48,768]{1,0:T(8,128)(2,1)S(1)}, u32[]{:S(2)}, u32[]{:S(2)}) collective-permute-start(bf16[48,768]{1,0:T(8,128)(2,1)S(1)} %get-tuple-element.34), channel_id=1, source_target_pairs={{0,24},{4,28},{8,0},{12,4},{16,8},{20,12},{24,16},{28,20},{32,56},... | collective-permute-start | bytes 221192 | tf_op jit(solution)/shard_map/ppermute | solution.py:486
  91.3 4.4 %collective-permute-start.15 = (bf16[48,768]{1,0:T(8,128)(2,1)S(1)}, bf16[48,768]{1,0:T(8,128)(2,1)S(1)}, u32[]{:S(2)}, u32[]{:S(2)}) collective-permute-start(bf16[48,768]{1,0:T(8,128)(2,1)S(1)} %sum_four.2.refs_0_), channel_id=1, source_target_pairs={{0,96},{4,100},{8,104},{12,108},{16,112},{20,116},{24,120},{28,124... | collective-permute-start | bytes 221192 | tf_op jit(solution)/shard_map/ppermute | solution.py:488
  94.3 4.8 %collective-permute-start.14 = (bf16[48,768]{1,0:T(8,128)(2,1)S(1)}, bf16[48,768]{1,0:T(8,128)(2,1)S(1)}, u32[]{:S(2)}, u32[]{:S(2)}) collective-permute-start(bf16[48,768]{1,0:T(8,128)(2,1)S(1)} %sum_four.2.refs_0_), channel_id=1, source_target_pairs={{0,64},{4,68},{8,72},{12,76},{16,80},{20,84},{24,88},{28,92},{32,9... | collective-permute-start | bytes 221192 | tf_op jit(solution)/shard_map/ppermute | solution.py:488
  94.8 5.0 %collective-permute-start.13 = (bf16[48,768]{1,0:T(8,128)(2,1)S(1)}, bf16[48,768]{1,0:T(8,128)(2,1)S(1)}, u32[]{:S(2)}, u32[]{:S(2)}) collective-permute-start(bf16[48,768]{1,0:T(8,128)(2,1)S(1)} %sum_four.2.refs_0_), channel_id=1, source_target_pairs={{0,32},{4,36},{8,40},{12,44},{16,48},{20,52},{24,56},{28,60},{32,6... | collective-permute-start | bytes 221192 | tf_op jit(solution)/shard_map/ppermute | solution.py:488
  99.8 4.5 %collective-permute-start.18 = (bf16[48,768]{1,0:T(8,128)(2,1)S(1)}, bf16[48,768]{1,0:T(8,128)(2,1)S(1)}, u32[]{:S(2)}, u32[]{:S(2)}) collective-permute-start(bf16[48,768]{1,0:T(8,128)(2,1)S(1)} %sum_four.3.refs_0_), channel_id=1, source_target_pairs={{0,24},{4,28},{8,0},{12,4},{16,8},{20,12},{24,16},{28,20},{32,56},... | collective-permute-start | bytes 221192 | tf_op jit(solution)/shard_map/ppermute | solution.py:491
  102.2 4.8 %collective-permute-start.17 = (bf16[48,768]{1,0:T(8,128)(2,1)S(1)}, bf16[48,768]{1,0:T(8,128)(2,1)S(1)}, u32[]{:S(2)}, u32[]{:S(2)}) collective-permute-start(bf16[48,768]{1,0:T(8,128)(2,1)S(1)} %sum_four.3.refs_0_), channel_id=1, source_target_pairs={{0,16},{4,20},{8,24},{12,28},{16,0},{20,4},{24,8},{28,12},{32,48},... | collective-permute-start | bytes 221192 | tf_op jit(solution)/shard_map/ppermute | solution.py:491
  102.2 5.2 %collective-permute-start.16 = (bf16[48,768]{1,0:T(8,128)(2,1)S(1)}, bf16[48,768]{1,0:T(8,128)(2,1)S(1)}, u32[]{:S(2)}, u32[]{:S(2)}) collective-permute-start(bf16[48,768]{1,0:T(8,128)(2,1)S(1)} %sum_four.3.refs_0_), channel_id=1, source_target_pairs={{0,8},{4,12},{8,16},{12,20},{16,24},{20,28},{24,0},{28,4},{32,40},... | collective-permute-start | bytes 221192 | tf_op jit(solution)/shard_map/ppermute | solution.py:491
  107.4 6.0 %collective-permute-start.19 = (bf16[192,768]{1,0:T(8,128)(2,1)S(1)}, bf16[192,768]{1,0:T(8,128)(2,1)S(1)}, u32[]{:S(2)}, u32[]{:S(2)}) collective-permute-start(bf16[192,768]{1,0:T(8,128)(2,1)S(1)} %join_z.1.own), channel_id=1, source_target_pairs={{0,4},{4,0},{8,12},{12,8},{16,20},{20,16},{24,28},{28,24},{32,36},... | collective-permute-start | bytes 884744 | tf_op jit(solution)/shard_map/ppermute | solution.py:492
  (7 other events, 12.7 us)

commit v2 on v1

--- a/solution.py
+++ b/solution.py
@@ -56,7 +56,7 @@
 
 
 def d_attn_kernel(pos_ref, *refs):
-    own, mine, others, dout_hbm, out_ref, weight, dout, sems, dout_sem = (
+    own, mine, others, dout, out_ref, weight, sems = (
         refs[0], refs[1:4], refs[4:7], *refs[7:]
     )
     x, core = pos_ref[0], pos_ref[1]
@@ -69,12 +69,10 @@
         for i, (part, side) in enumerate(((mine[k - 1], core), (others[k - 1], 1 - core))):
             columns = pl.ds(pl.multiple_of(side * HALF, HALF), HALF)
             loads.append(pltpu.make_async_copy(part, weight.at[shard_rows(k), columns], sems.at[2 * k - 1 + i]))
-    block = pltpu.make_async_copy(dout_hbm, dout, dout_sem)
-    for load in loads + [block]:
+    for load in loads:
         load.start()
     for load in loads:
         load.wait()
-    block.wait()
     out_ref[...] = dot(weight[...], dout[...], NT).astype(BF16)
 
 
@@ -82,18 +80,16 @@
     return pl.pallas_call(
         d_attn_kernel,
         out_shape=shape((HQ * HD, TOK)),
-        in_specs=[SMEM] + [ANY] * 8,
+        in_specs=[SMEM] + [ANY] * 7 + [VMEM],
         out_specs=VMEM,
-        scratch_shapes=[
-            pltpu.VMEM((HQ * HD, D), BF16),
-            pltpu.VMEM((TOK, D), BF16),
-            pltpu.SemaphoreType.DMA((7,)),
-            pltpu.SemaphoreType.DMA,
-        ],
-        compiler_params=params(LARGE),
+        scratch_shapes=[pltpu.VMEM((HQ * HD, D), BF16), pltpu.SemaphoreType.DMA((7,))],
+        compiler_params=params(10),
         name="d_attn",
         cost_estimate=cost(2 * TOK * D * HQ * HD, 8 * 2**20),
     )(pos, own, *mine, *others, dout)
+
+
+TRIO = 3
 
 
 def keep_mask(tile, start):
@@ -155,24 +151,29 @@
         if tile == TILES - 1:
             rows_copy.start()
         value_t[:, span] = transposed(rows[span, VALUE])
-        mask = keep_mask(tile, start)
-
-        def raw_scores(head, width=width, span=span):
-            return dot(rows[:width, KEY], rows[span, head * HD : (head + 1) * HD], NT)
+        masks = jnp.concatenate([keep_mask(tile, start)] * TRIO, axis=1)
+
+        def raw_scores(first, width=width, span=span):
+            query = jnp.concatenate(
+                [rows[span, h * HD : (h + 1) * HD] for h in range(first, first + TRIO)], axis=0
+            )
+            return dot(rows[:width, KEY], query, NT)
 
         ahead = raw_scores(0)
-        for head in range(HQ):
-            here = slice(head * HD, (head + 1) * HD)
+        for first in range(0, HQ, TRIO):
             scores = ahead
-            if head + 1 < HQ:
-                ahead = raw_scores(head + 1)
-            scores = jnp.where(mask, scores, -jnp.inf)
+            if first + TRIO < HQ:
+                ahead = raw_scores(first + TRIO)
+            scores = jnp.where(masks, scores, -jnp.inf)
             top = jnp.max(scores, axis=0, keepdims=True)
             expo = jnp.exp2((scores - top) * EXP2_SCALE)
             total = jnp.sum(expo, axis=0, keepdims=True)
-            weights = (expo * (1.0 / total)).astype(BF16)
-            attn_ref[here, span] = dot(value_t[:, :width], weights, NN).astype(BF16)
-            stat_ref[head : head + 1, span] = top * EXP2_SCALE + jnp.log2(total)
+            attn = (dot(value_t[:, :width], expo.astype(BF16), NN) * (1.0 / total)).astype(BF16)
+            stat = top * EXP2_SCALE + jnp.log2(total)
+            for k in range(TRIO):
+                part = slice(k * TILE, (k + 1) * TILE)
+                attn_ref[(first + k) * HD : (first + k + 1) * HD, span] = attn[:, part]
+                stat_ref[first + k : first + k + 1, span] = stat[:, part]
     for copy in attn_copies:
         copy.start()
     dout_copy.wait()
@@ -232,32 +233,15 @@
 
 
 def backward_kernel(
-    rows_hbm, pack_ref, dt_hbm, attn_hbm, stat_ref, _, dq_out, kv_ref, token,
-    rows, dt, attn_ref, key_t, weight_t, score_t, acc, dq, dq_sems, load_sems,
+    rows, pack_ref, dt, attn_ref, stat_ref, _, dq_out, kv_ref, token,
+    key_t, weight_t, score_t, acc, dq, dq_sems,
 ):
     token[...] = jnp.zeros(token.shape, F32)
-    rows_load = pltpu.make_async_copy(rows_hbm, rows, load_sems.at[0])
-    rows_load.start()
-    head_loads = []
-    for h in range(HQ):
-        here = pl.ds(h * HD, HD)
-        head_loads.append(
-            [
-                pltpu.make_async_copy(dt_hbm.at[here, :], dt.at[here, :], load_sems.at[2 * h + 1]),
-                pltpu.make_async_copy(attn_hbm.at[here, :], attn_ref.at[here, :], load_sems.at[2 * h + 2]),
-            ]
-        )
-        for load in head_loads[h]:
-            load.start()
     start = pack_ref[...]
-    rows_load.wait()
     key_t[...] = transposed(rows[:, KEY])
     stores = []
     for first in range(0, HQ, PAIR):
         heads = range(first, first + PAIR)
-        for head in heads:
-            for load in head_loads[head]:
-                load.wait()
         steps = [(head, tile) for head in heads for tile in range(TILES)]
 
         def products(step):
@@ -315,28 +299,29 @@
     return pl.pallas_call(
         backward_kernel,
         out_shape=[shape((TOK, HQ * HD)), shape((TOK, 2 * HD)), TOKEN],
-        in_specs=[ANY, VMEM, ANY, ANY, VMEM, ANY],
+        in_specs=[VMEM] * 5 + [ANY],
         out_specs=[ANY, VMEM, VMEM],
         scratch_shapes=[
-            pltpu.VMEM((TOK, WIDTH), BF16),
-            pltpu.VMEM((HQ * HD, TOK), BF16),
-            pltpu.VMEM((HQ * HD, TOK), BF16),
             pltpu.VMEM((HD, TOK), BF16),
             pltpu.VMEM((TOK, PAIR * TOK), BF16),
             pltpu.VMEM((TOK, PAIR * TOK), BF16),
             pltpu.VMEM((TOK, 2 * HD), F32),
             pltpu.VMEM((HQ, TOK, HD), BF16),
             pltpu.SemaphoreType.DMA((HQ,)),
-            pltpu.SemaphoreType.DMA((2 * HQ + 1,)),
         ],
-        compiler_params=params(LARGE),
+        compiler_params=params(24),
         name="backward",
         cost_estimate=cost(30 * 10**9, 8 * 2**20, HQ * 655360),
     )(rows, pack, d_attn_t, attn_t, stats, after)
 
 
-def add_pair_kernel(x_ref, keep_ref, got_ref, *outs):
-    *outs, token = outs
+def add_pair_kernel(x_ref, keep_ref, got_hbm, *outs):
+    *outs, token, got_ref, sems = outs
+    loads = [pltpu.make_async_copy(got_hbm.at[k], got_ref.at[k], sems.at[k]) for k in range(N_FSDP)]
+    for load in loads:
+        load.start()
+    for load in loads:
+        load.wait()
     token[...] = jnp.zeros(token.shape, F32)
     x = x_ref[0]
     for k, out in enumerate(outs):
@@ -350,8 +335,9 @@
     return pl.pallas_call(
         add_pair_kernel,
         out_shape=[shape(dims, F32)] + [shape(dims)] * 3 + [TOKEN],
-        in_specs=[SMEM, VMEM, VMEM],
+        in_specs=[SMEM, VMEM, ANY],
         out_specs=[VMEM] * 5,
+        scratch_shapes=[pltpu.VMEM((N_FSDP, *dims), BF16), pltpu.SemaphoreType.DMA((N_FSDP,))],
         compiler_params=params(4),
         name="add_pair",
         cost_estimate=cost(4 * rows * HALF, 10 * rows * HALF * 2),
@@ -480,15 +466,16 @@
     rows, attn_t, stats, send = forward(core1, source, held, incoming, pack, d_out, d_attn_t)
     keep = keep_half(core1, attn_t, d_out)
     *parts, x_token = add_pair(x1, keep, lax.ppermute(send, "dp", swap))
-    by_x = [parts[0]] + [lax.ppermute(parts[k], "fsdp", x_shift(k)) for k in (1, 2, 3)]
+    by_x = [parts[0]] + [lax.ppermute(parts[k], "fsdp", x_shift(k)) for k in (2, 1, 3)]
     grad_query, grad_keyval, token = backward(rows, pack, d_attn_t, attn_t, stats, x_token)
     by_z = split_z(z1, token, by_x)
-    by_z = [by_z[0]] + [lax.ppermute(by_z[k], "dp", dp_shift(0, k, 0)) for k in (1, 2, 3)]
+    by_z = [by_z[0]] + [lax.ppermute(by_z[k], "dp", dp_shift(0, k, 0)) for k in (2, 1, 3)]
     z_sum = sum_four(by_z)
-    by_y = [z_sum] + [lax.ppermute(z_sum, "dp", dp_shift(k, 0, 0)) for k in (1, 2, 3)]
+    by_y = [z_sum] + [lax.ppermute(z_sum, "dp", dp_shift(k, 0, 0)) for k in (1, 3, 2)]
     factor = (TOK * lax.axis_size("dp") * lax.axis_size("fsdp")) ** (-0.5)
     total = sum_four(by_y, factor)
-    own = join_z(z1, [total] + [lax.ppermute(total, "dp", dp_shift(0, k, 0)) for k in (1, 2, 3)])
+    by_z = {k: lax.ppermute(total, "dp", dp_shift(0, k, 0)) for k in (1, 3, 2)}
+    own = join_z(z1, [total] + [by_z[k] for k in (1, 2, 3)])
     grad_weight = lay_out(core1, own, lax.ppermute(own, "dp", swap))
     return (grad_query, grad_keyval, grad_weight)
 

time: 115 us -> 111 us (0.965)
  Pallas kernels: 40.3 us -> 33.3 us
  starting transfers between devices: 35 us -> 39.1 us
    pallas_call x1, Pallas kernels: 14.5 us -> 11.9 us  [backward(): pl.pallas_call(backward_kernel, out_shape=[shape((TOK, HQ * HD)), shape((...]
    pallas_call x1, Pallas kernels: 7.07 us -> 4.69 us  [d_attn_transposed(): pl.pallas_call(d_attn_kernel, out_shape=shape((HQ * HD, TOK)), in_specs=[...]
    pallas_call x1, Pallas kernels: 14.3 us -> 12.1 us  [forward(): pl.pallas_call(forward_kernel, out_shape=[shape((TOK, WIDTH)), shape((n,...]
    ppermute x3, starting transfers between devices: 3.5 us -> 5.52 us  [per_device(): lax.ppermute(by_z[k], 'dp', dp_shift(0, k, 0))]
  transfers between devices with their start and end apart: 21 -> 21, of which waited for: 12 -> 11; matrix products, arithmetic and copies ran while one was open for 2% -> 2% of each run, Pallas kernels for 20% -> 16%
where the time goes in v2:
time: 111 us; the launch traced here: 110 us
  starting transfers between devices  39.1 us (35%)
  Pallas kernels  33.3 us (30%)
  waiting for transfers between devices  26.5 us (24%)
  local copies, waits for them, and re-layouts  8.22 us (7%)
  other arithmetic  2.2 us (2%)
    ppermute x3, waiting for transfers between devices, per_device(): weight_mine = [lax.ppermute(half, 'fsdp', x_shift(k)) for k in (1, 2, 3)]  14.4 us
    pallas_call x1, Pallas kernels, forward(): pl.pallas_call(forward_kernel, out_shape=[shape((TOK, WIDTH)), shape((n,...  12.1 us
    pallas_call x1, Pallas kernels, backward(): pl.pallas_call(backward_kernel, out_shape=[shape((TOK, HQ * HD)), shape((...  11.9 us
    all_to_all x1, starting transfers between devices, per_device(): lax.all_to_all(held[chosen], 'dp', split_axis=0, concat_axis=0, tiled=True)  9.92 us
    ppermute x3, starting transfers between devices, per_device(): lax.ppermute(by_z[k], 'dp', dp_shift(0, k, 0))  5.52 us
    ppermute x1, starting transfers between devices, per_device(): grad_weight = lay_out(core1, own, lax.ppermute(own, 'dp', swap))  5.06 us
    ppermute x3, starting transfers between devices, per_device(): lax.ppermute(parts[k], 'fsdp', x_shift(k))  4.97 us
    ppermute x3, waiting for transfers between devices, per_device(): by_z = {k: lax.ppermute(total, 'dp', dp_shift(0, k, 0)) for k in (1, 3, 2)}  4.73 us
  transfers between devices with their start and end apart: 21, of which 11 were waited for; matrix products, arithmetic and copies ran while one was open for 2% of the time, Pallas kernels for 16%

profile of v2, /device:TPU:1, one launch (start us, length us, event | category | flops | bytes accessed | tf_op | source)
XLA Modules:
  0.0 110.1 jit_solution(18354640412199655815)
XLA Ops:
  1.6 3.6 %gather_fusion = bf16[32,32,1024]{2,1,0:T(8,128)(2,1)} fusion(bf16[32,32,1024]{2,1,0:T(8,128)(2,1)} %bitcast.27, s32[1024]{0:T(1024)S(1)} %pad_clamp_fusion), kind=kCustom, calls=%fused_computation | custom fusion | bytes 4194432 | tf_op jit(solution)/shard_map/gather | solution.py:458
  5.2 9.9 %all-to-all-start = ((bf16[32,32,1024]{2,1,0:T(8,128)(2,1)}), bf16[32,32,1024]{2,1,0:T(8,128)(2,1)}, u32[]{:S(2)}, u32[]{:S(2)}) async-start(bf16[32,32,1024]{2,1,0:T(8,128)(2,1)} %gather_fusion), calls=%async_computation | async-start | bytes 4194304 | tf_op jit(solution)/shard_map/all_to_all | solution.py:458
  16.1 2.5 %collective-permute-start.2 = (bf16[192,768]{1,0:T(8,128)(2,1)S(1)}, bf16[192,768]{1,0:T(8,128)(2,1)S(1)}, u32[]{:S(2)}, u32[]{:S(2)}) collective-permute-start(bf16[192,768]{1,0:T(8,128)(2,1)S(1)} %constant_dynamic-slice_fusion), channel_id=1, source_target_pairs={{0,3},{1,0},{2,1},{3,2},{4,7},{5,4},{6,5},{7,6},{8,11},{9,8},{10,9... | collective-permute-start | bytes 884744 | tf_op jit(solution)/shard_map/ppermute | solution.py:461
  19.8 11.1 %collective-permute-done.2.refs_3_ = bf16[192,768]{1,0:T(8,128)(2,1)S(1)} collective-permute-done((bf16[192,768]{1,0:T(8,128)(2,1)S(1)}, bf16[192,768]{1,0:T(8,128)(2,1)S(1)}, u32[]{:S(2)}, u32[]{:S(2)}) %collective-permute-start.2) | collective-permute-done | bytes 294944 | tf_op jit(solution)/shard_map/ppermute | solution.py:461
  30.9 1.3 %collective-permute-start.5 = (bf16[192,768]{1,0:T(8,128)(2,1)S(1)}, bf16[192,768]{1,0:T(8,128)(2,1)}, u32[]{:S(2)}, u32[]{:S(2)}) collective-permute-start(bf16[192,768]{1,0:T(8,128)(2,1)S(1)} %collective-permute-done.2.refs_3_), channel_id=1, source_target_pairs={{0,4},{4,0},{8,12},{12,8},{16,20},{20,16},{24,28},{28,24},{32,36},... | collective-permute-start | bytes 884744 | tf_op jit(solution)/shard_map/ppermute | solution.py:462
  32.2 3.3 %collective-permute-done.refs_1_ = bf16[192,768]{1,0:T(8,128)(2,1)} collective-permute-done((bf16[192,768]{1,0:T(8,128)(2,1)S(1)}, bf16[192,768]{1,0:T(8,128)(2,1)}, u32[]{:S(2)}, u32[]{:S(2)}) %collective-permute-start) | collective-permute-done | bytes 294944 | tf_op jit(solution)/shard_map/ppermute | solution.py:461
  38.6 4.7 %d_attn.1._.dt = bf16[768,1024]{1,0:T(8,128)(2,1)S(1)} custom-call(s32[2]{0:T(128)S(1)} %pad_add_fusion.pos_ref, bf16[192,1536]{1,0:T(8,128)(2,1)S(1)} %copy-done.4, bf16[192,768]{1,0:T(8,128)(2,1)} %collective-permute-done.refs_1_, bf16[192,768]{1,0:T(8,128)(2,1)} %collective-permute-done.1.refs_2_, bf16[192,768]{1,0:T(8,128)(2,1)S(1)} %collective-permute-done.2.refs_3_, ...), custom_call_target="tpu_custom_call" | custom-call | flops 2415919104 | bytes 8388608 | tf_op jit(solution)/shard_map/d_attn/pallas_call | solution.py:80
  44.5 12.1 %forward.1 = (bf16[1024,1024]{1,0:T(8,128)(2,1)}, bf16[768,1024]{1,0:T(8,128)(2,1)}, f32[8,1024]{1,0:T(8,128)}, bf16[768,768]{1,0:T(8,128)(2,1)}) custom-call(s32[1]{0:T(128)} %bitcast.core_ref, s32[32]{0:T(128)} %compare_select_fusion.1.src_ref, bf16[32,32,1024]{2,1,0:T(8,128)(2,1)} %bitcast.28, bf16[32,32,1024]{2,1,0:T(8,128)(2,1)} %all-to-all-done.inc_ref, ...), custom_call_target="tpu_custom_call" | custom-call | flops 12000000000 | bytes 8388608 | tf_op jit(solution)/shard_map/forward/pallas_call | solution.py:188
  57.2 1.4 %copy-done.2 = bf16[768,1024]{1,0:T(8,128)(2,1)S(1)} copy-done((bf16[768,1024]{1,0:T(8,128)(2,1)S(1)}, bf16[768,1024]{1,0:T(8,128)(2,1)}, u32[]{:S(2)}) %copy-start.2) | copy-done | bytes 1572888
  58.6 1.5 %keep_half.1 = bf16[768,768]{1,0:T(8,128)(2,1)S(1)} custom-call(s32[1]{0:T(128)} %bitcast.core_ref, bf16[768,1024]{1,0:T(8,128)(2,1)S(1)} %copy-done.2, bf16[1024,1536]{1,0:T(8,128)(2,1)S(1)} %copy-done.1), custom_call_target="tpu_custom_call" | custom-call | flops 1207959552 | bytes 8388608 | tf_op jit(solution)/shard_map/keep_half/pallas_call | solution.py:220
  60.1 1.6 %add_pair.1 = (f32[192,768]{1,0:T(8,128)S(1)}, bf16[192,768]{1,0:T(8,128)(2,1)S(1)}, bf16[192,768]{1,0:T(8,128)(2,1)S(1)}, bf16[192,768]{1,0:T(8,128)(2,1)S(1)}, f32[8,128]{1,0:T(8,128)S(1)}) custom-call(s32[1]{0:T(128)} %bitcast.6.x_ref, bf16[4,192,768]{2,1,0:T(8,128)(2,1)S(1)} %bitcast.24, bf16[4,192,768]{2,1,0:T(8,128)(2,1)} %bitcast.8.got_hbm), custom_call_target="tpu_custom_call" | custom-call | flops 589824 | bytes 2949120 | tf_op jit(solution)/shard_map/add_pair/pallas_call | solution.py:335
  61.8 2.3 %collective-permute-start.7 = (bf16[192,768]{1,0:T(8,128)(2,1)S(1)}, bf16[192,768]{1,0:T(8,128)(2,1)S(1)}, u32[]{:S(2)}, u32[]{:S(2)}) collective-permute-start(bf16[192,768]{1,0:T(8,128)(2,1)S(1)} %get-tuple-element.28), channel_id=1, source_target_pairs={{0,2},{1,3},{2,0},{3,1},{4,6},{5,7},{6,4},{7,5},{8,10},{9,11},{10,... | collective-permute-start | bytes 884744 | tf_op jit(solution)/shard_map/ppermute | solution.py:469
  64.4 2.4 %collective-permute-start.9 = (bf16[192,768]{1,0:T(8,128)(2,1)S(1)}, bf16[192,768]{1,0:T(8,128)(2,1)S(1)}, u32[]{:S(2)}, u32[]{:S(2)}) collective-permute-start(bf16[192,768]{1,0:T(8,128)(2,1)S(1)} %get-tuple-element.30), channel_id=1, source_target_pairs={{0,3},{1,0},{2,1},{3,2},{4,7},{5,4},{6,5},{7,6},{8,11},{9,8},{10,9... | collective-permute-start | bytes 884744 | tf_op jit(solution)/shard_map/ppermute | solution.py:469
  66.8 11.9 %backward.1 = (bf16[1024,768]{1,0:T(8,128)(2,1)}, bf16[1024,256]{1,0:T(8,128)(2,1)}, f32[8,128]{1,0:T(8,128)S(1)}) custom-call(bf16[1024,1024]{1,0:T(8,128)(2,1)S(1)} %copy-done.8, s32[1,1024]{1,0:T(1,128)S(1)} %bitcast.26, bf16[768,1024]{1,0:T(8,128)(2,1)S(1)} %copy-done.7, bf16[768,1024]{1,0:T(8,128)(2,1)S(1)} %copy-done.3, f32[8,1024]{1,0:T(8,128)S(1)} %copy-done.9, ...), custom_call_target="tpu_custom_call" | custom-call | flops 30000001024 | bytes 8388608 | tf_op jit(solution)/shard_map/backward/pallas_call | solution.py:299
  79.0 2.8 %collective-permute-start.10 = (bf16[48,768]{1,0:T(8,128)(2,1)S(1)}, bf16[48,768]{1,0:T(8,128)(2,1)S(1)}, u32[]{:S(2)}, u32[]{:S(2)}) collective-permute-start(bf16[48,768]{1,0:T(8,128)(2,1)S(1)} %get-tuple-element.32), channel_id=1, source_target_pairs={{0,16},{4,20},{8,24},{12,28},{16,0},{20,4},{24,8},{28,12},{32,48},... | collective-permute-start | bytes 221192 | tf_op jit(solution)/shard_map/ppermute | solution.py:472
  82.1 2.4 %collective-permute-start.12 = (bf16[48,768]{1,0:T(8,128)(2,1)S(1)}, bf16[48,768]{1,0:T(8,128)(2,1)S(1)}, u32[]{:S(2)}, u32[]{:S(2)}) collective-permute-start(bf16[48,768]{1,0:T(8,128)(2,1)S(1)} %get-tuple-element.34), channel_id=1, source_target_pairs={{0,24},{4,28},{8,0},{12,4},{16,8},{20,12},{24,16},{28,20},{32,56},... | collective-permute-start | bytes 221192 | tf_op jit(solution)/shard_map/ppermute | solution.py:472
  84.5 1.9 %collective-permute-done.11.refs_2_ = bf16[48,768]{1,0:T(8,128)(2,1)S(1)} collective-permute-done((bf16[48,768]{1,0:T(8,128)(2,1)S(1)}, bf16[48,768]{1,0:T(8,128)(2,1)S(1)}, u32[]{:S(2)}, u32[]{:S(2)}) %collective-permute-start.11) | collective-permute-done | bytes 73760 | tf_op jit(solution)/shard_map/ppermute | solution.py:472
  86.5 2.6 %collective-permute-start.15 = (bf16[48,768]{1,0:T(8,128)(2,1)S(1)}, bf16[48,768]{1,0:T(8,128)(2,1)S(1)}, u32[]{:S(2)}, u32[]{:S(2)}) collective-permute-start(bf16[48,768]{1,0:T(8,128)(2,1)S(1)} %sum_four.2.refs_0_), channel_id=1, source_target_pairs={{0,64},{4,68},{8,72},{12,76},{16,80},{20,84},{24,88},{28,92},{32,9... | collective-permute-start | bytes 221192 | tf_op jit(solution)/shard_map/ppermute | solution.py:474
  92.3 2.2 %collective-permute-done.13.refs_1_ = bf16[48,768]{1,0:T(8,128)(2,1)S(1)} collective-permute-done((bf16[48,768]{1,0:T(8,128)(2,1)S(1)}, bf16[48,768]{1,0:T(8,128)(2,1)S(1)}, u32[]{:S(2)}, u32[]{:S(2)}) %collective-permute-start.13) | collective-permute-done | bytes 73760 | tf_op jit(solution)/shard_map/ppermute | solution.py:474
  94.6 2.7 %collective-permute-start.18 = (bf16[48,768]{1,0:T(8,128)(2,1)S(1)}, bf16[48,768]{1,0:T(8,128)(2,1)S(1)}, u32[]{:S(2)}, u32[]{:S(2)}) collective-permute-start(bf16[48,768]{1,0:T(8,128)(2,1)S(1)} %sum_four.3.refs_0_), channel_id=1, source_target_pairs={{0,24},{4,28},{8,0},{12,4},{16,8},{20,12},{24,16},{28,20},{32,56},... | collective-permute-start | bytes 221192 | tf_op jit(solution)/shard_map/ppermute | solution.py:477
  98.0 1.4 %collective-permute-done.18.refs_3_ = bf16[48,768]{1,0:T(8,128)(2,1)S(1)} collective-permute-done((bf16[48,768]{1,0:T(8,128)(2,1)S(1)}, bf16[48,768]{1,0:T(8,128)(2,1)S(1)}, u32[]{:S(2)}, u32[]{:S(2)}) %collective-permute-start.18) | collective-permute-done | bytes 73760 | tf_op jit(solution)/shard_map/ppermute | solution.py:477
  99.4 2.7 %collective-permute-done.17.refs_2_ = bf16[48,768]{1,0:T(8,128)(2,1)S(1)} collective-permute-done((bf16[48,768]{1,0:T(8,128)(2,1)S(1)}, bf16[48,768]{1,0:T(8,128)(2,1)S(1)}, u32[]{:S(2)}, u32[]{:S(2)}) %collective-permute-start.17) | collective-permute-done | bytes 73760 | tf_op jit(solution)/shard_map/ppermute | solution.py:477
  102.8 5.1 %collective-permute-start.19 = (bf16[192,768]{1,0:T(8,128)(2,1)S(1)}, bf16[192,768]{1,0:T(8,128)(2,1)S(1)}, u32[]{:S(2)}, u32[]{:S(2)}) collective-permute-start(bf16[192,768]{1,0:T(8,128)(2,1)S(1)} %join_z.1.own), channel_id=1, source_target_pairs={{0,4},{4,0},{8,12},{12,8},{16,20},{20,16},{24,28},{28,24},{32,36},... | collective-permute-start | bytes 884744 | tf_op jit(solution)/shard_map/ppermute | solution.py:479
  107.8 1.2 %collective-permute-done.19.got = bf16[192,768]{1,0:T(8,128)(2,1)S(1)} collective-permute-done((bf16[192,768]{1,0:T(8,128)(2,1)S(1)}, bf16[192,768]{1,0:T(8,128)(2,1)S(1)}, u32[]{:S(2)}, u32[]{:S(2)}) %collective-permute-start.19) | collective-permute-done | bytes 294944 | tf_op jit(solution)/shard_map/ppermute | solution.py:479
  (56 shorter events, 14.4 us)
Async XLA Ops:
  5.2 32.4 %copy-start = (bf16[1024,1536]{1,0:T(8,128)(2,1)S(1)}, bf16[1024,1536]{1,0:T(8,128)(2,1)}, u32[]{:S(2)}) copy-start(bf16[1024,1536]{1,0:T(8,128)(2,1)} %dout_hbm.3) | copy-start | bytes 9437188
  5.2 39.3 %all-to-all-start = ((bf16[32,32,1024]{2,1,0:T(8,128)(2,1)}), bf16[32,32,1024]{2,1,0:T(8,128)(2,1)}, u32[]{:S(2)}, u32[]{:S(2)}) async-start(bf16[32,32,1024]{2,1,0:T(8,128)(2,1)} %gather_fusion), calls=%async_computation | async-start | bytes 4194304 | tf_op jit(solution)/shard_map/all_to_all | solution.py:458
  16.1 14.8 %collective-permute-start.2 = (bf16[192,768]{1,0:T(8,128)(2,1)S(1)}, bf16[192,768]{1,0:T(8,128)(2,1)S(1)}, u32[]{:S(2)}, u32[]{:S(2)}) collective-permute-start(bf16[192,768]{1,0:T(8,128)(2,1)S(1)} %constant_dynamic-slice_fusion), channel_id=1, source_target_pairs={{0,3},{1,0},{2,1},{3,2},{4,7},{5,4},{6,5},{7,6},{8,11},{9,8},{10,9... | collective-permute-start | bytes 884744 | tf_op jit(solution)/shard_map/ppermute | solution.py:461
  18.6 13.6 %collective-permute-start.1 = (bf16[192,768]{1,0:T(8,128)(2,1)S(1)}, bf16[192,768]{1,0:T(8,128)(2,1)}, u32[]{:S(2)}, u32[]{:S(2)}) collective-permute-start(bf16[192,768]{1,0:T(8,128)(2,1)S(1)} %constant_dynamic-slice_fusion), channel_id=1, source_target_pairs={{0,2},{1,3},{2,0},{3,1},{4,6},{5,7},{6,4},{7,5},{8,10},{9,11},{10,... | collective-permute-start | bytes 884744 | tf_op jit(solution)/shard_map/ppermute | solution.py:461
  19.2 16.3 %collective-permute-start = (bf16[192,768]{1,0:T(8,128)(2,1)S(1)}, bf16[192,768]{1,0:T(8,128)(2,1)}, u32[]{:S(2)}, u32[]{:S(2)}) collective-permute-start(bf16[192,768]{1,0:T(8,128)(2,1)S(1)} %constant_dynamic-slice_fusion), channel_id=1, source_target_pairs={{0,1},{1,2},{2,3},{3,0},{4,5},{5,6},{6,7},{7,4},{8,9},{9,10},{10,1... | collective-permute-start | bytes 884744 | tf_op jit(solution)/shard_map/ppermute | solution.py:461
  30.9 6.4 %collective-permute-start.5 = (bf16[192,768]{1,0:T(8,128)(2,1)S(1)}, bf16[192,768]{1,0:T(8,128)(2,1)}, u32[]{:S(2)}, u32[]{:S(2)}) collective-permute-start(bf16[192,768]{1,0:T(8,128)(2,1)S(1)} %collective-permute-done.2.refs_3_), channel_id=1, source_target_pairs={{0,4},{4,0},{8,12},{12,8},{16,20},{20,16},{24,28},{28,24},{32,36},... | collective-permute-start | bytes 884744 | tf_op jit(solution)/shard_map/ppermute | solution.py:462
  32.2 5.1 %collective-permute-start.4 = (bf16[192,768]{1,0:T(8,128)(2,1)}, bf16[192,768]{1,0:T(8,128)(2,1)}, u32[]{:S(2)}, u32[]{:S(2)}) collective-permute-start(bf16[192,768]{1,0:T(8,128)(2,1)} %collective-permute-done.1.refs_2_), channel_id=1, source_target_pairs={{0,4},{4,0},{8,12},{12,8},{16,20},{20,16},{24,28},{28,24},{32,36},... | collective-permute-start | bytes 884744 | tf_op jit(solution)/shard_map/ppermute | solution.py:462
  35.5 2.0 %collective-permute-start.3 = (bf16[192,768]{1,0:T(8,128)(2,1)}, bf16[192,768]{1,0:T(8,128)(2,1)}, u32[]{:S(2)}, u32[]{:S(2)}) collective-permute-start(bf16[192,768]{1,0:T(8,128)(2,1)} %collective-permute-done.refs_1_), channel_id=1, source_target_pairs={{0,4},{4,0},{8,12},{12,8},{16,20},{20,16},{24,28},{28,24},{32,36},... | collective-permute-start | bytes 884744 | tf_op jit(solution)/shard_map/ppermute | solution.py:462
  44.5 12.7 %copy-start.1 = (bf16[1024,1536]{1,0:T(8,128)(2,1)S(1)}, bf16[1024,1536]{1,0:T(8,128)(2,1)}, u32[]{:S(2)}) copy-start(bf16[1024,1536]{1,0:T(8,128)(2,1)} %dout_hbm.3) | copy-start | bytes 9437188
  56.5 3.6 %collective-permute-start.6 = (bf16[768,768]{1,0:T(8,128)(2,1)}, bf16[768,768]{1,0:T(8,128)(2,1)}, u32[]{:S(2)}, u32[]{:S(2)}) collective-permute-start(bf16[768,768]{1,0:T(8,128)(2,1)} %get-tuple-element.22), channel_id=1, source_target_pairs={{0,4},{4,0},{8,12},{12,8},{16,20},{20,16},{24,28},{28,24},{32,36},... | collective-permute-start | bytes 3538952 | tf_op jit(solution)/shard_map/ppermute | solution.py:468
  58.6 8.2 %copy-start.8 = (bf16[1024,1024]{1,0:T(8,128)(2,1)S(1)}, bf16[1024,1024]{1,0:T(8,128)(2,1)}, u32[]{:S(2)}) copy-start(bf16[1024,1024]{1,0:T(8,128)(2,1)} %get-tuple-element.19.rows) | copy-start | bytes 6291460
  61.8 16.9 %collective-permute-start.7 = (bf16[192,768]{1,0:T(8,128)(2,1)S(1)}, bf16[192,768]{1,0:T(8,128)(2,1)S(1)}, u32[]{:S(2)}, u32[]{:S(2)}) collective-permute-start(bf16[192,768]{1,0:T(8,128)(2,1)S(1)} %get-tuple-element.28), channel_id=1, source_target_pairs={{0,2},{1,3},{2,0},{3,1},{4,6},{5,7},{6,4},{7,5},{8,10},{9,11},{10,... | collective-permute-start | bytes 884744 | tf_op jit(solution)/shard_map/ppermute | solution.py:469
  64.1 14.7 %collective-permute-start.8 = (bf16[192,768]{1,0:T(8,128)(2,1)S(1)}, bf16[192,768]{1,0:T(8,128)(2,1)S(1)}, u32[]{:S(2)}, u32[]{:S(2)}) collective-permute-start(bf16[192,768]{1,0:T(8,128)(2,1)S(1)} %get-tuple-element.29), channel_id=1, source_target_pairs={{0,1},{1,2},{2,3},{3,0},{4,5},{5,6},{6,7},{7,4},{8,9},{9,10},{10,1... | collective-permute-start | bytes 884744 | tf_op jit(solution)/shard_map/ppermute | solution.py:469
  64.4 14.3 %collective-permute-start.9 = (bf16[192,768]{1,0:T(8,128)(2,1)S(1)}, bf16[192,768]{1,0:T(8,128)(2,1)S(1)}, u32[]{:S(2)}, u32[]{:S(2)}) collective-permute-start(bf16[192,768]{1,0:T(8,128)(2,1)S(1)} %get-tuple-element.30), channel_id=1, source_target_pairs={{0,3},{1,0},{2,1},{3,2},{4,7},{5,4},{6,5},{7,6},{8,11},{9,8},{10,9... | collective-permute-start | bytes 884744 | tf_op jit(solution)/shard_map/ppermute | solution.py:469
  79.0 5.5 %collective-permute-start.10 = (bf16[48,768]{1,0:T(8,128)(2,1)S(1)}, bf16[48,768]{1,0:T(8,128)(2,1)S(1)}, u32[]{:S(2)}, u32[]{:S(2)}) collective-permute-start(bf16[48,768]{1,0:T(8,128)(2,1)S(1)} %get-tuple-element.32), channel_id=1, source_target_pairs={{0,16},{4,20},{8,24},{12,28},{16,0},{20,4},{24,8},{28,12},{32,48},... | collective-permute-start | bytes 221192 | tf_op jit(solution)/shard_map/ppermute | solution.py:472
  81.8 4.6 %collective-permute-start.11 = (bf16[48,768]{1,0:T(8,128)(2,1)S(1)}, bf16[48,768]{1,0:T(8,128)(2,1)S(1)}, u32[]{:S(2)}, u32[]{:S(2)}) collective-permute-start(bf16[48,768]{1,0:T(8,128)(2,1)S(1)} %get-tuple-element.33), channel_id=1, source_target_pairs={{0,8},{4,12},{8,16},{12,20},{16,24},{20,28},{24,0},{28,4},{32,40},... | collective-permute-start | bytes 221192 | tf_op jit(solution)/shard_map/ppermute | solution.py:472
  82.1 4.3 %collective-permute-start.12 = (bf16[48,768]{1,0:T(8,128)(2,1)S(1)}, bf16[48,768]{1,0:T(8,128)(2,1)S(1)}, u32[]{:S(2)}, u32[]{:S(2)}) collective-permute-start(bf16[48,768]{1,0:T(8,128)(2,1)S(1)} %get-tuple-element.34), channel_id=1, source_target_pairs={{0,24},{4,28},{8,0},{12,4},{16,8},{20,12},{24,16},{28,20},{32,56},... | collective-permute-start | bytes 221192 | tf_op jit(solution)/shard_map/ppermute | solution.py:472
  86.5 4.8 %collective-permute-start.15 = (bf16[48,768]{1,0:T(8,128)(2,1)S(1)}, bf16[48,768]{1,0:T(8,128)(2,1)S(1)}, u32[]{:S(2)}, u32[]{:S(2)}) collective-permute-start(bf16[48,768]{1,0:T(8,128)(2,1)S(1)} %sum_four.2.refs_0_), channel_id=1, source_target_pairs={{0,64},{4,68},{8,72},{12,76},{16,80},{20,84},{24,88},{28,92},{32,9... | collective-permute-start | bytes 221192 | tf_op jit(solution)/shard_map/ppermute | solution.py:474
  89.1 3.2 %collective-permute-start.14 = (bf16[48,768]{1,0:T(8,128)(2,1)S(1)}, bf16[48,768]{1,0:T(8,128)(2,1)S(1)}, u32[]{:S(2)}, u32[]{:S(2)}) collective-permute-start(bf16[48,768]{1,0:T(8,128)(2,1)S(1)} %sum_four.2.refs_0_), channel_id=1, source_target_pairs={{0,96},{4,100},{8,104},{12,108},{16,112},{20,116},{24,120},{28,124... | collective-permute-start | bytes 221192 | tf_op jit(solution)/shard_map/ppermute | solution.py:474
  90.0 4.6 %collective-permute-start.13 = (bf16[48,768]{1,0:T(8,128)(2,1)S(1)}, bf16[48,768]{1,0:T(8,128)(2,1)S(1)}, u32[]{:S(2)}, u32[]{:S(2)}) collective-permute-start(bf16[48,768]{1,0:T(8,128)(2,1)S(1)} %sum_four.2.refs_0_), channel_id=1, source_target_pairs={{0,32},{4,36},{8,40},{12,44},{16,48},{20,52},{24,56},{28,60},{32,6... | collective-permute-start | bytes 221192 | tf_op jit(solution)/shard_map/ppermute | solution.py:474
  94.6 4.8 %collective-permute-start.18 = (bf16[48,768]{1,0:T(8,128)(2,1)S(1)}, bf16[48,768]{1,0:T(8,128)(2,1)S(1)}, u32[]{:S(2)}, u32[]{:S(2)}) collective-permute-start(bf16[48,768]{1,0:T(8,128)(2,1)S(1)} %sum_four.3.refs_0_), channel_id=1, source_target_pairs={{0,24},{4,28},{8,0},{12,4},{16,8},{20,12},{24,16},{28,20},{32,56},... | collective-permute-start | bytes 221192 | tf_op jit(solution)/shard_map/ppermute | solution.py:477
  97.3 4.8 %collective-permute-start.17 = (bf16[48,768]{1,0:T(8,128)(2,1)S(1)}, bf16[48,768]{1,0:T(8,128)(2,1)S(1)}, u32[]{:S(2)}, u32[]{:S(2)}) collective-permute-start(bf16[48,768]{1,0:T(8,128)(2,1)S(1)} %sum_four.3.refs_0_), channel_id=1, source_target_pairs={{0,16},{4,20},{8,24},{12,28},{16,0},{20,4},{24,8},{28,12},{32,48},... | collective-permute-start | bytes 221192 | tf_op jit(solution)/shard_map/ppermute | solution.py:477
  97.5 5.2 %collective-permute-start.16 = (bf16[48,768]{1,0:T(8,128)(2,1)S(1)}, bf16[48,768]{1,0:T(8,128)(2,1)S(1)}, u32[]{:S(2)}, u32[]{:S(2)}) collective-permute-start(bf16[48,768]{1,0:T(8,128)(2,1)S(1)} %sum_four.3.refs_0_), channel_id=1, source_target_pairs={{0,8},{4,12},{8,16},{12,20},{16,24},{20,28},{24,0},{28,4},{32,40},... | collective-permute-start | bytes 221192 | tf_op jit(solution)/shard_map/ppermute | solution.py:477
  102.8 6.3 %collective-permute-start.19 = (bf16[192,768]{1,0:T(8,128)(2,1)S(1)}, bf16[192,768]{1,0:T(8,128)(2,1)S(1)}, u32[]{:S(2)}, u32[]{:S(2)}) collective-permute-start(bf16[192,768]{1,0:T(8,128)(2,1)S(1)} %join_z.1.own), channel_id=1, source_target_pairs={{0,4},{4,0},{8,12},{12,8},{16,20},{20,16},{24,28},{28,24},{32,36},... | collective-permute-start | bytes 884744 | tf_op jit(solution)/shard_map/ppermute | solution.py:479
  (7 other events, 31.8 us)

commit v3 on v2

--- a/solution.py
+++ b/solution.py
@@ -55,11 +55,11 @@
     return pl.CostEstimate(flops=int(flops), bytes_accessed=int(size), transcendentals=int(exps))
 
 
-def d_attn_kernel(pos_ref, *refs):
+def d_attn_kernel(x_ref, core_ref, *refs):
     own, mine, others, dout, out_ref, weight, sems = (
         refs[0], refs[1:4], refs[4:7], *refs[7:]
     )
-    x, core = pos_ref[0], pos_ref[1]
+    x, core = x_ref[0], core_ref[0]
 
     def shard_rows(k):
         return pl.ds(pl.multiple_of(lax.rem(x - k + N_FSDP, N_FSDP) * SHARD, SHARD), SHARD)
@@ -76,17 +76,17 @@
     out_ref[...] = dot(weight[...], dout[...], NT).astype(BF16)
 
 
-def d_attn_transposed(pos, own, mine, others, dout):
+def d_attn_transposed(x, core, own, mine, others, dout):
     return pl.pallas_call(
         d_attn_kernel,
         out_shape=shape((HQ * HD, TOK)),
-        in_specs=[SMEM] + [ANY] * 7 + [VMEM],
+        in_specs=[SMEM, SMEM] + [ANY] * 7 + [VMEM],
         out_specs=VMEM,
         scratch_shapes=[pltpu.VMEM((HQ * HD, D), BF16), pltpu.SemaphoreType.DMA((7,))],
         compiler_params=params(10),
         name="d_attn",
         cost_estimate=cost(2 * TOK * D * HQ * HD, 8 * 2**20),
-    )(pos, own, *mine, *others, dout)
+    )(x, core, own, *mine, *others, dout)
 
 
 TRIO = 3
@@ -103,20 +103,22 @@
     return x.astype(F32).T.astype(BF16)
 
 
-def gather_rows(src_ref, held_ref, inc_ref, rows, sems):
+def gather_rows(group, place_ref, held_ref, inc_ref, rows, sems):
     def copy(ref, b, source):
         return pltpu.make_async_copy(ref.at[source], rows.at[pl.ds(b * BLK, BLK), :], sems.at[b])
 
     for b in range(NB):
-        source = src_ref[b]
-
-        @pl.when(source < NB)
-        def _(b=b, source=source):
-            copy(held_ref, b, source).start()
-
-        @pl.when(source >= NB)
-        def _(b=b, source=source):
-            copy(inc_ref, b, source - NB).start()
+        place = place_ref[group, b]
+        holder = lax.shift_right_logical(place, 5)
+        slot = place - holder * NB
+
+        @pl.when(holder == group)
+        def _(b=b, slot=slot):
+            copy(held_ref, b, slot).start()
+
+        @pl.when(holder != group)
+        def _(b=b, holder=holder):
+            copy(inc_ref, b, holder).start()
 
     def wait_rows(tile):
         per_tile = TILE // BLK
@@ -127,16 +129,24 @@
 
 
 def forward_kernel(
-    core_ref, src_ref, held_ref, inc_ref, pack_ref, dout_hbm, _,
+    group_ref, place_ref, held_ref, inc_ref, pack_ref, dout_hbm, _,
     rows_out, attn_out, stat_ref, send_out,
     rows, attn_ref, send_ref, dout, value_t, sems, side_sems, attn_sems,
 ):
-    wait_rows = gather_rows(src_ref, held_ref, inc_ref, rows, sems)
-    other = pl.ds(pl.multiple_of((1 - core_ref[0]) * HALF, HALF), HALF)
+    group = group_ref[0]
+    wait_rows = gather_rows(group, place_ref, held_ref, inc_ref, rows, sems)
+    other = pl.ds(pl.multiple_of((1 - lax.rem(group, 2)) * HALF, HALF), HALF)
     dout_copy = pltpu.make_async_copy(dout_hbm.at[:, other], dout, side_sems.at[0])
     dout_copy.start()
     rows_copy = pltpu.make_async_copy(rows, rows_out, side_sems.at[1])
-    send_copy = pltpu.make_async_copy(send_ref, send_out, side_sems.at[2])
+    send_copies = [
+        pltpu.make_async_copy(
+            send_ref.at[pl.ds(half * (HQ * HD // 2), HQ * HD // 2), :],
+            send_out.at[pl.ds(half * (HQ * HD // 2), HQ * HD // 2), :],
+            side_sems.at[2 + half],
+        )
+        for half in range(2)
+    ]
     attn_copies = [
         pltpu.make_async_copy(
             attn_ref.at[pl.ds(h * HD, HD), :], attn_out.at[pl.ds(h * HD, HD), :], attn_sems.at[h]
@@ -177,13 +187,15 @@
     for copy in attn_copies:
         copy.start()
     dout_copy.wait()
-    send_ref[...] = dot(attn_ref[...], dout[...], NN).astype(BF16)
-    send_copy.start()
-    for copy in (rows_copy, *attn_copies, send_copy):
+    for half, copy in enumerate(send_copies):
+        part = slice(half * (HQ * HD // 2), (half + 1) * (HQ * HD // 2))
+        send_ref[part, :] = dot(attn_ref[part, :], dout[...], NN).astype(BF16)
+        copy.start()
+    for copy in (rows_copy, *attn_copies, *send_copies):
         copy.wait()
 
 
-def forward(core, src, held, inc, pack, dout, after):
+def forward(group, place, held, inc, pack, dout, after):
     n = HQ * HD
     return pl.pallas_call(
         forward_kernel,
@@ -199,13 +211,13 @@
             pltpu.VMEM((TOK, HALF), BF16),
             pltpu.VMEM((HD, TOK), BF16),
             pltpu.SemaphoreType.DMA((NB,)),
-            pltpu.SemaphoreType.DMA((3,)),
+            pltpu.SemaphoreType.DMA((4,)),
             pltpu.SemaphoreType.DMA((HQ,)),
         ],
         compiler_params=params(LARGE),
         name="forward",
         cost_estimate=cost(12 * 10**9, 8 * 2**20, HQ * 655360),
-    )(core, src, held, inc, pack, dout, after)
+    )(group, place, held, inc, pack, dout, after)
 
 
 def keep_kernel(core_ref, attn_ref, dout_hbm, keep_ref, dout, sem):
@@ -317,15 +329,13 @@
 
 def add_pair_kernel(x_ref, keep_ref, got_hbm, *outs):
     *outs, token, got_ref, sems = outs
-    loads = [pltpu.make_async_copy(got_hbm.at[k], got_ref.at[k], sems.at[k]) for k in range(N_FSDP)]
-    for load in loads:
-        load.start()
-    for load in loads:
-        load.wait()
+    for k in range(N_FSDP):
+        pltpu.make_async_copy(got_hbm.at[k], got_ref.at[k], sems.at[k]).start()
     token[...] = jnp.zeros(token.shape, F32)
     x = x_ref[0]
     for k, out in enumerate(outs):
         shard = lax.rem(x + k, N_FSDP)
+        pltpu.make_async_copy(got_hbm.at[shard], got_ref.at[shard], sems.at[shard]).wait()
         out[...] = (keep_ref[shard].astype(F32) + got_ref[shard].astype(F32)).astype(out.dtype)
 
 
@@ -451,8 +461,6 @@
     holder = stash_place // NB
     slot = stash_place % NB
     chosen = jnp.sum(jnp.where((holder == group) & (peers[:, None] != group), slot, 0), axis=1)
-    mine = lax.dynamic_index_in_dim(stash_place, group, 0, keepdims=False)
-    source = jnp.where(mine // NB == group, mine % NB, NB + mine // NB)
     x1, z1, core1 = x.reshape(1), z.reshape(1), core.reshape(1)
 
     incoming = lax.all_to_all(held[chosen], "dp", split_axis=0, concat_axis=0, tiled=True)
@@ -460,10 +468,10 @@
     half = lax.dynamic_slice_in_dim(out_weight, core * HALF, HALF, 1)
     weight_mine = [lax.ppermute(half, "fsdp", x_shift(k)) for k in (1, 2, 3)]
     weight_other = [lax.ppermute(part, "dp", swap) for part in weight_mine]
-    d_attn_t = d_attn_transposed(jnp.stack([x, core]), out_weight, weight_mine, weight_other, d_out)
+    d_attn_t = d_attn_transposed(x1, core1, out_weight, weight_mine, weight_other, d_out)
 
     pack = pack_start.reshape(1, TOK)
-    rows, attn_t, stats, send = forward(core1, source, held, incoming, pack, d_out, d_attn_t)
+    rows, attn_t, stats, send = forward(group.reshape(1), stash_place, held, incoming, pack, d_out, d_attn_t)
     keep = keep_half(core1, attn_t, d_out)
     *parts, x_token = add_pair(x1, keep, lax.ppermute(send, "dp", swap))
     by_x = [parts[0]] + [lax.ppermute(parts[k], "fsdp", x_shift(k)) for k in (2, 1, 3)]

time: 111 us -> 109 us (0.982)
  waiting for transfers between devices: 26.5 us -> 29 us
  Pallas kernels: 33.3 us -> 32 us
  other arithmetic: 2.2 us -> 0.92 us
  starting transfers between devices: 39.1 us -> 37.9 us
    ppermute x3, waiting for transfers between devices: 0.27 us -> 1.55 us  [per_device(): weight_other = [lax.ppermute(part, 'dp', swap) for part in weight_mine]]
    select_n x1 -> x0, other arithmetic: 1.2 us -> none  [per_device(): source = jnp.where(mine // NB == group, mine % NB, NB + mine // NB)]
  transfers between devices with their start and end apart: 21 -> 21, of which waited for: 11 -> 11; matrix products, arithmetic and copies ran while one was open for 2% -> 1% of each run, Pallas kernels for 16% -> 16%
where the time goes in v3:
time: 109 us
  starting transfers between devices  37.9 us (35%)
  Pallas kernels  32 us (29%)
  waiting for transfers between devices  29 us (27%)
  local copies, waits for them, and re-layouts  8.22 us (8%)
    ppermute x3, waiting for transfers between devices, per_device(): weight_mine = [lax.ppermute(half, 'fsdp', x_shift(k)) for k in (1, 2, 3)]  14.4 us
    pallas_call x1, Pallas kernels, backward(): pl.pallas_call(backward_kernel, out_shape=[shape((TOK, HQ * HD)), shape((...  11.9 us
    pallas_call x1, Pallas kernels, forward(): pl.pallas_call(forward_kernel, out_shape=[shape((TOK, WIDTH)), shape((n,...  11.5 us
    all_to_all x1, starting transfers between devices, per_device(): lax.all_to_all(held[chosen], 'dp', split_axis=0, concat_axis=0, tiled=True)  9.92 us
    ppermute x3, starting transfers between devices, per_device(): lax.ppermute(parts[k], 'fsdp', x_shift(k))  5.64 us
    ppermute x1, starting transfers between devices, per_device(): grad_weight = lay_out(core1, own, lax.ppermute(own, 'dp', swap))  5.06 us
    ppermute x3, starting transfers between devices, per_device(): lax.ppermute(by_z[k], 'dp', dp_shift(0, k, 0))  4.82 us
    ppermute x3, waiting for transfers between devices, per_device(): by_z = {k: lax.ppermute(total, 'dp', dp_shift(0, k, 0)) for k in (1, 3, 2)}  4.72 us
  transfers between devices with their start and end apart: 21, of which 11 were waited for; matrix products, arithmetic and copies ran while one was open for 1% of the time, Pallas kernels for 16%

profile of v3, /device:TPU:1, one launch (start us, length us, event | category | flops | bytes accessed | tf_op | source)
XLA Modules:
  0.0 108.8 jit_solution(3511634428176931450)
XLA Ops:
  1.6 3.6 %gather_fusion = bf16[32,32,1024]{2,1,0:T(8,128)(2,1)} fusion(bf16[32,32,1024]{2,1,0:T(8,128)(2,1)} %bitcast.15, s32[1024]{0:T(1024)S(1)} %pad_clamp_fusion), kind=kCustom, calls=%fused_computation | custom fusion | bytes 4194432 | tf_op jit(solution)/shard_map/gather | solution.py:466
  5.2 9.9 %all-to-all-start = ((bf16[32,32,1024]{2,1,0:T(8,128)(2,1)}), bf16[32,32,1024]{2,1,0:T(8,128)(2,1)}, u32[]{:S(2)}, u32[]{:S(2)}) async-start(bf16[32,32,1024]{2,1,0:T(8,128)(2,1)} %gather_fusion), calls=%async_computation | async-start | bytes 4194304 | tf_op jit(solution)/shard_map/all_to_all | solution.py:466
  16.1 2.5 %collective-permute-start.2 = (bf16[192,768]{1,0:T(8,128)(2,1)S(1)}, bf16[192,768]{1,0:T(8,128)(2,1)S(1)}, u32[]{:S(2)}, u32[]{:S(2)}) collective-permute-start(bf16[192,768]{1,0:T(8,128)(2,1)S(1)} %constant_dynamic-slice_fusion), channel_id=1, source_target_pairs={{0,3},{1,0},{2,1},{3,2},{4,7},{5,4},{6,5},{7,6},{8,11},{9,8},{10,9... | collective-permute-start | bytes 884744 | tf_op jit(solution)/shard_map/ppermute | solution.py:469
  19.8 11.1 %collective-permute-done.2.refs_3_ = bf16[192,768]{1,0:T(8,128)(2,1)S(1)} collective-permute-done((bf16[192,768]{1,0:T(8,128)(2,1)S(1)}, bf16[192,768]{1,0:T(8,128)(2,1)S(1)}, u32[]{:S(2)}, u32[]{:S(2)}) %collective-permute-start.2) | collective-permute-done | bytes 294944 | tf_op jit(solution)/shard_map/ppermute | solution.py:469
  32.2 3.3 %collective-permute-done.refs_1_ = bf16[192,768]{1,0:T(8,128)(2,1)} collective-permute-done((bf16[192,768]{1,0:T(8,128)(2,1)S(1)}, bf16[192,768]{1,0:T(8,128)(2,1)}, u32[]{:S(2)}, u32[]{:S(2)}) %collective-permute-start) | collective-permute-done | bytes 294944 | tf_op jit(solution)/shard_map/ppermute | solution.py:469
  36.0 1.5 %collective-permute-done.3.refs_4_ = bf16[192,768]{1,0:T(8,128)(2,1)} collective-permute-done((bf16[192,768]{1,0:T(8,128)(2,1)}, bf16[192,768]{1,0:T(8,128)(2,1)}, u32[]{:S(2)}, u32[]{:S(2)}) %collective-permute-start.3) | collective-permute-done | bytes 294944 | tf_op jit(solution)/shard_map/ppermute | solution.py:470
  38.6 4.1 %d_attn.1._.dt = bf16[768,1024]{1,0:T(8,128)(2,1)S(1)} custom-call(s32[1]{0:T(128)} %bitcast.5.x_ref, s32[1]{0:T(128)} %bitcast.6.core_ref, bf16[192,1536]{1,0:T(8,128)(2,1)S(1)} %copy-done.4, bf16[192,768]{1,0:T(8,128)(2,1)} %collective-permute-done.refs_1_, bf16[192,768]{1,0:T(8,128)(2,1)} %collective-permute-done.1.refs_2_, ...), custom_call_target="tpu_custom_call" | custom-call | flops 2415919104 | bytes 8388608 | tf_op jit(solution)/shard_map/d_attn/pallas_call | solution.py:80
  43.9 11.5 %forward.1 = (bf16[1024,1024]{1,0:T(8,128)(2,1)}, bf16[768,1024]{1,0:T(8,128)(2,1)}, f32[8,1024]{1,0:T(8,128)}, bf16[768,768]{1,0:T(8,128)(2,1)}) custom-call(s32[1]{0:T(128)} %bitcast.group_ref, s32[32,32]{1,0:T(8,128)} %place_ref.1, bf16[32,32,1024]{2,1,0:T(8,128)(2,1)} %bitcast.16, bf16[32,32,1024]{2,1,0:T(8,128)(2,1)} %all-to-all-done.inc_ref, ...), custom_call_target="tpu_custom_call" | custom-call | flops 12000000000 | bytes 8388608 | tf_op jit(solution)/shard_map/forward/pallas_call | solution.py:200
  56.1 1.4 %copy-done.2 = bf16[768,1024]{1,0:T(8,128)(2,1)S(1)} copy-done((bf16[768,1024]{1,0:T(8,128)(2,1)S(1)}, bf16[768,1024]{1,0:T(8,128)(2,1)}, u32[]{:S(2)}) %copy-start.2) | copy-done | bytes 1572888
  57.5 1.5 %keep_half.1 = bf16[768,768]{1,0:T(8,128)(2,1)S(1)} custom-call(s32[1]{0:T(128)} %bitcast.6.core_ref, bf16[768,1024]{1,0:T(8,128)(2,1)S(1)} %copy-done.2, bf16[1024,1536]{1,0:T(8,128)(2,1)S(1)} %copy-done.1), custom_call_target="tpu_custom_call" | custom-call | flops 1207959552 | bytes 8388608 | tf_op jit(solution)/shard_map/keep_half/pallas_call | solution.py:232
  59.1 1.4 %add_pair.1 = (f32[192,768]{1,0:T(8,128)S(1)}, bf16[192,768]{1,0:T(8,128)(2,1)S(1)}, bf16[192,768]{1,0:T(8,128)(2,1)S(1)}, bf16[192,768]{1,0:T(8,128)(2,1)S(1)}, f32[8,128]{1,0:T(8,128)S(1)}) custom-call(s32[1]{0:T(128)} %bitcast.5.x_ref, bf16[4,192,768]{2,1,0:T(8,128)(2,1)S(1)} %bitcast.12, bf16[4,192,768]{2,1,0:T(8,128)(2,1)} %bitcast.8.got_hbm), custom_call_target="tpu_custom_call" | custom-call | flops 589824 | bytes 2949120 | tf_op jit(solution)/shard_map/add_pair/pallas_call | solution.py:345
  60.5 3.0 %collective-permute-start.7 = (bf16[192,768]{1,0:T(8,128)(2,1)S(1)}, bf16[192,768]{1,0:T(8,128)(2,1)S(1)}, u32[]{:S(2)}, u32[]{:S(2)}) collective-permute-start(bf16[192,768]{1,0:T(8,128)(2,1)S(1)} %get-tuple-element.28), channel_id=1, source_target_pairs={{0,2},{1,3},{2,0},{3,1},{4,6},{5,7},{6,4},{7,5},{8,10},{9,11},{10,... | collective-permute-start | bytes 884744 | tf_op jit(solution)/shard_map/ppermute | solution.py:477
  63.9 2.3 %collective-permute-start.9 = (bf16[192,768]{1,0:T(8,128)(2,1)S(1)}, bf16[192,768]{1,0:T(8,128)(2,1)S(1)}, u32[]{:S(2)}, u32[]{:S(2)}) collective-permute-start(bf16[192,768]{1,0:T(8,128)(2,1)S(1)} %get-tuple-element.30), channel_id=1, source_target_pairs={{0,3},{1,0},{2,1},{3,2},{4,7},{5,4},{6,5},{7,6},{8,11},{9,8},{10,9... | collective-permute-start | bytes 884744 | tf_op jit(solution)/shard_map/ppermute | solution.py:477
  66.2 11.9 %backward.1 = (bf16[1024,768]{1,0:T(8,128)(2,1)}, bf16[1024,256]{1,0:T(8,128)(2,1)}, f32[8,128]{1,0:T(8,128)S(1)}) custom-call(bf16[1024,1024]{1,0:T(8,128)(2,1)S(1)} %copy-done.8, s32[1,1024]{1,0:T(1,128)S(1)} %bitcast.14, bf16[768,1024]{1,0:T(8,128)(2,1)S(1)} %copy-done.7, bf16[768,1024]{1,0:T(8,128)(2,1)S(1)} %copy-done.3, f32[8,1024]{1,0:T(8,128)S(1)} %copy-done.9, ...), custom_call_target="tpu_custom_call" | custom-call | flops 30000001024 | bytes 8388608 | tf_op jit(solution)/shard_map/backward/pallas_call | solution.py:311
  78.4 2.1 %collective-permute-start.10 = (bf16[48,768]{1,0:T(8,128)(2,1)S(1)}, bf16[48,768]{1,0:T(8,128)(2,1)S(1)}, u32[]{:S(2)}, u32[]{:S(2)}) collective-permute-start(bf16[48,768]{1,0:T(8,128)(2,1)S(1)} %get-tuple-element.32), channel_id=1, source_target_pairs={{0,16},{4,20},{8,24},{12,28},{16,0},{20,4},{24,8},{28,12},{32,48},... | collective-permute-start | bytes 221192 | tf_op jit(solution)/shard_map/ppermute | solution.py:480
  80.8 2.4 %collective-permute-start.12 = (bf16[48,768]{1,0:T(8,128)(2,1)S(1)}, bf16[48,768]{1,0:T(8,128)(2,1)S(1)}, u32[]{:S(2)}, u32[]{:S(2)}) collective-permute-start(bf16[48,768]{1,0:T(8,128)(2,1)S(1)} %get-tuple-element.34), channel_id=1, source_target_pairs={{0,24},{4,28},{8,0},{12,4},{16,8},{20,12},{24,16},{28,20},{32,56},... | collective-permute-start | bytes 221192 | tf_op jit(solution)/shard_map/ppermute | solution.py:480
  83.2 2.8 %collective-permute-done.11.refs_2_ = bf16[48,768]{1,0:T(8,128)(2,1)S(1)} collective-permute-done((bf16[48,768]{1,0:T(8,128)(2,1)S(1)}, bf16[48,768]{1,0:T(8,128)(2,1)S(1)}, u32[]{:S(2)}, u32[]{:S(2)}) %collective-permute-start.11) | collective-permute-done | bytes 73760 | tf_op jit(solution)/shard_map/ppermute | solution.py:480
  86.0 1.7 %collective-permute-start.15 = (bf16[48,768]{1,0:T(8,128)(2,1)S(1)}, bf16[48,768]{1,0:T(8,128)(2,1)S(1)}, u32[]{:S(2)}, u32[]{:S(2)}) collective-permute-start(bf16[48,768]{1,0:T(8,128)(2,1)S(1)} %sum_four.2.refs_0_), channel_id=1, source_target_pairs={{0,64},{4,68},{8,72},{12,76},{16,80},{20,84},{24,88},{28,92},{32,9... | collective-permute-start | bytes 221192 | tf_op jit(solution)/shard_map/ppermute | solution.py:482
  89.2 1.6 %collective-permute-done.15.refs_3_ = bf16[48,768]{1,0:T(8,128)(2,1)S(1)} collective-permute-done((bf16[48,768]{1,0:T(8,128)(2,1)S(1)}, bf16[48,768]{1,0:T(8,128)(2,1)S(1)}, u32[]{:S(2)}, u32[]{:S(2)}) %collective-permute-start.15) | collective-permute-done | bytes 73760 | tf_op jit(solution)/shard_map/ppermute | solution.py:482
  91.0 2.5 %collective-permute-done.13.refs_1_ = bf16[48,768]{1,0:T(8,128)(2,1)S(1)} collective-permute-done((bf16[48,768]{1,0:T(8,128)(2,1)S(1)}, bf16[48,768]{1,0:T(8,128)(2,1)S(1)}, u32[]{:S(2)}, u32[]{:S(2)}) %collective-permute-start.13) | collective-permute-done | bytes 73760 | tf_op jit(solution)/shard_map/ppermute | solution.py:482
  93.5 2.5 %collective-permute-start.18 = (bf16[48,768]{1,0:T(8,128)(2,1)S(1)}, bf16[48,768]{1,0:T(8,128)(2,1)S(1)}, u32[]{:S(2)}, u32[]{:S(2)}) collective-permute-start(bf16[48,768]{1,0:T(8,128)(2,1)S(1)} %sum_four.3.refs_0_), channel_id=1, source_target_pairs={{0,24},{4,28},{8,0},{12,4},{16,8},{20,12},{24,16},{28,20},{32,56},... | collective-permute-start | bytes 221192 | tf_op jit(solution)/shard_map/ppermute | solution.py:485
  96.7 1.4 %collective-permute-done.18.refs_3_ = bf16[48,768]{1,0:T(8,128)(2,1)S(1)} collective-permute-done((bf16[48,768]{1,0:T(8,128)(2,1)S(1)}, bf16[48,768]{1,0:T(8,128)(2,1)S(1)}, u32[]{:S(2)}, u32[]{:S(2)}) %collective-permute-start.18) | collective-permute-done | bytes 73760 | tf_op jit(solution)/shard_map/ppermute | solution.py:485
  98.1 2.7 %collective-permute-done.17.refs_2_ = bf16[48,768]{1,0:T(8,128)(2,1)S(1)} collective-permute-done((bf16[48,768]{1,0:T(8,128)(2,1)S(1)}, bf16[48,768]{1,0:T(8,128)(2,1)S(1)}, u32[]{:S(2)}, u32[]{:S(2)}) %collective-permute-start.17) | collective-permute-done | bytes 73760 | tf_op jit(solution)/shard_map/ppermute | solution.py:485
  101.4 5.1 %collective-permute-start.19 = (bf16[192,768]{1,0:T(8,128)(2,1)S(1)}, bf16[192,768]{1,0:T(8,128)(2,1)S(1)}, u32[]{:S(2)}, u32[]{:S(2)}) collective-permute-start(bf16[192,768]{1,0:T(8,128)(2,1)S(1)} %join_z.1.own), channel_id=1, source_target_pairs={{0,4},{4,0},{8,12},{12,8},{16,20},{20,16},{24,28},{28,24},{32,36},... | collective-permute-start | bytes 884744 | tf_op jit(solution)/shard_map/ppermute | solution.py:487
  (54 shorter events, 13.9 us)
Async XLA Ops:
  5.2 32.4 %copy-start = (bf16[1024,1536]{1,0:T(8,128)(2,1)S(1)}, bf16[1024,1536]{1,0:T(8,128)(2,1)}, u32[]{:S(2)}) copy-start(bf16[1024,1536]{1,0:T(8,128)(2,1)} %dout_hbm.3) | copy-start | bytes 9437188
  5.2 38.7 %all-to-all-start = ((bf16[32,32,1024]{2,1,0:T(8,128)(2,1)}), bf16[32,32,1024]{2,1,0:T(8,128)(2,1)}, u32[]{:S(2)}, u32[]{:S(2)}) async-start(bf16[32,32,1024]{2,1,0:T(8,128)(2,1)} %gather_fusion), calls=%async_computation | async-start | bytes 4194304 | tf_op jit(solution)/shard_map/all_to_all | solution.py:466
  16.1 14.8 %collective-permute-start.2 = (bf16[192,768]{1,0:T(8,128)(2,1)S(1)}, bf16[192,768]{1,0:T(8,128)(2,1)S(1)}, u32[]{:S(2)}, u32[]{:S(2)}) collective-permute-start(bf16[192,768]{1,0:T(8,128)(2,1)S(1)} %constant_dynamic-slice_fusion), channel_id=1, source_target_pairs={{0,3},{1,0},{2,1},{3,2},{4,7},{5,4},{6,5},{7,6},{8,11},{9,8},{10,9... | collective-permute-start | bytes 884744 | tf_op jit(solution)/shard_map/ppermute | solution.py:469
  18.6 13.6 %collective-permute-start.1 = (bf16[192,768]{1,0:T(8,128)(2,1)S(1)}, bf16[192,768]{1,0:T(8,128)(2,1)}, u32[]{:S(2)}, u32[]{:S(2)}) collective-permute-start(bf16[192,768]{1,0:T(8,128)(2,1)S(1)} %constant_dynamic-slice_fusion), channel_id=1, source_target_pairs={{0,2},{1,3},{2,0},{3,1},{4,6},{5,7},{6,4},{7,5},{8,10},{9,11},{10,... | collective-permute-start | bytes 884744 | tf_op jit(solution)/shard_map/ppermute | solution.py:469
  19.2 16.3 %collective-permute-start = (bf16[192,768]{1,0:T(8,128)(2,1)S(1)}, bf16[192,768]{1,0:T(8,128)(2,1)}, u32[]{:S(2)}, u32[]{:S(2)}) collective-permute-start(bf16[192,768]{1,0:T(8,128)(2,1)S(1)} %constant_dynamic-slice_fusion), channel_id=1, source_target_pairs={{0,1},{1,2},{2,3},{3,0},{4,5},{5,6},{6,7},{7,4},{8,9},{9,10},{10,1... | collective-permute-start | bytes 884744 | tf_op jit(solution)/shard_map/ppermute | solution.py:469
  30.9 5.1 %collective-permute-start.5 = (bf16[192,768]{1,0:T(8,128)(2,1)S(1)}, bf16[192,768]{1,0:T(8,128)(2,1)}, u32[]{:S(2)}, u32[]{:S(2)}) collective-permute-start(bf16[192,768]{1,0:T(8,128)(2,1)S(1)} %collective-permute-done.2.refs_3_), channel_id=1, source_target_pairs={{0,4},{4,0},{8,12},{12,8},{16,20},{20,16},{24,28},{28,24},{32,36},... | collective-permute-start | bytes 884744 | tf_op jit(solution)/shard_map/ppermute | solution.py:470
  32.2 3.8 %collective-permute-start.4 = (bf16[192,768]{1,0:T(8,128)(2,1)}, bf16[192,768]{1,0:T(8,128)(2,1)}, u32[]{:S(2)}, u32[]{:S(2)}) collective-permute-start(bf16[192,768]{1,0:T(8,128)(2,1)} %collective-permute-done.1.refs_2_), channel_id=1, source_target_pairs={{0,4},{4,0},{8,12},{12,8},{16,20},{20,16},{24,28},{28,24},{32,36},... | collective-permute-start | bytes 884744 | tf_op jit(solution)/shard_map/ppermute | solution.py:470
  35.5 2.0 %collective-permute-start.3 = (bf16[192,768]{1,0:T(8,128)(2,1)}, bf16[192,768]{1,0:T(8,128)(2,1)}, u32[]{:S(2)}, u32[]{:S(2)}) collective-permute-start(bf16[192,768]{1,0:T(8,128)(2,1)} %collective-permute-done.refs_1_), channel_id=1, source_target_pairs={{0,4},{4,0},{8,12},{12,8},{16,20},{20,16},{24,28},{28,24},{32,36},... | collective-permute-start | bytes 884744 | tf_op jit(solution)/shard_map/ppermute | solution.py:470
  43.9 12.2 %copy-start.1 = (bf16[1024,1536]{1,0:T(8,128)(2,1)S(1)}, bf16[1024,1536]{1,0:T(8,128)(2,1)}, u32[]{:S(2)}) copy-start(bf16[1024,1536]{1,0:T(8,128)(2,1)} %dout_hbm.3) | copy-start | bytes 9437188
  55.4 3.6 %collective-permute-start.6 = (bf16[768,768]{1,0:T(8,128)(2,1)}, bf16[768,768]{1,0:T(8,128)(2,1)}, u32[]{:S(2)}, u32[]{:S(2)}) collective-permute-start(bf16[768,768]{1,0:T(8,128)(2,1)} %get-tuple-element.22), channel_id=1, source_target_pairs={{0,4},{4,0},{8,12},{12,8},{16,20},{20,16},{24,28},{28,24},{32,36},... | collective-permute-start | bytes 3538952 | tf_op jit(solution)/shard_map/ppermute | solution.py:476
  57.5 8.7 %copy-start.8 = (bf16[1024,1024]{1,0:T(8,128)(2,1)S(1)}, bf16[1024,1024]{1,0:T(8,128)(2,1)}, u32[]{:S(2)}) copy-start(bf16[1024,1024]{1,0:T(8,128)(2,1)} %get-tuple-element.19.rows) | copy-start | bytes 6291460
  60.5 17.6 %collective-permute-start.7 = (bf16[192,768]{1,0:T(8,128)(2,1)S(1)}, bf16[192,768]{1,0:T(8,128)(2,1)S(1)}, u32[]{:S(2)}, u32[]{:S(2)}) collective-permute-start(bf16[192,768]{1,0:T(8,128)(2,1)S(1)} %get-tuple-element.28), channel_id=1, source_target_pairs={{0,2},{1,3},{2,0},{3,1},{4,6},{5,7},{6,4},{7,5},{8,10},{9,11},{10,... | collective-permute-start | bytes 884744 | tf_op jit(solution)/shard_map/ppermute | solution.py:477
  63.5 14.7 %collective-permute-start.8 = (bf16[192,768]{1,0:T(8,128)(2,1)S(1)}, bf16[192,768]{1,0:T(8,128)(2,1)S(1)}, u32[]{:S(2)}, u32[]{:S(2)}) collective-permute-start(bf16[192,768]{1,0:T(8,128)(2,1)S(1)} %get-tuple-element.29), channel_id=1, source_target_pairs={{0,1},{1,2},{2,3},{3,0},{4,5},{5,6},{6,7},{7,4},{8,9},{9,10},{10,1... | collective-permute-start | bytes 884744 | tf_op jit(solution)/shard_map/ppermute | solution.py:477
  63.9 14.3 %collective-permute-start.9 = (bf16[192,768]{1,0:T(8,128)(2,1)S(1)}, bf16[192,768]{1,0:T(8,128)(2,1)S(1)}, u32[]{:S(2)}, u32[]{:S(2)}) collective-permute-start(bf16[192,768]{1,0:T(8,128)(2,1)S(1)} %get-tuple-element.30), channel_id=1, source_target_pairs={{0,3},{1,0},{2,1},{3,2},{4,7},{5,4},{6,5},{7,6},{8,11},{9,8},{10,9... | collective-permute-start | bytes 884744 | tf_op jit(solution)/shard_map/ppermute | solution.py:477
  78.4 4.8 %collective-permute-start.10 = (bf16[48,768]{1,0:T(8,128)(2,1)S(1)}, bf16[48,768]{1,0:T(8,128)(2,1)S(1)}, u32[]{:S(2)}, u32[]{:S(2)}) collective-permute-start(bf16[48,768]{1,0:T(8,128)(2,1)S(1)} %get-tuple-element.32), channel_id=1, source_target_pairs={{0,16},{4,20},{8,24},{12,28},{16,0},{20,4},{24,8},{28,12},{32,48},... | collective-permute-start | bytes 221192 | tf_op jit(solution)/shard_map/ppermute | solution.py:480
  80.5 5.5 %collective-permute-start.11 = (bf16[48,768]{1,0:T(8,128)(2,1)S(1)}, bf16[48,768]{1,0:T(8,128)(2,1)S(1)}, u32[]{:S(2)}, u32[]{:S(2)}) collective-permute-start(bf16[48,768]{1,0:T(8,128)(2,1)S(1)} %get-tuple-element.33), channel_id=1, source_target_pairs={{0,8},{4,12},{8,16},{12,20},{16,24},{20,28},{24,0},{28,4},{32,40},... | collective-permute-start | bytes 221192 | tf_op jit(solution)/shard_map/ppermute | solution.py:480
  80.8 5.2 %collective-permute-start.12 = (bf16[48,768]{1,0:T(8,128)(2,1)S(1)}, bf16[48,768]{1,0:T(8,128)(2,1)S(1)}, u32[]{:S(2)}, u32[]{:S(2)}) collective-permute-start(bf16[48,768]{1,0:T(8,128)(2,1)S(1)} %get-tuple-element.34), channel_id=1, source_target_pairs={{0,24},{4,28},{8,0},{12,4},{16,8},{20,12},{24,16},{28,20},{32,56},... | collective-permute-start | bytes 221192 | tf_op jit(solution)/shard_map/ppermute | solution.py:480
  86.0 4.8 %collective-permute-start.15 = (bf16[48,768]{1,0:T(8,128)(2,1)S(1)}, bf16[48,768]{1,0:T(8,128)(2,1)S(1)}, u32[]{:S(2)}, u32[]{:S(2)}) collective-permute-start(bf16[48,768]{1,0:T(8,128)(2,1)S(1)} %sum_four.2.refs_0_), channel_id=1, source_target_pairs={{0,64},{4,68},{8,72},{12,76},{16,80},{20,84},{24,88},{28,92},{32,9... | collective-permute-start | bytes 221192 | tf_op jit(solution)/shard_map/ppermute | solution.py:482
  87.8 3.2 %collective-permute-start.14 = (bf16[48,768]{1,0:T(8,128)(2,1)S(1)}, bf16[48,768]{1,0:T(8,128)(2,1)S(1)}, u32[]{:S(2)}, u32[]{:S(2)}) collective-permute-start(bf16[48,768]{1,0:T(8,128)(2,1)S(1)} %sum_four.2.refs_0_), channel_id=1, source_target_pairs={{0,96},{4,100},{8,104},{12,108},{16,112},{20,116},{24,120},{28,124... | collective-permute-start | bytes 221192 | tf_op jit(solution)/shard_map/ppermute | solution.py:482
  88.6 4.8 %collective-permute-start.13 = (bf16[48,768]{1,0:T(8,128)(2,1)S(1)}, bf16[48,768]{1,0:T(8,128)(2,1)S(1)}, u32[]{:S(2)}, u32[]{:S(2)}) collective-permute-start(bf16[48,768]{1,0:T(8,128)(2,1)S(1)} %sum_four.2.refs_0_), channel_id=1, source_target_pairs={{0,32},{4,36},{8,40},{12,44},{16,48},{20,52},{24,56},{28,60},{32,6... | collective-permute-start | bytes 221192 | tf_op jit(solution)/shard_map/ppermute | solution.py:482
  93.5 4.6 %collective-permute-start.18 = (bf16[48,768]{1,0:T(8,128)(2,1)S(1)}, bf16[48,768]{1,0:T(8,128)(2,1)S(1)}, u32[]{:S(2)}, u32[]{:S(2)}) collective-permute-start(bf16[48,768]{1,0:T(8,128)(2,1)S(1)} %sum_four.3.refs_0_), channel_id=1, source_target_pairs={{0,24},{4,28},{8,0},{12,4},{16,8},{20,12},{24,16},{28,20},{32,56},... | collective-permute-start | bytes 221192 | tf_op jit(solution)/shard_map/ppermute | solution.py:485
  96.0 4.8 %collective-permute-start.17 = (bf16[48,768]{1,0:T(8,128)(2,1)S(1)}, bf16[48,768]{1,0:T(8,128)(2,1)S(1)}, u32[]{:S(2)}, u32[]{:S(2)}) collective-permute-start(bf16[48,768]{1,0:T(8,128)(2,1)S(1)} %sum_four.3.refs_0_), channel_id=1, source_target_pairs={{0,16},{4,20},{8,24},{12,28},{16,0},{20,4},{24,8},{28,12},{32,48},... | collective-permute-start | bytes 221192 | tf_op jit(solution)/shard_map/ppermute | solution.py:485
  96.2 5.2 %collective-permute-start.16 = (bf16[48,768]{1,0:T(8,128)(2,1)S(1)}, bf16[48,768]{1,0:T(8,128)(2,1)S(1)}, u32[]{:S(2)}, u32[]{:S(2)}) collective-permute-start(bf16[48,768]{1,0:T(8,128)(2,1)S(1)} %sum_four.3.refs_0_), channel_id=1, source_target_pairs={{0,8},{4,12},{8,16},{12,20},{16,24},{20,28},{24,0},{28,4},{32,40},... | collective-permute-start | bytes 221192 | tf_op jit(solution)/shard_map/ppermute | solution.py:485
  101.4 6.3 %collective-permute-start.19 = (bf16[192,768]{1,0:T(8,128)(2,1)S(1)}, bf16[192,768]{1,0:T(8,128)(2,1)S(1)}, u32[]{:S(2)}, u32[]{:S(2)}) collective-permute-start(bf16[192,768]{1,0:T(8,128)(2,1)S(1)} %join_z.1.own), channel_id=1, source_target_pairs={{0,4},{4,0},{8,12},{12,8},{16,20},{20,16},{24,28},{28,24},{32,36},... | collective-permute-start | bytes 884744 | tf_op jit(solution)/shard_map/ppermute | solution.py:487
  (7 other events, 33.7 us)

commit v4 on v3

--- a/solution.py
+++ b/solution.py
@@ -355,10 +355,8 @@
 
 
 def sum4(parts):
-    total = parts[0].astype(F32)
-    for part in parts[1:]:
-        total = total + part.astype(F32)
-    return total
+    own, next_one, last, opposite = (part.astype(F32) for part in parts)
+    return (own + opposite) + (next_one + last)
 
 
 def split_z_kernel(z_ref, _, *refs):

time: 109 us -> 109 us (level)
  no operation moved by 1% of the time
where the time goes in v4:
time: 109 us
  starting transfers between devices  37.9 us (35%)
  Pallas kernels  32 us (29%)
  waiting for transfers between devices  29 us (27%)
  local copies, waits for them, and re-layouts  8.22 us (8%)
    ppermute x3, waiting for transfers between devices, per_device(): weight_mine = [lax.ppermute(half, 'fsdp', x_shift(k)) for k in (1, 2, 3)]  14.4 us
    pallas_call x1, Pallas kernels, backward(): pl.pallas_call(backward_kernel, out_shape=[shape((TOK, HQ * HD)), shape((...  11.9 us
    pallas_call x1, Pallas kernels, forward(): pl.pallas_call(forward_kernel, out_shape=[shape((TOK, WIDTH)), shape((n,...  11.5 us
    all_to_all x1, starting transfers between devices, per_device(): lax.all_to_all(held[chosen], 'dp', split_axis=0, concat_axis=0, tiled=True)  9.92 us
    ppermute x3, starting transfers between devices, per_device(): lax.ppermute(parts[k], 'fsdp', x_shift(k))  5.64 us
    ppermute x1, starting transfers between devices, per_device(): grad_weight = lay_out(core1, own, lax.ppermute(own, 'dp', swap))  5.07 us
    ppermute x3, starting transfers between devices, per_device(): lax.ppermute(by_z[k], 'dp', dp_shift(0, k, 0))  4.81 us
    ppermute x3, waiting for transfers between devices, per_device(): by_z = {k: lax.ppermute(total, 'dp', dp_shift(0, k, 0)) for k in (1, 3, 2)}  4.72 us
  transfers between devices with their start and end apart: 21, of which 11 were waited for; matrix products, arithmetic and copies ran while one was open for 1% of the time, Pallas kernels for 16%

profile of v4, /device:TPU:1, one launch (start us, length us, event | category | flops | bytes accessed | tf_op | source)
XLA Modules:
  0.0 108.9 jit_solution(14798993394635185355)
XLA Ops:
  1.6 3.6 %gather_fusion = bf16[32,32,1024]{2,1,0:T(8,128)(2,1)} fusion(bf16[32,32,1024]{2,1,0:T(8,128)(2,1)} %bitcast.15, s32[1024]{0:T(1024)S(1)} %pad_clamp_fusion), kind=kCustom, calls=%fused_computation | custom fusion | bytes 4194432 | tf_op jit(solution)/shard_map/gather | solution.py:464
  5.2 9.9 %all-to-all-start = ((bf16[32,32,1024]{2,1,0:T(8,128)(2,1)}), bf16[32,32,1024]{2,1,0:T(8,128)(2,1)}, u32[]{:S(2)}, u32[]{:S(2)}) async-start(bf16[32,32,1024]{2,1,0:T(8,128)(2,1)} %gather_fusion), calls=%async_computation | async-start | bytes 4194304 | tf_op jit(solution)/shard_map/all_to_all | solution.py:464
  16.1 2.5 %collective-permute-start.2 = (bf16[192,768]{1,0:T(8,128)(2,1)S(1)}, bf16[192,768]{1,0:T(8,128)(2,1)S(1)}, u32[]{:S(2)}, u32[]{:S(2)}) collective-permute-start(bf16[192,768]{1,0:T(8,128)(2,1)S(1)} %constant_dynamic-slice_fusion), channel_id=1, source_target_pairs={{0,3},{1,0},{2,1},{3,2},{4,7},{5,4},{6,5},{7,6},{8,11},{9,8},{10,9... | collective-permute-start | bytes 884744 | tf_op jit(solution)/shard_map/ppermute | solution.py:467
  19.8 11.1 %collective-permute-done.2.refs_3_ = bf16[192,768]{1,0:T(8,128)(2,1)S(1)} collective-permute-done((bf16[192,768]{1,0:T(8,128)(2,1)S(1)}, bf16[192,768]{1,0:T(8,128)(2,1)S(1)}, u32[]{:S(2)}, u32[]{:S(2)}) %collective-permute-start.2) | collective-permute-done | bytes 294944 | tf_op jit(solution)/shard_map/ppermute | solution.py:467
  32.2 3.3 %collective-permute-done.refs_1_ = bf16[192,768]{1,0:T(8,128)(2,1)} collective-permute-done((bf16[192,768]{1,0:T(8,128)(2,1)S(1)}, bf16[192,768]{1,0:T(8,128)(2,1)}, u32[]{:S(2)}, u32[]{:S(2)}) %collective-permute-start) | collective-permute-done | bytes 294944 | tf_op jit(solution)/shard_map/ppermute | solution.py:467
  36.0 1.5 %collective-permute-done.3.refs_4_ = bf16[192,768]{1,0:T(8,128)(2,1)} collective-permute-done((bf16[192,768]{1,0:T(8,128)(2,1)}, bf16[192,768]{1,0:T(8,128)(2,1)}, u32[]{:S(2)}, u32[]{:S(2)}) %collective-permute-start.3) | collective-permute-done | bytes 294944 | tf_op jit(solution)/shard_map/ppermute | solution.py:468
  38.6 4.1 %d_attn.1._.dt = bf16[768,1024]{1,0:T(8,128)(2,1)S(1)} custom-call(s32[1]{0:T(128)} %bitcast.5.x_ref, s32[1]{0:T(128)} %bitcast.6.core_ref, bf16[192,1536]{1,0:T(8,128)(2,1)S(1)} %copy-done.4, bf16[192,768]{1,0:T(8,128)(2,1)} %collective-permute-done.refs_1_, bf16[192,768]{1,0:T(8,128)(2,1)} %collective-permute-done.1.refs_2_, ...), custom_call_target="tpu_custom_call" | custom-call | flops 2415919104 | bytes 8388608 | tf_op jit(solution)/shard_map/d_attn/pallas_call | solution.py:80
  43.9 11.5 %forward.1 = (bf16[1024,1024]{1,0:T(8,128)(2,1)}, bf16[768,1024]{1,0:T(8,128)(2,1)}, f32[8,1024]{1,0:T(8,128)}, bf16[768,768]{1,0:T(8,128)(2,1)}) custom-call(s32[1]{0:T(128)} %bitcast.group_ref, s32[32,32]{1,0:T(8,128)} %place_ref.1, bf16[32,32,1024]{2,1,0:T(8,128)(2,1)} %bitcast.16, bf16[32,32,1024]{2,1,0:T(8,128)(2,1)} %all-to-all-done.inc_ref, ...), custom_call_target="tpu_custom_call" | custom-call | flops 12000000000 | bytes 8388608 | tf_op jit(solution)/shard_map/forward/pallas_call | solution.py:200
  56.1 1.4 %copy-done.2 = bf16[768,1024]{1,0:T(8,128)(2,1)S(1)} copy-done((bf16[768,1024]{1,0:T(8,128)(2,1)S(1)}, bf16[768,1024]{1,0:T(8,128)(2,1)}, u32[]{:S(2)}) %copy-start.2) | copy-done | bytes 1572888
  57.5 1.5 %keep_half.1 = bf16[768,768]{1,0:T(8,128)(2,1)S(1)} custom-call(s32[1]{0:T(128)} %bitcast.6.core_ref, bf16[768,1024]{1,0:T(8,128)(2,1)S(1)} %copy-done.2, bf16[1024,1536]{1,0:T(8,128)(2,1)S(1)} %copy-done.1), custom_call_target="tpu_custom_call" | custom-call | flops 1207959552 | bytes 8388608 | tf_op jit(solution)/shard_map/keep_half/pallas_call | solution.py:232
  59.1 1.4 %add_pair.1 = (f32[192,768]{1,0:T(8,128)S(1)}, bf16[192,768]{1,0:T(8,128)(2,1)S(1)}, bf16[192,768]{1,0:T(8,128)(2,1)S(1)}, bf16[192,768]{1,0:T(8,128)(2,1)S(1)}, f32[8,128]{1,0:T(8,128)S(1)}) custom-call(s32[1]{0:T(128)} %bitcast.5.x_ref, bf16[4,192,768]{2,1,0:T(8,128)(2,1)S(1)} %bitcast.12, bf16[4,192,768]{2,1,0:T(8,128)(2,1)} %bitcast.8.got_hbm), custom_call_target="tpu_custom_call" | custom-call | flops 589824 | bytes 2949120 | tf_op jit(solution)/shard_map/add_pair/pallas_call | solution.py:345
  60.5 3.0 %collective-permute-start.7 = (bf16[192,768]{1,0:T(8,128)(2,1)S(1)}, bf16[192,768]{1,0:T(8,128)(2,1)S(1)}, u32[]{:S(2)}, u32[]{:S(2)}) collective-permute-start(bf16[192,768]{1,0:T(8,128)(2,1)S(1)} %get-tuple-element.28), channel_id=1, source_target_pairs={{0,2},{1,3},{2,0},{3,1},{4,6},{5,7},{6,4},{7,5},{8,10},{9,11},{10,... | collective-permute-start | bytes 884744 | tf_op jit(solution)/shard_map/ppermute | solution.py:475
  63.9 2.3 %collective-permute-start.9 = (bf16[192,768]{1,0:T(8,128)(2,1)S(1)}, bf16[192,768]{1,0:T(8,128)(2,1)S(1)}, u32[]{:S(2)}, u32[]{:S(2)}) collective-permute-start(bf16[192,768]{1,0:T(8,128)(2,1)S(1)} %get-tuple-element.30), channel_id=1, source_target_pairs={{0,3},{1,0},{2,1},{3,2},{4,7},{5,4},{6,5},{7,6},{8,11},{9,8},{10,9... | collective-permute-start | bytes 884744 | tf_op jit(solution)/shard_map/ppermute | solution.py:475
  66.2 11.9 %backward.1 = (bf16[1024,768]{1,0:T(8,128)(2,1)}, bf16[1024,256]{1,0:T(8,128)(2,1)}, f32[8,128]{1,0:T(8,128)S(1)}) custom-call(bf16[1024,1024]{1,0:T(8,128)(2,1)S(1)} %copy-done.8, s32[1,1024]{1,0:T(1,128)S(1)} %bitcast.14, bf16[768,1024]{1,0:T(8,128)(2,1)S(1)} %copy-done.7, bf16[768,1024]{1,0:T(8,128)(2,1)S(1)} %copy-done.3, f32[8,1024]{1,0:T(8,128)S(1)} %copy-done.9, ...), custom_call_target="tpu_custom_call" | custom-call | flops 30000001024 | bytes 8388608 | tf_op jit(solution)/shard_map/backward/pallas_call | solution.py:311
  78.5 2.1 %collective-permute-start.10 = (bf16[48,768]{1,0:T(8,128)(2,1)S(1)}, bf16[48,768]{1,0:T(8,128)(2,1)S(1)}, u32[]{:S(2)}, u32[]{:S(2)}) collective-permute-start(bf16[48,768]{1,0:T(8,128)(2,1)S(1)} %get-tuple-element.32), channel_id=1, source_target_pairs={{0,16},{4,20},{8,24},{12,28},{16,0},{20,4},{24,8},{28,12},{32,48},... | collective-permute-start | bytes 221192 | tf_op jit(solution)/shard_map/ppermute | solution.py:478
  80.9 2.4 %collective-permute-start.12 = (bf16[48,768]{1,0:T(8,128)(2,1)S(1)}, bf16[48,768]{1,0:T(8,128)(2,1)S(1)}, u32[]{:S(2)}, u32[]{:S(2)}) collective-permute-start(bf16[48,768]{1,0:T(8,128)(2,1)S(1)} %get-tuple-element.34), channel_id=1, source_target_pairs={{0,24},{4,28},{8,0},{12,4},{16,8},{20,12},{24,16},{28,20},{32,56},... | collective-permute-start | bytes 221192 | tf_op jit(solution)/shard_map/ppermute | solution.py:478
  83.3 2.8 %collective-permute-done.11.refs_2_ = bf16[48,768]{1,0:T(8,128)(2,1)S(1)} collective-permute-done((bf16[48,768]{1,0:T(8,128)(2,1)S(1)}, bf16[48,768]{1,0:T(8,128)(2,1)S(1)}, u32[]{:S(2)}, u32[]{:S(2)}) %collective-permute-start.11) | collective-permute-done | bytes 73760 | tf_op jit(solution)/shard_map/ppermute | solution.py:478
  86.1 1.7 %collective-permute-start.15 = (bf16[48,768]{1,0:T(8,128)(2,1)S(1)}, bf16[48,768]{1,0:T(8,128)(2,1)S(1)}, u32[]{:S(2)}, u32[]{:S(2)}) collective-permute-start(bf16[48,768]{1,0:T(8,128)(2,1)S(1)} %sum_four.2.refs_0_), channel_id=1, source_target_pairs={{0,64},{4,68},{8,72},{12,76},{16,80},{20,84},{24,88},{28,92},{32,9... | collective-permute-start | bytes 221192 | tf_op jit(solution)/shard_map/ppermute | solution.py:480
  89.3 1.6 %collective-permute-done.15.refs_3_ = bf16[48,768]{1,0:T(8,128)(2,1)S(1)} collective-permute-done((bf16[48,768]{1,0:T(8,128)(2,1)S(1)}, bf16[48,768]{1,0:T(8,128)(2,1)S(1)}, u32[]{:S(2)}, u32[]{:S(2)}) %collective-permute-start.15) | collective-permute-done | bytes 73760 | tf_op jit(solution)/shard_map/ppermute | solution.py:480
  91.0 2.5 %collective-permute-done.13.refs_1_ = bf16[48,768]{1,0:T(8,128)(2,1)S(1)} collective-permute-done((bf16[48,768]{1,0:T(8,128)(2,1)S(1)}, bf16[48,768]{1,0:T(8,128)(2,1)S(1)}, u32[]{:S(2)}, u32[]{:S(2)}) %collective-permute-start.13) | collective-permute-done | bytes 73760 | tf_op jit(solution)/shard_map/ppermute | solution.py:480
  93.6 2.5 %collective-permute-start.18 = (bf16[48,768]{1,0:T(8,128)(2,1)S(1)}, bf16[48,768]{1,0:T(8,128)(2,1)S(1)}, u32[]{:S(2)}, u32[]{:S(2)}) collective-permute-start(bf16[48,768]{1,0:T(8,128)(2,1)S(1)} %sum_four.3.refs_0_), channel_id=1, source_target_pairs={{0,24},{4,28},{8,0},{12,4},{16,8},{20,12},{24,16},{28,20},{32,56},... | collective-permute-start | bytes 221192 | tf_op jit(solution)/shard_map/ppermute | solution.py:483
  96.7 1.4 %collective-permute-done.18.refs_3_ = bf16[48,768]{1,0:T(8,128)(2,1)S(1)} collective-permute-done((bf16[48,768]{1,0:T(8,128)(2,1)S(1)}, bf16[48,768]{1,0:T(8,128)(2,1)S(1)}, u32[]{:S(2)}, u32[]{:S(2)}) %collective-permute-start.18) | collective-permute-done | bytes 73760 | tf_op jit(solution)/shard_map/ppermute | solution.py:483
  98.2 2.7 %collective-permute-done.17.refs_2_ = bf16[48,768]{1,0:T(8,128)(2,1)S(1)} collective-permute-done((bf16[48,768]{1,0:T(8,128)(2,1)S(1)}, bf16[48,768]{1,0:T(8,128)(2,1)S(1)}, u32[]{:S(2)}, u32[]{:S(2)}) %collective-permute-start.17) | collective-permute-done | bytes 73760 | tf_op jit(solution)/shard_map/ppermute | solution.py:483
  101.5 5.1 %collective-permute-start.19 = (bf16[192,768]{1,0:T(8,128)(2,1)S(1)}, bf16[192,768]{1,0:T(8,128)(2,1)S(1)}, u32[]{:S(2)}, u32[]{:S(2)}) collective-permute-start(bf16[192,768]{1,0:T(8,128)(2,1)S(1)} %join_z.1.own), channel_id=1, source_target_pairs={{0,4},{4,0},{8,12},{12,8},{16,20},{20,16},{24,28},{28,24},{32,36},... | collective-permute-start | bytes 884744 | tf_op jit(solution)/shard_map/ppermute | solution.py:485
  (54 shorter events, 14.0 us)
Async XLA Ops:
  5.2 32.4 %copy-start = (bf16[1024,1536]{1,0:T(8,128)(2,1)S(1)}, bf16[1024,1536]{1,0:T(8,128)(2,1)}, u32[]{:S(2)}) copy-start(bf16[1024,1536]{1,0:T(8,128)(2,1)} %dout_hbm.3) | copy-start | bytes 9437188
  5.2 38.7 %all-to-all-start = ((bf16[32,32,1024]{2,1,0:T(8,128)(2,1)}), bf16[32,32,1024]{2,1,0:T(8,128)(2,1)}, u32[]{:S(2)}, u32[]{:S(2)}) async-start(bf16[32,32,1024]{2,1,0:T(8,128)(2,1)} %gather_fusion), calls=%async_computation | async-start | bytes 4194304 | tf_op jit(solution)/shard_map/all_to_all | solution.py:464
  16.1 14.8 %collective-permute-start.2 = (bf16[192,768]{1,0:T(8,128)(2,1)S(1)}, bf16[192,768]{1,0:T(8,128)(2,1)S(1)}, u32[]{:S(2)}, u32[]{:S(2)}) collective-permute-start(bf16[192,768]{1,0:T(8,128)(2,1)S(1)} %constant_dynamic-slice_fusion), channel_id=1, source_target_pairs={{0,3},{1,0},{2,1},{3,2},{4,7},{5,4},{6,5},{7,6},{8,11},{9,8},{10,9... | collective-permute-start | bytes 884744 | tf_op jit(solution)/shard_map/ppermute | solution.py:467
  18.6 13.6 %collective-permute-start.1 = (bf16[192,768]{1,0:T(8,128)(2,1)S(1)}, bf16[192,768]{1,0:T(8,128)(2,1)}, u32[]{:S(2)}, u32[]{:S(2)}) collective-permute-start(bf16[192,768]{1,0:T(8,128)(2,1)S(1)} %constant_dynamic-slice_fusion), channel_id=1, source_target_pairs={{0,2},{1,3},{2,0},{3,1},{4,6},{5,7},{6,4},{7,5},{8,10},{9,11},{10,... | collective-permute-start | bytes 884744 | tf_op jit(solution)/shard_map/ppermute | solution.py:467
  19.2 16.3 %collective-permute-start = (bf16[192,768]{1,0:T(8,128)(2,1)S(1)}, bf16[192,768]{1,0:T(8,128)(2,1)}, u32[]{:S(2)}, u32[]{:S(2)}) collective-permute-start(bf16[192,768]{1,0:T(8,128)(2,1)S(1)} %constant_dynamic-slice_fusion), channel_id=1, source_target_pairs={{0,1},{1,2},{2,3},{3,0},{4,5},{5,6},{6,7},{7,4},{8,9},{9,10},{10,1... | collective-permute-start | bytes 884744 | tf_op jit(solution)/shard_map/ppermute | solution.py:467
  30.9 5.1 %collective-permute-start.5 = (bf16[192,768]{1,0:T(8,128)(2,1)S(1)}, bf16[192,768]{1,0:T(8,128)(2,1)}, u32[]{:S(2)}, u32[]{:S(2)}) collective-permute-start(bf16[192,768]{1,0:T(8,128)(2,1)S(1)} %collective-permute-done.2.refs_3_), channel_id=1, source_target_pairs={{0,4},{4,0},{8,12},{12,8},{16,20},{20,16},{24,28},{28,24},{32,36},... | collective-permute-start | bytes 884744 | tf_op jit(solution)/shard_map/ppermute | solution.py:468
  32.2 3.8 %collective-permute-start.4 = (bf16[192,768]{1,0:T(8,128)(2,1)}, bf16[192,768]{1,0:T(8,128)(2,1)}, u32[]{:S(2)}, u32[]{:S(2)}) collective-permute-start(bf16[192,768]{1,0:T(8,128)(2,1)} %collective-permute-done.1.refs_2_), channel_id=1, source_target_pairs={{0,4},{4,0},{8,12},{12,8},{16,20},{20,16},{24,28},{28,24},{32,36},... | collective-permute-start | bytes 884744 | tf_op jit(solution)/shard_map/ppermute | solution.py:468
  35.5 2.0 %collective-permute-start.3 = (bf16[192,768]{1,0:T(8,128)(2,1)}, bf16[192,768]{1,0:T(8,128)(2,1)}, u32[]{:S(2)}, u32[]{:S(2)}) collective-permute-start(bf16[192,768]{1,0:T(8,128)(2,1)} %collective-permute-done.refs_1_), channel_id=1, source_target_pairs={{0,4},{4,0},{8,12},{12,8},{16,20},{20,16},{24,28},{28,24},{32,36},... | collective-permute-start | bytes 884744 | tf_op jit(solution)/shard_map/ppermute | solution.py:468
  43.9 12.2 %copy-start.1 = (bf16[1024,1536]{1,0:T(8,128)(2,1)S(1)}, bf16[1024,1536]{1,0:T(8,128)(2,1)}, u32[]{:S(2)}) copy-start(bf16[1024,1536]{1,0:T(8,128)(2,1)} %dout_hbm.3) | copy-start | bytes 9437188
  55.4 3.6 %collective-permute-start.6 = (bf16[768,768]{1,0:T(8,128)(2,1)}, bf16[768,768]{1,0:T(8,128)(2,1)}, u32[]{:S(2)}, u32[]{:S(2)}) collective-permute-start(bf16[768,768]{1,0:T(8,128)(2,1)} %get-tuple-element.22), channel_id=1, source_target_pairs={{0,4},{4,0},{8,12},{12,8},{16,20},{20,16},{24,28},{28,24},{32,36},... | collective-permute-start | bytes 3538952 | tf_op jit(solution)/shard_map/ppermute | solution.py:474
  57.5 8.7 %copy-start.8 = (bf16[1024,1024]{1,0:T(8,128)(2,1)S(1)}, bf16[1024,1024]{1,0:T(8,128)(2,1)}, u32[]{:S(2)}) copy-start(bf16[1024,1024]{1,0:T(8,128)(2,1)} %get-tuple-element.19.rows) | copy-start | bytes 6291460
  60.5 17.6 %collective-permute-start.7 = (bf16[192,768]{1,0:T(8,128)(2,1)S(1)}, bf16[192,768]{1,0:T(8,128)(2,1)S(1)}, u32[]{:S(2)}, u32[]{:S(2)}) collective-permute-start(bf16[192,768]{1,0:T(8,128)(2,1)S(1)} %get-tuple-element.28), channel_id=1, source_target_pairs={{0,2},{1,3},{2,0},{3,1},{4,6},{5,7},{6,4},{7,5},{8,10},{9,11},{10,... | collective-permute-start | bytes 884744 | tf_op jit(solution)/shard_map/ppermute | solution.py:475
  63.5 14.7 %collective-permute-start.8 = (bf16[192,768]{1,0:T(8,128)(2,1)S(1)}, bf16[192,768]{1,0:T(8,128)(2,1)S(1)}, u32[]{:S(2)}, u32[]{:S(2)}) collective-permute-start(bf16[192,768]{1,0:T(8,128)(2,1)S(1)} %get-tuple-element.29), channel_id=1, source_target_pairs={{0,1},{1,2},{2,3},{3,0},{4,5},{5,6},{6,7},{7,4},{8,9},{9,10},{10,1... | collective-permute-start | bytes 884744 | tf_op jit(solution)/shard_map/ppermute | solution.py:475
  63.9 14.3 %collective-permute-start.9 = (bf16[192,768]{1,0:T(8,128)(2,1)S(1)}, bf16[192,768]{1,0:T(8,128)(2,1)S(1)}, u32[]{:S(2)}, u32[]{:S(2)}) collective-permute-start(bf16[192,768]{1,0:T(8,128)(2,1)S(1)} %get-tuple-element.30), channel_id=1, source_target_pairs={{0,3},{1,0},{2,1},{3,2},{4,7},{5,4},{6,5},{7,6},{8,11},{9,8},{10,9... | collective-permute-start | bytes 884744 | tf_op jit(solution)/shard_map/ppermute | solution.py:475
  78.5 4.8 %collective-permute-start.10 = (bf16[48,768]{1,0:T(8,128)(2,1)S(1)}, bf16[48,768]{1,0:T(8,128)(2,1)S(1)}, u32[]{:S(2)}, u32[]{:S(2)}) collective-permute-start(bf16[48,768]{1,0:T(8,128)(2,1)S(1)} %get-tuple-element.32), channel_id=1, source_target_pairs={{0,16},{4,20},{8,24},{12,28},{16,0},{20,4},{24,8},{28,12},{32,48},... | collective-permute-start | bytes 221192 | tf_op jit(solution)/shard_map/ppermute | solution.py:478
  80.6 5.5 %collective-permute-start.11 = (bf16[48,768]{1,0:T(8,128)(2,1)S(1)}, bf16[48,768]{1,0:T(8,128)(2,1)S(1)}, u32[]{:S(2)}, u32[]{:S(2)}) collective-permute-start(bf16[48,768]{1,0:T(8,128)(2,1)S(1)} %get-tuple-element.33), channel_id=1, source_target_pairs={{0,8},{4,12},{8,16},{12,20},{16,24},{20,28},{24,0},{28,4},{32,40},... | collective-permute-start | bytes 221192 | tf_op jit(solution)/shard_map/ppermute | solution.py:478
  80.9 5.2 %collective-permute-start.12 = (bf16[48,768]{1,0:T(8,128)(2,1)S(1)}, bf16[48,768]{1,0:T(8,128)(2,1)S(1)}, u32[]{:S(2)}, u32[]{:S(2)}) collective-permute-start(bf16[48,768]{1,0:T(8,128)(2,1)S(1)} %get-tuple-element.34), channel_id=1, source_target_pairs={{0,24},{4,28},{8,0},{12,4},{16,8},{20,12},{24,16},{28,20},{32,56},... | collective-permute-start | bytes 221192 | tf_op jit(solution)/shard_map/ppermute | solution.py:478
  86.1 4.8 %collective-permute-start.15 = (bf16[48,768]{1,0:T(8,128)(2,1)S(1)}, bf16[48,768]{1,0:T(8,128)(2,1)S(1)}, u32[]{:S(2)}, u32[]{:S(2)}) collective-permute-start(bf16[48,768]{1,0:T(8,128)(2,1)S(1)} %sum_four.2.refs_0_), channel_id=1, source_target_pairs={{0,64},{4,68},{8,72},{12,76},{16,80},{20,84},{24,88},{28,92},{32,9... | collective-permute-start | bytes 221192 | tf_op jit(solution)/shard_map/ppermute | solution.py:480
  87.8 3.2 %collective-permute-start.14 = (bf16[48,768]{1,0:T(8,128)(2,1)S(1)}, bf16[48,768]{1,0:T(8,128)(2,1)S(1)}, u32[]{:S(2)}, u32[]{:S(2)}) collective-permute-start(bf16[48,768]{1,0:T(8,128)(2,1)S(1)} %sum_four.2.refs_0_), channel_id=1, source_target_pairs={{0,96},{4,100},{8,104},{12,108},{16,112},{20,116},{24,120},{28,124... | collective-permute-start | bytes 221192 | tf_op jit(solution)/shard_map/ppermute | solution.py:480
  88.7 4.8 %collective-permute-start.13 = (bf16[48,768]{1,0:T(8,128)(2,1)S(1)}, bf16[48,768]{1,0:T(8,128)(2,1)S(1)}, u32[]{:S(2)}, u32[]{:S(2)}) collective-permute-start(bf16[48,768]{1,0:T(8,128)(2,1)S(1)} %sum_four.2.refs_0_), channel_id=1, source_target_pairs={{0,32},{4,36},{8,40},{12,44},{16,48},{20,52},{24,56},{28,60},{32,6... | collective-permute-start | bytes 221192 | tf_op jit(solution)/shard_map/ppermute | solution.py:480
  93.6 4.6 %collective-permute-start.18 = (bf16[48,768]{1,0:T(8,128)(2,1)S(1)}, bf16[48,768]{1,0:T(8,128)(2,1)S(1)}, u32[]{:S(2)}, u32[]{:S(2)}) collective-permute-start(bf16[48,768]{1,0:T(8,128)(2,1)S(1)} %sum_four.3.refs_0_), channel_id=1, source_target_pairs={{0,24},{4,28},{8,0},{12,4},{16,8},{20,12},{24,16},{28,20},{32,56},... | collective-permute-start | bytes 221192 | tf_op jit(solution)/shard_map/ppermute | solution.py:483
  96.1 4.8 %collective-permute-start.17 = (bf16[48,768]{1,0:T(8,128)(2,1)S(1)}, bf16[48,768]{1,0:T(8,128)(2,1)S(1)}, u32[]{:S(2)}, u32[]{:S(2)}) collective-permute-start(bf16[48,768]{1,0:T(8,128)(2,1)S(1)} %sum_four.3.refs_0_), channel_id=1, source_target_pairs={{0,16},{4,20},{8,24},{12,28},{16,0},{20,4},{24,8},{28,12},{32,48},... | collective-permute-start | bytes 221192 | tf_op jit(solution)/shard_map/ppermute | solution.py:483
  96.3 5.2 %collective-permute-start.16 = (bf16[48,768]{1,0:T(8,128)(2,1)S(1)}, bf16[48,768]{1,0:T(8,128)(2,1)S(1)}, u32[]{:S(2)}, u32[]{:S(2)}) collective-permute-start(bf16[48,768]{1,0:T(8,128)(2,1)S(1)} %sum_four.3.refs_0_), channel_id=1, source_target_pairs={{0,8},{4,12},{8,16},{12,20},{16,24},{20,28},{24,0},{28,4},{32,40},... | collective-permute-start | bytes 221192 | tf_op jit(solution)/shard_map/ppermute | solution.py:483
  101.5 6.3 %collective-permute-start.19 = (bf16[192,768]{1,0:T(8,128)(2,1)S(1)}, bf16[192,768]{1,0:T(8,128)(2,1)S(1)}, u32[]{:S(2)}, u32[]{:S(2)}) collective-permute-start(bf16[192,768]{1,0:T(8,128)(2,1)S(1)} %join_z.1.own), channel_id=1, source_target_pairs={{0,4},{4,0},{8,12},{12,8},{16,20},{20,16},{24,28},{28,24},{32,36},... | collective-permute-start | bytes 884744 | tf_op jit(solution)/shard_map/ppermute | solution.py:485
  (7 other events, 33.7 us)

commit v5 on v4

--- a/solution.py
+++ b/solution.py
@@ -456,12 +456,12 @@
     z = lax.rem(group // 2, 4)
     held = stash.reshape(NB, BLK, WIDTH)
     peers = jnp.arange(NB, dtype=jnp.int32)
-    holder = stash_place // NB
-    slot = stash_place % NB
+    holder = lax.shift_right_logical(stash_place, 5)
+    slot = stash_place - holder * NB
     chosen = jnp.sum(jnp.where((holder == group) & (peers[:, None] != group), slot, 0), axis=1)
     x1, z1, core1 = x.reshape(1), z.reshape(1), core.reshape(1)
 
-    incoming = lax.all_to_all(held[chosen], "dp", split_axis=0, concat_axis=0, tiled=True)
+    incoming = lax.all_to_all(held.at[chosen].get(mode="promise_in_bounds"), "dp", split_axis=0, concat_axis=0, tiled=True)
     swap = dp_shift(0, 0, 1)
     half = lax.dynamic_slice_in_dim(out_weight, core * HALF, HALF, 1)
     weight_mine = [lax.ppermute(half, "fsdp", x_shift(k)) for k in (1, 2, 3)]

time: 109 us -> 109 us (level)
  no operation moved by 1% of the time
where the time goes in v5:
time: 109 us
  starting transfers between devices  37.9 us (35%)
  Pallas kernels  32 us (29%)
  waiting for transfers between devices  29 us (27%)
  local copies, waits for them, and re-layouts  8.22 us (8%)
    ppermute x3, waiting for transfers between devices, per_device(): weight_mine = [lax.ppermute(half, 'fsdp', x_shift(k)) for k in (1, 2, 3)]  14.4 us
    pallas_call x1, Pallas kernels, backward(): pl.pallas_call(backward_kernel, out_shape=[shape((TOK, HQ * HD)), shape((...  11.9 us
    pallas_call x1, Pallas kernels, forward(): pl.pallas_call(forward_kernel, out_shape=[shape((TOK, WIDTH)), shape((n,...  11.5 us
    all_to_all x1, starting transfers between devices, per_device(): lax.all_to_all(held.at[chosen].get(mode='promise_in_bounds'), 'dp', split...  9.92 us
    ppermute x3, starting transfers between devices, per_device(): lax.ppermute(parts[k], 'fsdp', x_shift(k))  5.64 us
    ppermute x1, starting transfers between devices, per_device(): grad_weight = lay_out(core1, own, lax.ppermute(own, 'dp', swap))  5.07 us
    ppermute x3, starting transfers between devices, per_device(): lax.ppermute(by_z[k], 'dp', dp_shift(0, k, 0))  4.81 us
    ppermute x3, waiting for transfers between devices, per_device(): by_z = {k: lax.ppermute(total, 'dp', dp_shift(0, k, 0)) for k in (1, 3, 2)}  4.72 us
  transfers between devices with their start and end apart: 21, of which 11 were waited for; matrix products, arithmetic and copies ran while one was open for 1% of the time, Pallas kernels for 16%

profile of v5, /device:TPU:1, one launch (start us, length us, event | category | flops | bytes accessed | tf_op | source)
XLA Modules:
  0.0 108.9 jit_solution(13609437536539503953)
XLA Ops:
  1.6 3.6 %gather_fusion = bf16[32,32,1024]{2,1,0:T(8,128)(2,1)} fusion(bf16[32,32,1024]{2,1,0:T(8,128)(2,1)} %bitcast.15, s32[1024]{0:T(1024)S(1)} %pad_clamp_fusion), kind=kCustom, calls=%fused_computation | custom fusion | bytes 4194432 | tf_op jit(solution)/shard_map/gather | solution.py:464
  5.2 9.9 %all-to-all-start = ((bf16[32,32,1024]{2,1,0:T(8,128)(2,1)}), bf16[32,32,1024]{2,1,0:T(8,128)(2,1)}, u32[]{:S(2)}, u32[]{:S(2)}) async-start(bf16[32,32,1024]{2,1,0:T(8,128)(2,1)} %gather_fusion), calls=%async_computation | async-start | bytes 4194304 | tf_op jit(solution)/shard_map/all_to_all | solution.py:464
  16.1 2.5 %collective-permute-start.2 = (bf16[192,768]{1,0:T(8,128)(2,1)S(1)}, bf16[192,768]{1,0:T(8,128)(2,1)S(1)}, u32[]{:S(2)}, u32[]{:S(2)}) collective-permute-start(bf16[192,768]{1,0:T(8,128)(2,1)S(1)} %constant_dynamic-slice_fusion), channel_id=1, source_target_pairs={{0,3},{1,0},{2,1},{3,2},{4,7},{5,4},{6,5},{7,6},{8,11},{9,8},{10,9... | collective-permute-start | bytes 884744 | tf_op jit(solution)/shard_map/ppermute | solution.py:467
  19.8 11.1 %collective-permute-done.2.refs_3_ = bf16[192,768]{1,0:T(8,128)(2,1)S(1)} collective-permute-done((bf16[192,768]{1,0:T(8,128)(2,1)S(1)}, bf16[192,768]{1,0:T(8,128)(2,1)S(1)}, u32[]{:S(2)}, u32[]{:S(2)}) %collective-permute-start.2) | collective-permute-done | bytes 294944 | tf_op jit(solution)/shard_map/ppermute | solution.py:467
  32.2 3.3 %collective-permute-done.refs_1_ = bf16[192,768]{1,0:T(8,128)(2,1)} collective-permute-done((bf16[192,768]{1,0:T(8,128)(2,1)S(1)}, bf16[192,768]{1,0:T(8,128)(2,1)}, u32[]{:S(2)}, u32[]{:S(2)}) %collective-permute-start) | collective-permute-done | bytes 294944 | tf_op jit(solution)/shard_map/ppermute | solution.py:467
  36.0 1.5 %collective-permute-done.3.refs_4_ = bf16[192,768]{1,0:T(8,128)(2,1)} collective-permute-done((bf16[192,768]{1,0:T(8,128)(2,1)}, bf16[192,768]{1,0:T(8,128)(2,1)}, u32[]{:S(2)}, u32[]{:S(2)}) %collective-permute-start.3) | collective-permute-done | bytes 294944 | tf_op jit(solution)/shard_map/ppermute | solution.py:468
  38.6 4.1 %d_attn.1._.dt = bf16[768,1024]{1,0:T(8,128)(2,1)S(1)} custom-call(s32[1]{0:T(128)} %bitcast.5.x_ref, s32[1]{0:T(128)} %bitcast.6.core_ref, bf16[192,1536]{1,0:T(8,128)(2,1)S(1)} %copy-done.4, bf16[192,768]{1,0:T(8,128)(2,1)} %collective-permute-done.refs_1_, bf16[192,768]{1,0:T(8,128)(2,1)} %collective-permute-done.1.refs_2_, ...), custom_call_target="tpu_custom_call" | custom-call | flops 2415919104 | bytes 8388608 | tf_op jit(solution)/shard_map/d_attn/pallas_call | solution.py:80
  43.9 11.5 %forward.1 = (bf16[1024,1024]{1,0:T(8,128)(2,1)}, bf16[768,1024]{1,0:T(8,128)(2,1)}, f32[8,1024]{1,0:T(8,128)}, bf16[768,768]{1,0:T(8,128)(2,1)}) custom-call(s32[1]{0:T(128)} %bitcast.group_ref, s32[32,32]{1,0:T(8,128)} %place_ref.1, bf16[32,32,1024]{2,1,0:T(8,128)(2,1)} %bitcast.16, bf16[32,32,1024]{2,1,0:T(8,128)(2,1)} %all-to-all-done.inc_ref, ...), custom_call_target="tpu_custom_call" | custom-call | flops 12000000000 | bytes 8388608 | tf_op jit(solution)/shard_map/forward/pallas_call | solution.py:200
  56.1 1.4 %copy-done.2 = bf16[768,1024]{1,0:T(8,128)(2,1)S(1)} copy-done((bf16[768,1024]{1,0:T(8,128)(2,1)S(1)}, bf16[768,1024]{1,0:T(8,128)(2,1)}, u32[]{:S(2)}) %copy-start.2) | copy-done | bytes 1572888
  57.5 1.5 %keep_half.1 = bf16[768,768]{1,0:T(8,128)(2,1)S(1)} custom-call(s32[1]{0:T(128)} %bitcast.6.core_ref, bf16[768,1024]{1,0:T(8,128)(2,1)S(1)} %copy-done.2, bf16[1024,1536]{1,0:T(8,128)(2,1)S(1)} %copy-done.1), custom_call_target="tpu_custom_call" | custom-call | flops 1207959552 | bytes 8388608 | tf_op jit(solution)/shard_map/keep_half/pallas_call | solution.py:232
  59.1 1.4 %add_pair.1 = (f32[192,768]{1,0:T(8,128)S(1)}, bf16[192,768]{1,0:T(8,128)(2,1)S(1)}, bf16[192,768]{1,0:T(8,128)(2,1)S(1)}, bf16[192,768]{1,0:T(8,128)(2,1)S(1)}, f32[8,128]{1,0:T(8,128)S(1)}) custom-call(s32[1]{0:T(128)} %bitcast.5.x_ref, bf16[4,192,768]{2,1,0:T(8,128)(2,1)S(1)} %bitcast.12, bf16[4,192,768]{2,1,0:T(8,128)(2,1)} %bitcast.8.got_hbm), custom_call_target="tpu_custom_call" | custom-call | flops 589824 | bytes 2949120 | tf_op jit(solution)/shard_map/add_pair/pallas_call | solution.py:345
  60.5 3.0 %collective-permute-start.7 = (bf16[192,768]{1,0:T(8,128)(2,1)S(1)}, bf16[192,768]{1,0:T(8,128)(2,1)S(1)}, u32[]{:S(2)}, u32[]{:S(2)}) collective-permute-start(bf16[192,768]{1,0:T(8,128)(2,1)S(1)} %get-tuple-element.28), channel_id=1, source_target_pairs={{0,2},{1,3},{2,0},{3,1},{4,6},{5,7},{6,4},{7,5},{8,10},{9,11},{10,... | collective-permute-start | bytes 884744 | tf_op jit(solution)/shard_map/ppermute | solution.py:475
  63.9 2.3 %collective-permute-start.9 = (bf16[192,768]{1,0:T(8,128)(2,1)S(1)}, bf16[192,768]{1,0:T(8,128)(2,1)S(1)}, u32[]{:S(2)}, u32[]{:S(2)}) collective-permute-start(bf16[192,768]{1,0:T(8,128)(2,1)S(1)} %get-tuple-element.30), channel_id=1, source_target_pairs={{0,3},{1,0},{2,1},{3,2},{4,7},{5,4},{6,5},{7,6},{8,11},{9,8},{10,9... | collective-permute-start | bytes 884744 | tf_op jit(solution)/shard_map/ppermute | solution.py:475
  66.2 11.9 %backward.1 = (bf16[1024,768]{1,0:T(8,128)(2,1)}, bf16[1024,256]{1,0:T(8,128)(2,1)}, f32[8,128]{1,0:T(8,128)S(1)}) custom-call(bf16[1024,1024]{1,0:T(8,128)(2,1)S(1)} %copy-done.8, s32[1,1024]{1,0:T(1,128)S(1)} %bitcast.14, bf16[768,1024]{1,0:T(8,128)(2,1)S(1)} %copy-done.7, bf16[768,1024]{1,0:T(8,128)(2,1)S(1)} %copy-done.3, f32[8,1024]{1,0:T(8,128)S(1)} %copy-done.9, ...), custom_call_target="tpu_custom_call" | custom-call | flops 30000001024 | bytes 8388608 | tf_op jit(solution)/shard_map/backward/pallas_call | solution.py:311
  78.5 2.1 %collective-permute-start.10 = (bf16[48,768]{1,0:T(8,128)(2,1)S(1)}, bf16[48,768]{1,0:T(8,128)(2,1)S(1)}, u32[]{:S(2)}, u32[]{:S(2)}) collective-permute-start(bf16[48,768]{1,0:T(8,128)(2,1)S(1)} %get-tuple-element.32), channel_id=1, source_target_pairs={{0,16},{4,20},{8,24},{12,28},{16,0},{20,4},{24,8},{28,12},{32,48},... | collective-permute-start | bytes 221192 | tf_op jit(solution)/shard_map/ppermute | solution.py:478
  80.9 2.4 %collective-permute-start.12 = (bf16[48,768]{1,0:T(8,128)(2,1)S(1)}, bf16[48,768]{1,0:T(8,128)(2,1)S(1)}, u32[]{:S(2)}, u32[]{:S(2)}) collective-permute-start(bf16[48,768]{1,0:T(8,128)(2,1)S(1)} %get-tuple-element.34), channel_id=1, source_target_pairs={{0,24},{4,28},{8,0},{12,4},{16,8},{20,12},{24,16},{28,20},{32,56},... | collective-permute-start | bytes 221192 | tf_op jit(solution)/shard_map/ppermute | solution.py:478
  83.3 2.8 %collective-permute-done.11.refs_2_ = bf16[48,768]{1,0:T(8,128)(2,1)S(1)} collective-permute-done((bf16[48,768]{1,0:T(8,128)(2,1)S(1)}, bf16[48,768]{1,0:T(8,128)(2,1)S(1)}, u32[]{:S(2)}, u32[]{:S(2)}) %collective-permute-start.11) | collective-permute-done | bytes 73760 | tf_op jit(solution)/shard_map/ppermute | solution.py:478
  86.1 1.7 %collective-permute-start.15 = (bf16[48,768]{1,0:T(8,128)(2,1)S(1)}, bf16[48,768]{1,0:T(8,128)(2,1)S(1)}, u32[]{:S(2)}, u32[]{:S(2)}) collective-permute-start(bf16[48,768]{1,0:T(8,128)(2,1)S(1)} %sum_four.2.refs_0_), channel_id=1, source_target_pairs={{0,64},{4,68},{8,72},{12,76},{16,80},{20,84},{24,88},{28,92},{32,9... | collective-permute-start | bytes 221192 | tf_op jit(solution)/shard_map/ppermute | solution.py:480
  89.3 1.6 %collective-permute-done.15.refs_3_ = bf16[48,768]{1,0:T(8,128)(2,1)S(1)} collective-permute-done((bf16[48,768]{1,0:T(8,128)(2,1)S(1)}, bf16[48,768]{1,0:T(8,128)(2,1)S(1)}, u32[]{:S(2)}, u32[]{:S(2)}) %collective-permute-start.15) | collective-permute-done | bytes 73760 | tf_op jit(solution)/shard_map/ppermute | solution.py:480
  91.0 2.5 %collective-permute-done.13.refs_1_ = bf16[48,768]{1,0:T(8,128)(2,1)S(1)} collective-permute-done((bf16[48,768]{1,0:T(8,128)(2,1)S(1)}, bf16[48,768]{1,0:T(8,128)(2,1)S(1)}, u32[]{:S(2)}, u32[]{:S(2)}) %collective-permute-start.13) | collective-permute-done | bytes 73760 | tf_op jit(solution)/shard_map/ppermute | solution.py:480
  93.6 2.5 %collective-permute-start.18 = (bf16[48,768]{1,0:T(8,128)(2,1)S(1)}, bf16[48,768]{1,0:T(8,128)(2,1)S(1)}, u32[]{:S(2)}, u32[]{:S(2)}) collective-permute-start(bf16[48,768]{1,0:T(8,128)(2,1)S(1)} %sum_four.3.refs_0_), channel_id=1, source_target_pairs={{0,24},{4,28},{8,0},{12,4},{16,8},{20,12},{24,16},{28,20},{32,56},... | collective-permute-start | bytes 221192 | tf_op jit(solution)/shard_map/ppermute | solution.py:483
  96.7 1.4 %collective-permute-done.18.refs_3_ = bf16[48,768]{1,0:T(8,128)(2,1)S(1)} collective-permute-done((bf16[48,768]{1,0:T(8,128)(2,1)S(1)}, bf16[48,768]{1,0:T(8,128)(2,1)S(1)}, u32[]{:S(2)}, u32[]{:S(2)}) %collective-permute-start.18) | collective-permute-done | bytes 73760 | tf_op jit(solution)/shard_map/ppermute | solution.py:483
  98.2 2.7 %collective-permute-done.17.refs_2_ = bf16[48,768]{1,0:T(8,128)(2,1)S(1)} collective-permute-done((bf16[48,768]{1,0:T(8,128)(2,1)S(1)}, bf16[48,768]{1,0:T(8,128)(2,1)S(1)}, u32[]{:S(2)}, u32[]{:S(2)}) %collective-permute-start.17) | collective-permute-done | bytes 73760 | tf_op jit(solution)/shard_map/ppermute | solution.py:483
  101.5 5.1 %collective-permute-start.19 = (bf16[192,768]{1,0:T(8,128)(2,1)S(1)}, bf16[192,768]{1,0:T(8,128)(2,1)S(1)}, u32[]{:S(2)}, u32[]{:S(2)}) collective-permute-start(bf16[192,768]{1,0:T(8,128)(2,1)S(1)} %join_z.1.own), channel_id=1, source_target_pairs={{0,4},{4,0},{8,12},{12,8},{16,20},{20,16},{24,28},{28,24},{32,36},... | collective-permute-start | bytes 884744 | tf_op jit(solution)/shard_map/ppermute | solution.py:485
  (54 shorter events, 14.0 us)
Async XLA Ops:
  5.2 32.4 %copy-start = (bf16[1024,1536]{1,0:T(8,128)(2,1)S(1)}, bf16[1024,1536]{1,0:T(8,128)(2,1)}, u32[]{:S(2)}) copy-start(bf16[1024,1536]{1,0:T(8,128)(2,1)} %dout_hbm.3) | copy-start | bytes 9437188
  5.2 38.7 %all-to-all-start = ((bf16[32,32,1024]{2,1,0:T(8,128)(2,1)}), bf16[32,32,1024]{2,1,0:T(8,128)(2,1)}, u32[]{:S(2)}, u32[]{:S(2)}) async-start(bf16[32,32,1024]{2,1,0:T(8,128)(2,1)} %gather_fusion), calls=%async_computation | async-start | bytes 4194304 | tf_op jit(solution)/shard_map/all_to_all | solution.py:464
  16.1 14.8 %collective-permute-start.2 = (bf16[192,768]{1,0:T(8,128)(2,1)S(1)}, bf16[192,768]{1,0:T(8,128)(2,1)S(1)}, u32[]{:S(2)}, u32[]{:S(2)}) collective-permute-start(bf16[192,768]{1,0:T(8,128)(2,1)S(1)} %constant_dynamic-slice_fusion), channel_id=1, source_target_pairs={{0,3},{1,0},{2,1},{3,2},{4,7},{5,4},{6,5},{7,6},{8,11},{9,8},{10,9... | collective-permute-start | bytes 884744 | tf_op jit(solution)/shard_map/ppermute | solution.py:467
  18.6 13.6 %collective-permute-start.1 = (bf16[192,768]{1,0:T(8,128)(2,1)S(1)}, bf16[192,768]{1,0:T(8,128)(2,1)}, u32[]{:S(2)}, u32[]{:S(2)}) collective-permute-start(bf16[192,768]{1,0:T(8,128)(2,1)S(1)} %constant_dynamic-slice_fusion), channel_id=1, source_target_pairs={{0,2},{1,3},{2,0},{3,1},{4,6},{5,7},{6,4},{7,5},{8,10},{9,11},{10,... | collective-permute-start | bytes 884744 | tf_op jit(solution)/shard_map/ppermute | solution.py:467
  19.2 16.3 %collective-permute-start = (bf16[192,768]{1,0:T(8,128)(2,1)S(1)}, bf16[192,768]{1,0:T(8,128)(2,1)}, u32[]{:S(2)}, u32[]{:S(2)}) collective-permute-start(bf16[192,768]{1,0:T(8,128)(2,1)S(1)} %constant_dynamic-slice_fusion), channel_id=1, source_target_pairs={{0,1},{1,2},{2,3},{3,0},{4,5},{5,6},{6,7},{7,4},{8,9},{9,10},{10,1... | collective-permute-start | bytes 884744 | tf_op jit(solution)/shard_map/ppermute | solution.py:467
  30.9 5.1 %collective-permute-start.5 = (bf16[192,768]{1,0:T(8,128)(2,1)S(1)}, bf16[192,768]{1,0:T(8,128)(2,1)}, u32[]{:S(2)}, u32[]{:S(2)}) collective-permute-start(bf16[192,768]{1,0:T(8,128)(2,1)S(1)} %collective-permute-done.2.refs_3_), channel_id=1, source_target_pairs={{0,4},{4,0},{8,12},{12,8},{16,20},{20,16},{24,28},{28,24},{32,36},... | collective-permute-start | bytes 884744 | tf_op jit(solution)/shard_map/ppermute | solution.py:468
  32.2 3.8 %collective-permute-start.4 = (bf16[192,768]{1,0:T(8,128)(2,1)}, bf16[192,768]{1,0:T(8,128)(2,1)}, u32[]{:S(2)}, u32[]{:S(2)}) collective-permute-start(bf16[192,768]{1,0:T(8,128)(2,1)} %collective-permute-done.1.refs_2_), channel_id=1, source_target_pairs={{0,4},{4,0},{8,12},{12,8},{16,20},{20,16},{24,28},{28,24},{32,36},... | collective-permute-start | bytes 884744 | tf_op jit(solution)/shard_map/ppermute | solution.py:468
  35.5 2.0 %collective-permute-start.3 = (bf16[192,768]{1,0:T(8,128)(2,1)}, bf16[192,768]{1,0:T(8,128)(2,1)}, u32[]{:S(2)}, u32[]{:S(2)}) collective-permute-start(bf16[192,768]{1,0:T(8,128)(2,1)} %collective-permute-done.refs_1_), channel_id=1, source_target_pairs={{0,4},{4,0},{8,12},{12,8},{16,20},{20,16},{24,28},{28,24},{32,36},... | collective-permute-start | bytes 884744 | tf_op jit(solution)/shard_map/ppermute | solution.py:468
  43.9 12.2 %copy-start.1 = (bf16[1024,1536]{1,0:T(8,128)(2,1)S(1)}, bf16[1024,1536]{1,0:T(8,128)(2,1)}, u32[]{:S(2)}) copy-start(bf16[1024,1536]{1,0:T(8,128)(2,1)} %dout_hbm.3) | copy-start | bytes 9437188
  55.4 3.6 %collective-permute-start.6 = (bf16[768,768]{1,0:T(8,128)(2,1)}, bf16[768,768]{1,0:T(8,128)(2,1)}, u32[]{:S(2)}, u32[]{:S(2)}) collective-permute-start(bf16[768,768]{1,0:T(8,128)(2,1)} %get-tuple-element.22), channel_id=1, source_target_pairs={{0,4},{4,0},{8,12},{12,8},{16,20},{20,16},{24,28},{28,24},{32,36},... | collective-permute-start | bytes 3538952 | tf_op jit(solution)/shard_map/ppermute | solution.py:474
  57.5 8.7 %copy-start.8 = (bf16[1024,1024]{1,0:T(8,128)(2,1)S(1)}, bf16[1024,1024]{1,0:T(8,128)(2,1)}, u32[]{:S(2)}) copy-start(bf16[1024,1024]{1,0:T(8,128)(2,1)} %get-tuple-element.19.rows) | copy-start | bytes 6291460
  60.5 17.6 %collective-permute-start.7 = (bf16[192,768]{1,0:T(8,128)(2,1)S(1)}, bf16[192,768]{1,0:T(8,128)(2,1)S(1)}, u32[]{:S(2)}, u32[]{:S(2)}) collective-permute-start(bf16[192,768]{1,0:T(8,128)(2,1)S(1)} %get-tuple-element.28), channel_id=1, source_target_pairs={{0,2},{1,3},{2,0},{3,1},{4,6},{5,7},{6,4},{7,5},{8,10},{9,11},{10,... | collective-permute-start | bytes 884744 | tf_op jit(solution)/shard_map/ppermute | solution.py:475
  63.5 14.7 %collective-permute-start.8 = (bf16[192,768]{1,0:T(8,128)(2,1)S(1)}, bf16[192,768]{1,0:T(8,128)(2,1)S(1)}, u32[]{:S(2)}, u32[]{:S(2)}) collective-permute-start(bf16[192,768]{1,0:T(8,128)(2,1)S(1)} %get-tuple-element.29), channel_id=1, source_target_pairs={{0,1},{1,2},{2,3},{3,0},{4,5},{5,6},{6,7},{7,4},{8,9},{9,10},{10,1... | collective-permute-start | bytes 884744 | tf_op jit(solution)/shard_map/ppermute | solution.py:475
  63.9 14.3 %collective-permute-start.9 = (bf16[192,768]{1,0:T(8,128)(2,1)S(1)}, bf16[192,768]{1,0:T(8,128)(2,1)S(1)}, u32[]{:S(2)}, u32[]{:S(2)}) collective-permute-start(bf16[192,768]{1,0:T(8,128)(2,1)S(1)} %get-tuple-element.30), channel_id=1, source_target_pairs={{0,3},{1,0},{2,1},{3,2},{4,7},{5,4},{6,5},{7,6},{8,11},{9,8},{10,9... | collective-permute-start | bytes 884744 | tf_op jit(solution)/shard_map/ppermute | solution.py:475
  78.5 4.8 %collective-permute-start.10 = (bf16[48,768]{1,0:T(8,128)(2,1)S(1)}, bf16[48,768]{1,0:T(8,128)(2,1)S(1)}, u32[]{:S(2)}, u32[]{:S(2)}) collective-permute-start(bf16[48,768]{1,0:T(8,128)(2,1)S(1)} %get-tuple-element.32), channel_id=1, source_target_pairs={{0,16},{4,20},{8,24},{12,28},{16,0},{20,4},{24,8},{28,12},{32,48},... | collective-permute-start | bytes 221192 | tf_op jit(solution)/shard_map/ppermute | solution.py:478
  80.6 5.5 %collective-permute-start.11 = (bf16[48,768]{1,0:T(8,128)(2,1)S(1)}, bf16[48,768]{1,0:T(8,128)(2,1)S(1)}, u32[]{:S(2)}, u32[]{:S(2)}) collective-permute-start(bf16[48,768]{1,0:T(8,128)(2,1)S(1)} %get-tuple-element.33), channel_id=1, source_target_pairs={{0,8},{4,12},{8,16},{12,20},{16,24},{20,28},{24,0},{28,4},{32,40},... | collective-permute-start | bytes 221192 | tf_op jit(solution)/shard_map/ppermute | solution.py:478
  80.9 5.2 %collective-permute-start.12 = (bf16[48,768]{1,0:T(8,128)(2,1)S(1)}, bf16[48,768]{1,0:T(8,128)(2,1)S(1)}, u32[]{:S(2)}, u32[]{:S(2)}) collective-permute-start(bf16[48,768]{1,0:T(8,128)(2,1)S(1)} %get-tuple-element.34), channel_id=1, source_target_pairs={{0,24},{4,28},{8,0},{12,4},{16,8},{20,12},{24,16},{28,20},{32,56},... | collective-permute-start | bytes 221192 | tf_op jit(solution)/shard_map/ppermute | solution.py:478
  86.1 4.8 %collective-permute-start.15 = (bf16[48,768]{1,0:T(8,128)(2,1)S(1)}, bf16[48,768]{1,0:T(8,128)(2,1)S(1)}, u32[]{:S(2)}, u32[]{:S(2)}) collective-permute-start(bf16[48,768]{1,0:T(8,128)(2,1)S(1)} %sum_four.2.refs_0_), channel_id=1, source_target_pairs={{0,64},{4,68},{8,72},{12,76},{16,80},{20,84},{24,88},{28,92},{32,9... | collective-permute-start | bytes 221192 | tf_op jit(solution)/shard_map/ppermute | solution.py:480
  87.8 3.2 %collective-permute-start.14 = (bf16[48,768]{1,0:T(8,128)(2,1)S(1)}, bf16[48,768]{1,0:T(8,128)(2,1)S(1)}, u32[]{:S(2)}, u32[]{:S(2)}) collective-permute-start(bf16[48,768]{1,0:T(8,128)(2,1)S(1)} %sum_four.2.refs_0_), channel_id=1, source_target_pairs={{0,96},{4,100},{8,104},{12,108},{16,112},{20,116},{24,120},{28,124... | collective-permute-start | bytes 221192 | tf_op jit(solution)/shard_map/ppermute | solution.py:480
  88.7 4.8 %collective-permute-start.13 = (bf16[48,768]{1,0:T(8,128)(2,1)S(1)}, bf16[48,768]{1,0:T(8,128)(2,1)S(1)}, u32[]{:S(2)}, u32[]{:S(2)}) collective-permute-start(bf16[48,768]{1,0:T(8,128)(2,1)S(1)} %sum_four.2.refs_0_), channel_id=1, source_target_pairs={{0,32},{4,36},{8,40},{12,44},{16,48},{20,52},{24,56},{28,60},{32,6... | collective-permute-start | bytes 221192 | tf_op jit(solution)/shard_map/ppermute | solution.py:480
  93.6 4.6 %collective-permute-start.18 = (bf16[48,768]{1,0:T(8,128)(2,1)S(1)}, bf16[48,768]{1,0:T(8,128)(2,1)S(1)}, u32[]{:S(2)}, u32[]{:S(2)}) collective-permute-start(bf16[48,768]{1,0:T(8,128)(2,1)S(1)} %sum_four.3.refs_0_), channel_id=1, source_target_pairs={{0,24},{4,28},{8,0},{12,4},{16,8},{20,12},{24,16},{28,20},{32,56},... | collective-permute-start | bytes 221192 | tf_op jit(solution)/shard_map/ppermute | solution.py:483
  96.1 4.8 %collective-permute-start.17 = (bf16[48,768]{1,0:T(8,128)(2,1)S(1)}, bf16[48,768]{1,0:T(8,128)(2,1)S(1)}, u32[]{:S(2)}, u32[]{:S(2)}) collective-permute-start(bf16[48,768]{1,0:T(8,128)(2,1)S(1)} %sum_four.3.refs_0_), channel_id=1, source_target_pairs={{0,16},{4,20},{8,24},{12,28},{16,0},{20,4},{24,8},{28,12},{32,48},... | collective-permute-start | bytes 221192 | tf_op jit(solution)/shard_map/ppermute | solution.py:483
  96.3 5.2 %collective-permute-start.16 = (bf16[48,768]{1,0:T(8,128)(2,1)S(1)}, bf16[48,768]{1,0:T(8,128)(2,1)S(1)}, u32[]{:S(2)}, u32[]{:S(2)}) collective-permute-start(bf16[48,768]{1,0:T(8,128)(2,1)S(1)} %sum_four.3.refs_0_), channel_id=1, source_target_pairs={{0,8},{4,12},{8,16},{12,20},{16,24},{20,28},{24,0},{28,4},{32,40},... | collective-permute-start | bytes 221192 | tf_op jit(solution)/shard_map/ppermute | solution.py:483
  101.5 6.3 %collective-permute-start.19 = (bf16[192,768]{1,0:T(8,128)(2,1)S(1)}, bf16[192,768]{1,0:T(8,128)(2,1)S(1)}, u32[]{:S(2)}, u32[]{:S(2)}) collective-permute-start(bf16[192,768]{1,0:T(8,128)(2,1)S(1)} %join_z.1.own), channel_id=1, source_target_pairs={{0,4},{4,0},{8,12},{12,8},{16,20},{20,16},{24,28},{28,24},{32,36},... | collective-permute-start | bytes 884744 | tf_op jit(solution)/shard_map/ppermute | solution.py:485
  (7 other events, 33.7 us)
